TPU v7x, 128 devices: a whole 4x4x4 slice. The times are simulated.
128 devices in a mesh: pipe: 16 (over x, y), dp: 8 (over z, core).
Axes of the slice: x: 4, y: 4, z: 4, core: 2. Of those that a mesh axis runs over, the one named last changes fastest.
Arguments:
- stash_x: bfloat16 [16, 8, 12, 128, 4096], P('pipe', 'dp')
- stash_dy: bfloat16 [16, 8, 12, 128, 512], P('pipe', 'dp')
- queue: int32 [16, 12], P('pipe'), may hold values from 0 to 11, each once within a row
- micro_count: int32 [8], P('dp'), may hold values from 1 to 6, as said below
- master: float32 [16, 2, 4096, 512], P('pipe', None, 'dp'), may hold values from -6 to 6
- moment: float32 [16, 2, 4096, 512], P('pipe', None, 'dp'), may hold values from -0.3 to 0.3
- variance: float32 [16, 2, 4096, 512], P('pipe', None, 'dp'), may hold values from 0.0004 to 0.01
Outputs:
- new_master: float32 [16, 2, 4096, 512], P('pipe', None, 'dp')
- new_moment: float32 [16, 2, 4096, 512], P('pipe', None, 'dp')
- grad_norm: float32 [], replicated
Inputs may be any that keep to these rules, and one draw needn't show every extreme that they name: `queue`: each row holds every code from 0 to 11 once. `micro_count`: in every draw some data replica has all 6 microbatches live.
All inputs are finite; a program needn't handle non-finite values.
Results may differ from a plain program's by a relative error of at most 0.002.
Values may be sent and summed in bfloat16 or wider, within the bound.
No kernel may reach another device: no remote copies, remote signals or barrier semaphores. Data moves between devices by JAX's collectives and lax.ppermute only.
A program may use at most 128 MiB of HBM per device.

v0:
```python
import math

import jax
import jax.numpy as jnp
from jax import lax
from jax.sharding import PartitionSpec as P

first_fix = 1.0 - 0.9**20
second_fix = 1.0 - 0.95**20


def section_slots(slot_order, virtual, micro_half):
    slot_codes = jnp.arange(micro_half, dtype=jnp.int32) + virtual * micro_half
    slot_total = slot_order.shape[0]
    matches = slot_order[None, :] == slot_codes[:, None]
    indices = jnp.arange(slot_total, dtype=jnp.int32)[None, :]
    return jnp.sum(jnp.where(matches, indices, 0), axis=1)


def section_operands(tokens, cotangent, slot_order, live_count, virtual, micro_half):
    picked = section_slots(slot_order, virtual, micro_half)
    live_rows = (jnp.arange(micro_half, dtype=jnp.int32) < live_count).astype(cotangent.dtype)
    rows_x = jnp.take(tokens, picked, axis=0)
    rows_y = jnp.take(cotangent, picked, axis=0) * live_rows[:, None, None]
    return (rows_x.reshape(-1, rows_x.shape[-1]), rows_y.reshape(-1, rows_y.shape[-1]))


def weight_rows(rows_x, rows_y):
    return lax.dot_general(
        rows_x, rows_y, (((0,), (0,)), ((), ())), preferred_element_type=jnp.float32
    )


def on_device(stash_x, stash_dy, queue, micro_count, master, moment, variance):
    tokens = stash_x[0, 0]
    cotangent = stash_dy[0, 0]
    slot_order = queue[0]
    live_count = micro_count[0]
    micro_half = tokens.shape[0] // 2
    own_rows = master.shape[2]
    kv_width = master.shape[3]
    operands = [
        section_operands(tokens, cotangent, slot_order, live_count, virtual, micro_half)
        for virtual in range(2)
    ]
    section_grads = []
    for virtual in range(2):
        rows_x, rows_y = operands[virtual]
        section_grads.append(
            lax.psum_scatter(
                weight_rows(rows_x, rows_y).astype(jnp.bfloat16),
                "dp",
                scatter_dimension=0,
                tiled=True,
            ).astype(jnp.float32)
        )
    local_sq = jnp.sum(section_grads[0] * section_grads[0]) + jnp.sum(
        section_grads[1] * section_grads[1]
    )
    total_sq = lax.psum(local_sq, ("pipe", "dp"))
    grad_norm = jnp.sqrt(total_sq)
    params = 2 * lax.axis_size("pipe") * own_rows * lax.axis_size("dp") * kv_width
    max_norm = 0.05 * math.sqrt(params)
    clip_factor = jnp.minimum(jnp.float32(1.0), max_norm / (grad_norm + 1e-06))
    gradient = jnp.stack(section_grads)[None]
    scaled = clip_factor * gradient
    new_moment = 0.9 * moment + 0.1 * scaled
    second = 0.95 * variance + 0.05 * scaled * scaled
    update = new_moment / first_fix / (jnp.sqrt(second / second_fix) + 1e-08)
    new_master = master - 0.01 * update - 0.001 * master
    return (new_master, new_moment, grad_norm)


def solution(mesh):
    in_specs = (
        P("pipe", "dp", None, None, None),
        P("pipe", "dp", None, None, None),
        P("pipe", None),
        P("dp"),
        P("pipe", None, "dp", None),
        P("pipe", None, "dp", None),
        P("pipe", None, "dp", None),
    )
    out_specs = (P("pipe", None, "dp", None), P("pipe", None, "dp", None), P())
    return jax.shard_map(
        on_device, mesh=mesh, in_specs=in_specs, out_specs=out_specs, check_vma=False
    )
```

profile of v0, /device:TPU:1, one launch (start us, length us, event | category | flops | bytes accessed | tf_op | source)
XLA Modules:
  0.0 191.8 jit_solution(7770153290876367380)
XLA Ops:
  7.2 0.0 copy-start
  7.2 0.0 reduce-scatter.3.cloned.1.call-start
  7.2 1.0 select_reduce_fusion.1
  8.2 8.7 %gather_fusion = bf16[6,128,4096]{2,1,0:T(8,128)(2,1)} fusion(bf16[12,128,4096]{2,1,0:T(8,128)(2,1)} %bitcast.15, s32[1024]{0:T(1024)S(1)} %pad_clamp_fusion.1), kind=kCustom, calls=%fused_computation.clone | custom fusion | bytes 12582936 | tf_op jit(solution)/shard_map/jit(_take)/gather | solution.py:23
  16.9 0.0 copy-done
  16.9 0.6 gather_fusion.1
  18.2 8.2 %bitcast_convert_fusion.1 = bf16[4096,512]{1,0:T(8,128)(2,1)} fusion(bf16[6,128,4096]{2,1,0:T(8,128)(2,1)} %gather_fusion, pred[6]{0:T(512)(128)(4,1)S(1)} %compare_and_fusion.1, bf16[6,128,512]{2,1,0:T(8,128)(2,1)S(1)} %gather_fusion.1, bf16[6]{0:T(256)(128)(2,1)S(1)} %compare_convert_fusion), kind=kOutput, calls=%fused_computation.5 | convolution fusion | flops 3227254784 | bytes 11272210 | tf_op jit(solution)/shard_map/dot_general | solution.py:29
  26.4 0.0 reduce-scatter.3.cloned.1.call-update
  26.5 0.0 reduce-scatter.5.cloned.1.call-start
  26.5 8.6 %gather_fusion.2 = bf16[6,128,4096]{2,1,0:T(8,128)(2,1)} fusion(bf16[12,128,4096]{2,1,0:T(8,128)(2,1)} %bitcast.16, s32[1024]{0:T(1024)S(1)} %pad_clamp_fusion), kind=kCustom, calls=%fused_computation.2.clone | custom fusion | bytes 12582936 | tf_op jit(solution)/shard_map/jit(_take)/gather | solution.py:23
  35.2 0.6 gather_fusion.3
  35.8 8.2 %bitcast_convert_fusion = bf16[4096,512]{1,0:T(8,128)(2,1)} fusion(bf16[6,128,4096]{2,1,0:T(8,128)(2,1)} %gather_fusion.2, pred[6]{0:T(512)(128)(4,1)S(1)} %compare_and_fusion, bf16[6,128,512]{2,1,0:T(8,128)(2,1)S(1)} %gather_fusion.3, bf16[6]{0:T(256)(128)(2,1)S(1)} %compare_convert_fusion), kind=kOutput, calls=%fused_computation.4 | convolution fusion | flops 3227254784 | bytes 11272210 | tf_op jit(solution)/shard_map/dot_general | solution.py:29
  44.0 0.0 reduce-scatter.5.cloned.1.call-update
  44.0 21.0 %reduce-scatter.3.cloned.1.call-done = bf16[512,512]{1,0:T(8,128)(2,1)} async-done(((bf16[4096,512]{1,0:T(8,128)(2,1)}), bf16[512,512]{1,0:T(8,128)(2,1)}) %reduce-scatter.3.cloned.1.call-update) | async-done | bytes 524304 | tf_op jit(solution)/shard_map/reduce_scatter | solution.py:50
  65.0 1.9 fusion.14
  67.0 37.5 %reduce-scatter.5.cloned.1.call-done = bf16[512,512]{1,0:T(8,128)(2,1)} async-done(((bf16[4096,512]{1,0:T(8,128)(2,1)}), bf16[512,512]{1,0:T(8,128)(2,1)}) %reduce-scatter.5.cloned.1.call-update) | async-done | bytes 524304 | tf_op jit(solution)/shard_map/reduce_scatter | solution.py:50
  104.5 0.0 copy-start.2
  104.5 2.0 %fusion.15 = f32[]{:T(128)} fusion(bf16[512,512]{1,0:T(8,128)(2,1)} %reduce-scatter.5.cloned.1.call-done), kind=kLoop, calls=%fused_computation.28 | loop fusion | flops 786431 | bytes 524292 | tf_op jit(solution)/shard_map/reduce_sum | solution.py:57
  107.8 67.8 %psum.7 = f32[]{:T(128)} all-reduce(f32[]{:T(128)S(6)} %add.38), channel_id=1, replica_groups=mesh['pipe'=16,'dp'=8] {'pipe','dp'}, use_global_device_ids=true, to_apply=%region_6.9 | all-reduce | flops 1 | bytes 8 | tf_op jit(solution)/shard_map/psum | solution.py:60
  176.3 0.0 copy-start.1
  176.3 1.3 convert_bitcast_fusion.1
  177.6 0.0 copy-done.2
  177.6 0.1 convert_bitcast_fusion
  177.7 0.3 copy-done.1
  178.0 5.8 %fusion.13 = (f32[1,2,512,512]{3,2,1,0:T(8,128)}, f32[1,2,512,512]{3,2,1,0:T(8,128)}) fusion(f32[1,2,512,512]{3,2,1,0:T(8,128)S(1)} %copy-done.1, f32[1,2,512,512]{3,2,1,0:T(8,128)} %param.17, f32[1,1,512,512]{3,2,1,0:T(8,128)S(1)} %convert_bitcast_fusion, f32[1,1,512,512]{3,2,1,0:T(8,128)S(1)} %convert_bitcast_fusion.1, f32[]{:T(128)S(6)} %min_shard_map.3, ...), kind=kLoop, calls=%fused_computation.20 | loop fusion | flops 8912896 | bytes 12582916 | tf_op jit(solution)/shard_map/sub | solution.py:70
  (8 shorter events, 0.0 us)
Async XLA Ops:
  7.2 9.8 %copy-start = (bf16[1,1,12,128,512]{4,3,2,1,0:T(8,128)(2,1)S(1)}, bf16[1,1,12,128,512]{4,3,2,1,0:T(8,128)(2,1)}, u32[]{:S(2)}) copy-start(bf16[1,1,12,128,512]{4,3,2,1,0:T(8,128)(2,1)} %param.12) | copy-start | bytes 4718596
  7.2 57.9 %reduce-scatter.3.cloned.1.call-start = ((), (), s32[]{:S(2)}) async-start(), calls=%async_computation.2 | async-start | bytes 4718592 | tf_op jit(solution)/shard_map/reduce_scatter | solution.py:50
  26.5 78.0 %reduce-scatter.5.cloned.1.call-start = ((), (), s32[]{:S(2)}) async-start(), calls=%async_computation.3 | async-start | bytes 4718592 | tf_op jit(solution)/shard_map/reduce_scatter | solution.py:50
  104.5 73.1 %copy-start.2 = (bf16[512,512]{1,0:T(8,128)(2,1)S(1)}, bf16[512,512]{1,0:T(8,128)(2,1)}, u32[]{:S(2)}) copy-start(bf16[512,512]{1,0:T(8,128)(2,1)} %reduce-scatter.5.cloned.1.call-done) | copy-start | bytes 1572868
  176.3 1.8 copy-start.1
Sparse Core Ops, SparseCore 0:
  26.6 38.4 reduce-scatter.2
  67.4 36.9 reduce-scatter.4
where the time goes:
time: 192 us
  blocking collectives  67.8 us (35%)
  waiting for transfers between devices  58.6 us (31%)
  local copies, waits for them, and re-layouts  18.8 us (10%)
  between operations  18 us (9%)
  matrix products  16.4 us (9%)
  other arithmetic  12.2 us (6%)
    psum x1, blocking collectives, on_device(): total_sq = lax.psum(local_sq, ('pipe', 'dp'))  67.8 us
    reduce_scatter x2, waiting for transfers between devices, on_device(): lax.psum_scatter(weight_rows(rows_x, rows_y).astype(jnp.bfloat16), 'dp',...  58.5 us
    gather x2, local copies, waits for them, and re-layouts, section_operands(): rows_x = jnp.take(tokens, picked, axis=0)  17.3 us
    dot_general x2, matrix products, weight_rows(): lax.dot_general(rows_x, rows_y, (((0,), (0,)), ((), ())), preferred_eleme...  16.4 us
    sub x1, other arithmetic, on_device(): new_master = master - 0.01 * update - 0.001 * master  5.85 us
  transfers between devices with their start and end apart: 2, of which 2 were waited for; matrix products, arithmetic and copies ran while one was open for 10% of the time, Pallas kernels for 0%

commit v1 on v0

v1 whole, which is shorter than its diff:
```python
import functools
import math

import jax
import jax.numpy as jnp
from jax import lax
from jax.experimental import pallas as pl
from jax.experimental.pallas import tpu as pltpu
from jax.sharding import PartitionSpec as P

first_fix = 1.0 - 0.9**20
second_fix = 1.0 - 0.95**20

VMEM_LIMIT = 40 * 1024 * 1024


def place():
    me = lax.axis_index("dp")
    core = lax.rem(me, 2)
    return lax.div(me, 2), core, 1 - 2 * core


def section_kernel(step, mine, chips, *refs):
    queue, count, x_hbm, dy_hbm = refs[:4]
    others = refs[4:6] if mine else ()
    outs = refs[-6:-4]
    xbuf, ybuf, xsem, ysem = refs[-4:]
    slots, tokens, rows = xbuf.shape
    half = slots // 2
    z, core, sign = place()
    target = lax.rem(z + chips + step * sign, chips)
    owner = 2 * target + (core if mine else 1 - core)
    first = pl.multiple_of(owner * rows, rows)

    def copies(slot):
        code = queue[0, slot]
        return (
            pltpu.make_async_copy(x_hbm.at[0, 0, slot, :, pl.ds(first, rows)], xbuf.at[code], xsem.at[code]),
            pltpu.make_async_copy(dy_hbm.at[0, 0, slot], ybuf.at[code], ysem.at[code]),
        )

    for slot in range(slots):
        for copy in copies(slot):
            copy.start()
    live = count[0]
    width = ybuf.shape[2]
    tile = min(256, rows)
    for section in range(2):
        for code in range(section * half, (section + 1) * half):
            pltpu.make_async_copy(x_hbm.at[0, 0, 0, :, pl.ds(0, rows)], xbuf.at[code], xsem.at[code]).wait()
            pltpu.make_async_copy(dy_hbm.at[0, 0, 0], ybuf.at[code], ysem.at[code]).wait()
        span = slice(section * half, (section + 1) * half)
        dy = ybuf[span].reshape(half * tokens, width)
        micro = lax.broadcasted_iota(jnp.int32, (half * tokens, width), 0)
        dy = jnp.where(micro < live * tokens, dy, jnp.zeros_like(dy))
        for start in range(0, rows, tile):
            x = xbuf[span, :, start : start + tile].reshape(half * tokens, tile)
            total = lax.dot_general(x, dy, (((0,), (0,)), ((), ())), preferred_element_type=jnp.float32)
            if mine:
                total = total + others[section][start : start + tile, :].astype(jnp.float32)
            outs[section][start : start + tile, :] = total.astype(outs[section].dtype)


def section_rows(step, mine, chips, queue, count, x, dy, others=(), dtype=jnp.bfloat16):
    slots, tokens, features = x.shape[2:]
    width = dy.shape[4]
    rows = features // (2 * chips)
    smem = pl.BlockSpec(memory_space=pltpu.SMEM)
    hbm = pl.BlockSpec(memory_space=pl.ANY)
    vmem = pl.BlockSpec(memory_space=pltpu.VMEM)
    return pl.pallas_call(
        functools.partial(section_kernel, step, mine, chips),
        out_shape=(jax.ShapeDtypeStruct((rows, width), dtype),) * 2,
        in_specs=[smem, smem, hbm, hbm] + [vmem] * len(others),
        out_specs=(vmem, vmem),
        scratch_shapes=[
            pltpu.VMEM((slots, tokens, rows), x.dtype),
            pltpu.VMEM((slots, tokens, width), dy.dtype),
            pltpu.SemaphoreType.DMA((slots,)),
            pltpu.SemaphoreType.DMA((slots,)),
        ],
        compiler_params=pltpu.CompilerParams(vmem_limit_bytes=VMEM_LIMIT),
        cost_estimate=pl.CostEstimate(
            flops=2 * slots * tokens * rows * width,
            bytes_accessed=2 * slots * tokens * (rows + width) + 4 * rows * width,
            transcendentals=0,
        ),
        name=f"section_rows_{'keep' if mine else 'send'}_{step}",
    )(queue, count, x, dy, *others)


def sum_kernel(a, b, out):
    out[...] = (a[...].astype(jnp.float32) + b[...].astype(jnp.float32)).astype(out.dtype)


def add(a, b):
    return pl.pallas_call(sum_kernel, out_shape=jax.ShapeDtypeStruct(a.shape, a.dtype), name="ring_add")(a, b)


def total_kernel(own0, own1, a0, b0, a1, b1, grad, squares):
    norm = jnp.zeros((), jnp.float32)
    for section, parts in enumerate(((own0, a0, b0), (own1, a1, b1))):
        total = sum(part[...].astype(jnp.float32) for part in parts)
        grad[section] = total
        norm = norm + jnp.sum(total * total)
    squares[...] = jnp.full(squares.shape, norm, jnp.float32)


def totals(peers, own, a0, b0, a1, b1):
    rows, width = own[0].shape
    return pl.pallas_call(
        total_kernel,
        out_shape=(
            jax.ShapeDtypeStruct((2, rows, width), jnp.float32),
            jax.ShapeDtypeStruct((peers, 128), jnp.float32),
        ),
        compiler_params=pltpu.CompilerParams(vmem_limit_bytes=VMEM_LIMIT),
        name="totals",
    )(*own, a0, b0, a1, b1)


def update_kernel(max_norm, squares, grad, master, moment, variance, new_master, new_moment, norm_out):
    norm = jnp.sqrt(jnp.sum(squares[:, 0:1]))
    clip = jnp.minimum(jnp.float32(1.0), max_norm / (norm + 1e-06))
    norm_out[0, 0] = norm
    scaled = clip * grad[...]
    fresh = 0.9 * moment[...] + 0.1 * scaled
    second = 0.95 * variance[...] + 0.05 * scaled * scaled
    update = fresh / first_fix / (jnp.sqrt(second / second_fix) + 1e-08)
    new_moment[...] = fresh
    new_master[...] = master[...] - 0.01 * update - 0.001 * master[...]


def adam(max_norm, squares, grad, master, moment, variance):
    sections, rows, width = grad.shape
    tile = 128
    block = pl.BlockSpec((1, tile, width), lambda s, i: (s, i, 0))
    state = jax.ShapeDtypeStruct(grad.shape, jnp.float32)
    return pl.pallas_call(
        functools.partial(update_kernel, max_norm),
        grid=(sections, rows // tile),
        out_shape=(state, state, jax.ShapeDtypeStruct((1, 1), jnp.float32)),
        in_specs=[pl.BlockSpec(memory_space=pltpu.VMEM), block, block, block, block],
        out_specs=(block, block, pl.BlockSpec(memory_space=pltpu.SMEM)),
        compiler_params=pltpu.CompilerParams(vmem_limit_bytes=VMEM_LIMIT),
        name="adam",
    )(squares, grad, master, moment, variance)


def on_device(stash_x, stash_dy, queue, micro_count, master, moment, variance):
    own_rows, kv_width = master.shape[2:]
    peers = lax.axis_size("dp")
    chips = peers // 2
    everyone = lax.axis_size("pipe") * peers

    def ring(sign):
        return [
            (i, (i // 2 + sign * (1 - 2 * (i % 2))) % chips * 2 + i % 2) for i in range(peers)
        ]

    def sibling(value):
        return lax.ppermute(value, "dp", [(i, i ^ 1) for i in range(peers)])

    def along(value):
        return lax.ppermute(value, "dp", ring(1))

    def against(value):
        return lax.ppermute(value, "dp", ring(-1))

    rows = functools.partial(section_rows, chips=chips, queue=queue, count=micro_count, x=stash_x, dy=stash_dy)

    def chip_rows(step, dtype=jnp.bfloat16):
        sent = rows(-step, False)
        return rows(step, True, others=tuple(sibling(value) for value in sent), dtype=dtype)

    far = chip_rows(2)
    far_a, far_b = along(far[0]), against(far[1])
    near_a = chip_rows(1)
    near_b = chip_rows(-1)
    plain_a = along(near_a[1])
    plain_b = against(near_b[0])
    own = chip_rows(0, jnp.float32)
    sum_a = along(add(near_a[0], far_a))
    sum_b = against(add(near_b[1], far_b))
    grad, squares = totals(everyone, own, sum_a, plain_b, plain_a, sum_b)
    squares = lax.all_to_all(squares, ("pipe", "dp"), 0, 0, tiled=True)
    max_norm = 0.05 * math.sqrt(2 * lax.axis_size("pipe") * own_rows * peers * kv_width)
    new_master, new_moment, norm = adam(max_norm, squares, grad, master[0], moment[0], variance[0])
    return (new_master[None], new_moment[None], norm[0, 0])


def solution(mesh):
    in_specs = (
        P("pipe", "dp", None, None, None),
        P("pipe", "dp", None, None, None),
        P("pipe", None),
        P("dp"),
        P("pipe", None, "dp", None),
        P("pipe", None, "dp", None),
        P("pipe", None, "dp", None),
    )
    out_specs = (P("pipe", None, "dp", None), P("pipe", None, "dp", None), P())
    return jax.shard_map(
        on_device, mesh=mesh, in_specs=in_specs, out_specs=out_specs, check_vma=False
    )
```

time: 192 us -> 98.3 us (0.51)
  Pallas kernels: 0 us -> 53.6 us
  blocking collectives: 67.8 us -> 17.4 us
  waiting for transfers between devices: 58.6 us -> 8.87 us
  between operations: 18 us -> 1.47 us
  matrix products: 16.4 us -> 0 us
  local copies, waits for them, and re-layouts: 18.8 us -> 3.68 us
  starting transfers between devices: 0.08 us -> 12.7 us
  other arithmetic: 12.2 us -> 0 us
    psum x1 -> x0, blocking collectives: 67.8 us -> none  [on_device(): total_sq = lax.psum(local_sq, ('pipe', 'dp'))]
    reduce_scatter x2 -> x0, waiting for transfers between devices: 58.5 us -> none  [on_device(): lax.psum_scatter(weight_rows(rows_x, rows_y).astype(jnp.bfloat16), 'dp',...]
    pallas_call x0 -> x12, Pallas kernels: none -> 53.6 us  [the longest x8 41.6 us: section_rows(): pl.pallas_call(functools.partial(section_kernel, step, mine, chips), out_...]
    gather x4 -> x0, local copies, waits for them, and re-layouts: 18.5 us -> none  [the longest x2 17.3 us: section_operands(): rows_x = jnp.take(tokens, picked, axis=0)]
    all_to_all x0 -> x1, blocking collectives: none -> 17.4 us  [on_device(): squares = lax.all_to_all(squares, ('pipe', 'dp'), 0, 0, tiled=True)]
    dot_general x2 -> x0, matrix products: 16.4 us -> none  [weight_rows(): lax.dot_general(rows_x, rows_y, (((0,), (0,)), ((), ())), preferred_eleme...]
    ppermute x0 -> x14, starting transfers between devices: none -> 12.7 us  [the longest x3 9 us: along(): return lax.ppermute(value, 'dp', ring(1))]
    ppermute x0 -> x14, waiting for transfers between devices: none -> 8.87 us  [the longest x3 5.07 us: along(): return lax.ppermute(value, 'dp', ring(1))]
  transfers between devices with their start and end apart: 2 -> 14, of which waited for: 2 -> 2; matrix products, arithmetic and copies ran while one was open for 10% -> 0% of each run, Pallas kernels for 0% -> 42%
where the time goes in v1:
time: 98.3 us; the launch traced here: 97.8 us
  Pallas kernels  53.6 us (55%)
  blocking collectives  17.4 us (18%)
  starting transfers between devices  12.7 us (13%)
  waiting for transfers between devices  8.87 us (9%)
  local copies, waits for them, and re-layouts  3.68 us (4%)
  between operations  1.47 us (1%)
    pallas_call x8, Pallas kernels, section_rows(): pl.pallas_call(functools.partial(section_kernel, step, mine, chips), out_...  41.6 us
    all_to_all x1, blocking collectives, on_device(): squares = lax.all_to_all(squares, ('pipe', 'dp'), 0, 0, tiled=True)  17.4 us
    ppermute x3, starting transfers between devices, along(): return lax.ppermute(value, 'dp', ring(1))  9 us
    pallas_call x1, Pallas kernels, adam(): pl.pallas_call(functools.partial(update_kernel, max_norm), grid=(sections...  5.62 us
    ppermute x3, waiting for transfers between devices, along(): return lax.ppermute(value, 'dp', ring(1))  5.07 us
    pallas_call x2, Pallas kernels, add(): pl.pallas_call(sum_kernel, out_shape=jax.ShapeDtypeStruct(a.shape, a.dtyp...  4.22 us
    ppermute x3, waiting for transfers between devices, against(): return lax.ppermute(value, 'dp', ring(-1))  3.78 us
    ppermute x8, starting transfers between devices, sibling(): return lax.ppermute(value, 'dp', [(i, i ^ 1) for i in range(peers)])  3.73 us
  transfers between devices with their start and end apart: 14, of which 2 were waited for; matrix products, arithmetic and copies ran while one was open for 0% of the time, Pallas kernels for 42%

profile of v1, /device:TPU:1, one launch (start us, length us, event | category | flops | bytes accessed | tf_op | source)
XLA Modules:
  0.0 97.8 jit_solution(14459535902636602826)
XLA Ops:
  1.3 0.0 copy-start
  1.3 1.4 %copy-done = bf16[1,1,12,128,512]{4,3,2,1,0:T(8,128)(2,1)S(1)} copy-done((bf16[1,1,12,128,512]{4,3,2,1,0:T(8,128)(2,1)S(1)}, bf16[1,1,12,128,512]{4,3,2,1,0:T(8,128)(2,1)}, u32[]{:S(2)}) %copy-start) | copy-done | bytes 1572888
  2.7 0.7 copy-done.7
  3.3 4.9 %section_rows_send_-2.1 = (bf16[512,512]{1,0:T(8,128)(2,1)S(1)}, bf16[512,512]{1,0:T(8,128)(2,1)S(1)}) custom-call(s32[1,12]{1,0:T(1,128)S(1)} %copy-done.7, s32[1]{0:T(128)S(6)} %copy.11.refs_1_, bf16[1,1,12,128,4096]{4,3,2,1,0:T(8,128)(2,1)} %refs_2_.15, bf16[1,1,12,128,512]{4,3,2,1,0:T(8,128)(2,1)S(1)} %copy-done), custom_call_target="tpu_custom_call" | custom-call | flops 805306368 | bytes 4194304 | tf_op jit(solution)/shard_map/section_rows_send_-2/pallas_call | solution.py:71
  8.2 1.5 %collective-permute-start.4 = (bf16[512,512]{1,0:T(8,128)(2,1)S(1)}, bf16[512,512]{1,0:T(8,128)(2,1)S(1)}, u32[]{:S(2)}, u32[]{:S(2)}) collective-permute-start(bf16[512,512]{1,0:T(8,128)(2,1)S(1)} %get-tuple-element.31), channel_id=1, source_target_pairs={{0,1},{1,0},{2,3},{3,2},{4,5},{5,4},{6,7},{7,6},{8,9},{9,8},{10,11... | collective-permute-start | bytes 1572872 | tf_op jit(solution)/shard_map/ppermute | solution.py:162
  9.7 0.1 collective-permute-start.5
  9.8 4.9 %section_rows_send_-1.1 = (bf16[512,512]{1,0:T(8,128)(2,1)S(1)}, bf16[512,512]{1,0:T(8,128)(2,1)S(1)}) custom-call(s32[1,12]{1,0:T(1,128)S(1)} %copy-done.7, s32[1]{0:T(128)S(6)} %copy.11.refs_1_, bf16[1,1,12,128,4096]{4,3,2,1,0:T(8,128)(2,1)} %refs_2_.15, bf16[1,1,12,128,512]{4,3,2,1,0:T(8,128)(2,1)S(1)} %copy-done), custom_call_target="tpu_custom_call" | custom-call | flops 805306368 | bytes 4194304 | tf_op jit(solution)/shard_map/section_rows_send_-1/pallas_call | solution.py:71
  14.7 0.5 collective-permute-start.2
  15.2 0.1 collective-permute-start.3
  15.3 4.9 %section_rows_send_1.1 = (bf16[512,512]{1,0:T(8,128)(2,1)S(1)}, bf16[512,512]{1,0:T(8,128)(2,1)S(1)}) custom-call(s32[1,12]{1,0:T(1,128)S(1)} %copy-done.7, s32[1]{0:T(128)S(6)} %copy.11.refs_1_, bf16[1,1,12,128,4096]{4,3,2,1,0:T(8,128)(2,1)} %refs_2_.15, bf16[1,1,12,128,512]{4,3,2,1,0:T(8,128)(2,1)S(1)} %copy-done), custom_call_target="tpu_custom_call" | custom-call | flops 805306368 | bytes 4194304 | tf_op jit(solution)/shard_map/section_rows_send_1/pallas_call | solution.py:71
  20.2 0.5 collective-permute-start.8
  20.6 0.1 collective-permute-start.9
  20.8 5.7 %section_rows_keep_2.1 = (bf16[512,512]{1,0:T(8,128)(2,1)S(1)}, bf16[512,512]{1,0:T(8,128)(2,1)}) custom-call(s32[1,12]{1,0:T(1,128)S(1)} %copy-done.7, s32[1]{0:T(128)S(6)} %copy.11.refs_1_, bf16[1,1,12,128,4096]{4,3,2,1,0:T(8,128)(2,1)} %refs_2_.15, bf16[1,1,12,128,512]{4,3,2,1,0:T(8,128)(2,1)S(1)} %copy-done, ...), custom_call_target="tpu_custom_call" | custom-call | flops 805306368 | bytes 4194304 | tf_op jit(solution)/shard_map/section_rows_keep_2/pallas_call | solution.py:71
  26.4 3.9 %collective-permute-start.6 = (bf16[512,512]{1,0:T(8,128)(2,1)S(1)}, bf16[512,512]{1,0:T(8,128)(2,1)S(1)}, u32[]{:S(2)}, u32[]{:S(2)}) collective-permute-start(bf16[512,512]{1,0:T(8,128)(2,1)S(1)} %get-tuple-element.33), channel_id=1, source_target_pairs={{0,2},{1,7},{2,4},{3,1},{4,6},{5,3},{6,0},{7,5},{8,10},{9,15},{10,... | collective-permute-start | bytes 1572872 | tf_op jit(solution)/shard_map/ppermute | solution.py:165
  30.4 5.7 %section_rows_send_0.1 = (bf16[512,512]{1,0:T(8,128)(2,1)}, bf16[512,512]{1,0:T(8,128)(2,1)}) custom-call(s32[1,12]{1,0:T(1,128)S(1)} %copy-done.7, s32[1]{0:T(128)S(6)} %copy.11.refs_1_, bf16[1,1,12,128,4096]{4,3,2,1,0:T(8,128)(2,1)} %refs_2_.15, bf16[1,1,12,128,512]{4,3,2,1,0:T(8,128)(2,1)S(1)} %copy-done), custom_call_target="tpu_custom_call" | custom-call | flops 805306368 | bytes 4194304 | tf_op jit(solution)/shard_map/section_rows_send_0/pallas_call | solution.py:71
  36.1 0.9 collective-permute-start
  36.9 5.7 %section_rows_keep_1.1 = (bf16[512,512]{1,0:T(8,128)(2,1)S(1)}, bf16[512,512]{1,0:T(8,128)(2,1)}) custom-call(s32[1,12]{1,0:T(1,128)S(1)} %copy-done.7, s32[1]{0:T(128)S(6)} %copy.11.refs_1_, bf16[1,1,12,128,4096]{4,3,2,1,0:T(8,128)(2,1)} %refs_2_.15, bf16[1,1,12,128,512]{4,3,2,1,0:T(8,128)(2,1)S(1)} %copy-done, ...), custom_call_target="tpu_custom_call" | custom-call | flops 805306368 | bytes 4194304 | tf_op jit(solution)/shard_map/section_rows_keep_1/pallas_call | solution.py:71
  42.6 0.1 collective-permute-start.1
  42.7 2.4 %collective-permute-start.11 = (bf16[512,512]{1,0:T(8,128)(2,1)}, bf16[512,512]{1,0:T(8,128)(2,1)S(1)}, u32[]{:S(2)}, u32[]{:S(2)}) collective-permute-start(bf16[512,512]{1,0:T(8,128)(2,1)} %get-tuple-element.37), channel_id=1, source_target_pairs={{0,2},{1,7},{2,4},{3,1},{4,6},{5,3},{6,0},{7,5},{8,10},{9,15},{10,... | collective-permute-start | bytes 1572872 | tf_op jit(solution)/shard_map/ppermute | solution.py:165
  45.1 5.1 %section_rows_keep_-1.1 = (bf16[512,512]{1,0:T(8,128)(2,1)}, bf16[512,512]{1,0:T(8,128)(2,1)S(1)}) custom-call(s32[1,12]{1,0:T(1,128)S(1)} %copy-done.7, s32[1]{0:T(128)S(6)} %copy.11.refs_1_, bf16[1,1,12,128,4096]{4,3,2,1,0:T(8,128)(2,1)} %refs_2_.15, bf16[1,1,12,128,512]{4,3,2,1,0:T(8,128)(2,1)S(1)} %copy-done, ...), custom_call_target="tpu_custom_call" | custom-call | flops 805306368 | bytes 4194304 | tf_op jit(solution)/shard_map/section_rows_keep_-1/pallas_call | solution.py:71
  50.2 0.8 copy-done.6
  51.0 0.8 copy-done.9
  51.8 2.1 %ring_add.2 = bf16[512,512]{1,0:T(8,128)(2,1)} custom-call(bf16[512,512]{1,0:T(8,128)(2,1)} %copy-done.5, bf16[512,512]{1,0:T(8,128)(2,1)} %copy-done.9), custom_call_target="tpu_custom_call" | custom-call | tf_op jit(solution)/shard_map/ring_add/pallas_call | solution.py:97
  53.9 2.7 %collective-permute-start.7 = (bf16[512,512]{1,0:T(8,128)(2,1)}, bf16[512,512]{1,0:T(8,128)(2,1)}, u32[]{:S(2)}, u32[]{:S(2)}) collective-permute-start(bf16[512,512]{1,0:T(8,128)(2,1)} %ring_add.2), channel_id=1, source_target_pairs={{0,2},{1,7},{2,4},{3,1},{4,6},{5,3},{6,0},{7,5},{8,10},{9,15},{10,... | collective-permute-start | bytes 1572872 | tf_op jit(solution)/shard_map/ppermute | solution.py:165
  56.6 2.1 %ring_add.3 = bf16[512,512]{1,0:T(8,128)(2,1)} custom-call(bf16[512,512]{1,0:T(8,128)(2,1)} %copy-done.6, bf16[512,512]{1,0:T(8,128)(2,1)} %collective-permute-done.12.b), custom_call_target="tpu_custom_call" | custom-call | tf_op jit(solution)/shard_map/ring_add/pallas_call | solution.py:97
  58.8 0.0 copy-start.4
  58.8 4.9 %section_rows_keep_0.1 = (f32[512,512]{1,0:T(8,128)S(1)}, f32[512,512]{1,0:T(8,128)S(1)}) custom-call(s32[1,12]{1,0:T(1,128)S(1)} %copy-done.8, s32[1]{0:T(128)S(6)} %copy.11.refs_1_, bf16[1,1,12,128,4096]{4,3,2,1,0:T(8,128)(2,1)} %refs_2_.15, bf16[1,1,12,128,512]{4,3,2,1,0:T(8,128)(2,1)S(1)} %copy-done.1, ...), custom_call_target="tpu_custom_call" | custom-call | flops 805306368 | bytes 4194304 | tf_op jit(solution)/shard_map/section_rows_keep_0/pallas_call | solution.py:71
  63.7 5.1 %collective-permute-done.7.a0 = bf16[512,512]{1,0:T(8,128)(2,1)} collective-permute-done((bf16[512,512]{1,0:T(8,128)(2,1)}, bf16[512,512]{1,0:T(8,128)(2,1)}, u32[]{:S(2)}, u32[]{:S(2)}) %collective-permute-start.7) | collective-permute-done | bytes 524320 | tf_op jit(solution)/shard_map/ppermute | solution.py:165
  68.7 3.8 %collective-permute-done.13.b1 = bf16[512,512]{1,0:T(8,128)(2,1)S(1)} collective-permute-done((bf16[512,512]{1,0:T(8,128)(2,1)}, bf16[512,512]{1,0:T(8,128)(2,1)S(1)}, u32[]{:S(2)}, u32[]{:S(2)}) %collective-permute-start.13) | collective-permute-done | bytes 524320 | tf_op jit(solution)/shard_map/ppermute | solution.py:168
  72.5 2.2 %totals.1 = (f32[2,512,512]{2,1,0:T(8,128)S(1)}, f32[128,128]{1,0:T(8,128)S(1)}) custom-call(f32[512,512]{1,0:T(8,128)S(1)} %get-tuple-element.26.own0, f32[512,512]{1,0:T(8,128)S(1)} %get-tuple-element.27.own1, bf16[512,512]{1,0:T(8,128)(2,1)} %collective-permute-done.7.a0, bf16[512,512]{1,0:T(8,128)(2,1)} %collective-permute-done.10.b0, ...), custom_call_target="tpu_custom_call" | custom-call | tf_op jit(solution)/shard_map/totals/pallas_call | solution.py:111
  74.7 17.4 %all_to_all.11 = f32[128,1,128]{2,1,0:T(1,128)S(1)} all-to-all(f32[128,1,128]{2,1,0:T(1,128)S(1)} %bitcast.14), channel_id=1, replica_groups=mesh['pipe'=16,'dp'=8] {'pipe','dp'}, dimensions={0} | all-to-all | bytes 131072 | tf_op jit(solution)/shard_map/all_to_all | solution.py:186
  92.1 5.6 %adam.1 = (f32[2,512,512]{2,1,0:T(8,128)}, f32[2,512,512]{2,1,0:T(8,128)}, f32[1,1]{1,0:T(1,128)}) custom-call(f32[128,128]{1,0:T(8,128)S(1)} %bitcast.13, f32[2,512,512]{2,1,0:T(8,128)S(1)} %get-tuple-element.41.grad, f32[2,512,512]{2,1,0:T(8,128)S(1)} %bitcast.10, f32[2,512,512]{2,1,0:T(8,128)S(1)} %bitcast.11, f32[2,512,512]{2,1,0:T(8,128)S(1)} %bitcast.12), custom_call_target="tpu_custom_call" | custom-call | tf_op jit(solution)/shard_map/adam/pallas_call | solution.py:139
  (29 shorter events, 0.1 us)
Async XLA Ops:
  1.3 1.4 %copy-start = (bf16[1,1,12,128,512]{4,3,2,1,0:T(8,128)(2,1)S(1)}, bf16[1,1,12,128,512]{4,3,2,1,0:T(8,128)(2,1)}, u32[]{:S(2)}) copy-start(bf16[1,1,12,128,512]{4,3,2,1,0:T(8,128)(2,1)} %refs_3_.15) | copy-start | bytes 4718596
  2.7 0.7 copy-start.7
  8.2 12.4 %collective-permute-start.4 = (bf16[512,512]{1,0:T(8,128)(2,1)S(1)}, bf16[512,512]{1,0:T(8,128)(2,1)S(1)}, u32[]{:S(2)}, u32[]{:S(2)}) collective-permute-start(bf16[512,512]{1,0:T(8,128)(2,1)S(1)} %get-tuple-element.31), channel_id=1, source_target_pairs={{0,1},{1,0},{2,3},{3,2},{4,5},{5,4},{6,7},{7,6},{8,9},{9,8},{10,11... | collective-permute-start | bytes 1572872 | tf_op jit(solution)/shard_map/ppermute | solution.py:162
  9.7 11.0 %collective-permute-start.5 = (bf16[512,512]{1,0:T(8,128)(2,1)S(1)}, bf16[512,512]{1,0:T(8,128)(2,1)S(1)}, u32[]{:S(2)}, u32[]{:S(2)}) collective-permute-start(bf16[512,512]{1,0:T(8,128)(2,1)S(1)} %get-tuple-element.32), channel_id=1, source_target_pairs={{0,1},{1,0},{2,3},{3,2},{4,5},{5,4},{6,7},{7,6},{8,9},{9,8},{10,11... | collective-permute-start | bytes 1572872 | tf_op jit(solution)/shard_map/ppermute | solution.py:162
  14.7 15.7 %collective-permute-start.2 = (bf16[512,512]{1,0:T(8,128)(2,1)S(1)}, bf16[512,512]{1,0:T(8,128)(2,1)S(1)}, u32[]{:S(2)}, u32[]{:S(2)}) collective-permute-start(bf16[512,512]{1,0:T(8,128)(2,1)S(1)} %get-tuple-element.28), channel_id=1, source_target_pairs={{0,1},{1,0},{2,3},{3,2},{4,5},{5,4},{6,7},{7,6},{8,9},{9,8},{10,11... | collective-permute-start | bytes 1572872 | tf_op jit(solution)/shard_map/ppermute | solution.py:162
  15.2 20.9 %collective-permute-start.3 = (bf16[512,512]{1,0:T(8,128)(2,1)S(1)}, bf16[512,512]{1,0:T(8,128)(2,1)S(1)}, u32[]{:S(2)}, u32[]{:S(2)}) collective-permute-start(bf16[512,512]{1,0:T(8,128)(2,1)S(1)} %get-tuple-element.29), channel_id=1, source_target_pairs={{0,1},{1,0},{2,3},{3,2},{4,5},{5,4},{6,7},{7,6},{8,9},{9,8},{10,11... | collective-permute-start | bytes 1572872 | tf_op jit(solution)/shard_map/ppermute | solution.py:162
  20.2 22.5 %collective-permute-start.8 = (bf16[512,512]{1,0:T(8,128)(2,1)S(1)}, bf16[512,512]{1,0:T(8,128)(2,1)S(1)}, u32[]{:S(2)}, u32[]{:S(2)}) collective-permute-start(bf16[512,512]{1,0:T(8,128)(2,1)S(1)} %get-tuple-element.34), channel_id=1, source_target_pairs={{0,1},{1,0},{2,3},{3,2},{4,5},{5,4},{6,7},{7,6},{8,9},{9,8},{10,11... | collective-permute-start | bytes 1572872 | tf_op jit(solution)/shard_map/ppermute | solution.py:162
  20.6 22.1 %collective-permute-start.9 = (bf16[512,512]{1,0:T(8,128)(2,1)S(1)}, bf16[512,512]{1,0:T(8,128)(2,1)S(1)}, u32[]{:S(2)}, u32[]{:S(2)}) collective-permute-start(bf16[512,512]{1,0:T(8,128)(2,1)S(1)} %get-tuple-element.35), channel_id=1, source_target_pairs={{0,1},{1,0},{2,3},{3,2},{4,5},{5,4},{6,7},{7,6},{8,9},{9,8},{10,11... | collective-permute-start | bytes 1572872 | tf_op jit(solution)/shard_map/ppermute | solution.py:162
  26.4 24.6 %collective-permute-start.6 = (bf16[512,512]{1,0:T(8,128)(2,1)S(1)}, bf16[512,512]{1,0:T(8,128)(2,1)S(1)}, u32[]{:S(2)}, u32[]{:S(2)}) collective-permute-start(bf16[512,512]{1,0:T(8,128)(2,1)S(1)} %get-tuple-element.33), channel_id=1, source_target_pairs={{0,2},{1,7},{2,4},{3,1},{4,6},{5,3},{6,0},{7,5},{8,10},{9,15},{10,... | collective-permute-start | bytes 1572872 | tf_op jit(solution)/shard_map/ppermute | solution.py:165
  30.4 23.6 %collective-permute-start.12 = (bf16[512,512]{1,0:T(8,128)(2,1)}, bf16[512,512]{1,0:T(8,128)(2,1)}, u32[]{:S(2)}, u32[]{:S(2)}) collective-permute-start(bf16[512,512]{1,0:T(8,128)(2,1)} %get-tuple-element.39), channel_id=1, source_target_pairs={{0,6},{1,3},{2,0},{3,5},{4,2},{5,7},{6,4},{7,1},{8,14},{9,11},{10,... | collective-permute-start | bytes 1572872 | tf_op jit(solution)/shard_map/ppermute | solution.py:168
  36.1 22.7 %collective-permute-start = (bf16[512,512]{1,0:T(8,128)(2,1)}, bf16[512,512]{1,0:T(8,128)(2,1)S(1)}, u32[]{:S(2)}, u32[]{:S(2)}) collective-permute-start(bf16[512,512]{1,0:T(8,128)(2,1)} %get-tuple-element.24), channel_id=1, source_target_pairs={{0,1},{1,0},{2,3},{3,2},{4,5},{5,4},{6,7},{7,6},{8,9},{9,8},{10,11... | collective-permute-start | bytes 1572872 | tf_op jit(solution)/shard_map/ppermute | solution.py:162
  42.6 7.6 %copy-start.5 = (bf16[512,512]{1,0:T(8,128)(2,1)}, bf16[512,512]{1,0:T(8,128)(2,1)S(1)}, u32[]{:S(2)}) copy-start(bf16[512,512]{1,0:T(8,128)(2,1)S(1)} %get-tuple-element.30.a) | copy-start | bytes 1572868
  42.6 16.1 %collective-permute-start.1 = (bf16[512,512]{1,0:T(8,128)(2,1)}, bf16[512,512]{1,0:T(8,128)(2,1)S(1)}, u32[]{:S(2)}, u32[]{:S(2)}) collective-permute-start(bf16[512,512]{1,0:T(8,128)(2,1)} %get-tuple-element.25), channel_id=1, source_target_pairs={{0,1},{1,0},{2,3},{3,2},{4,5},{5,4},{6,7},{7,6},{8,9},{9,8},{10,11... | collective-permute-start | bytes 1572872 | tf_op jit(solution)/shard_map/ppermute | solution.py:162
  42.7 20.9 %collective-permute-start.11 = (bf16[512,512]{1,0:T(8,128)(2,1)}, bf16[512,512]{1,0:T(8,128)(2,1)S(1)}, u32[]{:S(2)}, u32[]{:S(2)}) collective-permute-start(bf16[512,512]{1,0:T(8,128)(2,1)} %get-tuple-element.37), channel_id=1, source_target_pairs={{0,2},{1,7},{2,4},{3,1},{4,6},{5,3},{6,0},{7,5},{8,10},{9,15},{10,... | collective-permute-start | bytes 1572872 | tf_op jit(solution)/shard_map/ppermute | solution.py:165
  50.2 0.8 copy-start.6
  51.0 7.7 %copy-start.1 = (bf16[1,1,12,128,512]{4,3,2,1,0:T(8,128)(2,1)S(1)}, bf16[1,1,12,128,512]{4,3,2,1,0:T(8,128)(2,1)}, u32[]{:S(2)}) copy-start(bf16[1,1,12,128,512]{4,3,2,1,0:T(8,128)(2,1)} %refs_3_.15) | copy-start | bytes 4718596
  51.0 7.7 %copy-start.8 = (s32[1,12]{1,0:T(1,128)S(1)}, s32[1,12]{1,0:T(1,128)}, u32[]{:S(2)}) copy-start(s32[1,12]{1,0:T(1,128)} %refs_0_.15) | copy-start | bytes 148
  51.0 0.8 copy-start.9
  51.8 11.8 %collective-permute-start.10 = (bf16[512,512]{1,0:T(8,128)(2,1)}, bf16[512,512]{1,0:T(8,128)(2,1)}, u32[]{:S(2)}, u32[]{:S(2)}) collective-permute-start(bf16[512,512]{1,0:T(8,128)(2,1)} %get-tuple-element.36), channel_id=1, source_target_pairs={{0,6},{1,3},{2,0},{3,5},{4,2},{5,7},{6,4},{7,1},{8,14},{9,11},{10,... | collective-permute-start | bytes 1572872 | tf_op jit(solution)/shard_map/ppermute | solution.py:168
  53.9 14.8 %collective-permute-start.7 = (bf16[512,512]{1,0:T(8,128)(2,1)}, bf16[512,512]{1,0:T(8,128)(2,1)}, u32[]{:S(2)}, u32[]{:S(2)}) collective-permute-start(bf16[512,512]{1,0:T(8,128)(2,1)} %ring_add.2), channel_id=1, source_target_pairs={{0,2},{1,7},{2,4},{3,1},{4,6},{5,3},{6,0},{7,5},{8,10},{9,15},{10,... | collective-permute-start | bytes 1572872 | tf_op jit(solution)/shard_map/ppermute | solution.py:165
  58.7 13.8 %collective-permute-start.13 = (bf16[512,512]{1,0:T(8,128)(2,1)}, bf16[512,512]{1,0:T(8,128)(2,1)S(1)}, u32[]{:S(2)}, u32[]{:S(2)}) collective-permute-start(bf16[512,512]{1,0:T(8,128)(2,1)} %ring_add.3), channel_id=1, source_target_pairs={{0,6},{1,3},{2,0},{3,5},{4,2},{5,7},{6,4},{7,1},{8,14},{9,11},{10,... | collective-permute-start | bytes 1572872 | tf_op jit(solution)/shard_map/ppermute | solution.py:168
  58.8 33.4 %copy-start.4 = (f32[1,2,512,512]{3,2,1,0:T(8,128)S(1)}, f32[1,2,512,512]{3,2,1,0:T(8,128)}, u32[]{:S(2)}) copy-start(f32[1,2,512,512]{3,2,1,0:T(8,128)} %param.13) | copy-start | bytes 6291460
  72.5 19.6 %copy-start.2 = (f32[1,2,512,512]{3,2,1,0:T(8,128)S(1)}, f32[1,2,512,512]{3,2,1,0:T(8,128)}, u32[]{:S(2)}) copy-start(f32[1,2,512,512]{3,2,1,0:T(8,128)} %param.11) | copy-start | bytes 6291460
  72.5 19.6 %copy-start.3 = (f32[1,2,512,512]{3,2,1,0:T(8,128)S(1)}, f32[1,2,512,512]{3,2,1,0:T(8,128)}, u32[]{:S(2)}) copy-start(f32[1,2,512,512]{3,2,1,0:T(8,128)} %param.12) | copy-start | bytes 6291460

commit v2 on v1

v2 whole, which is shorter than its diff:
```python
import functools
import math

import jax
import jax.numpy as jnp
from jax import lax
from jax.experimental import pallas as pl
from jax.experimental.pallas import tpu as pltpu
from jax.sharding import PartitionSpec as P

first_fix = 1.0 - 0.9**20
second_fix = 1.0 - 0.95**20

def vmem_limit(mib):
    return pltpu.CompilerParams(vmem_limit_bytes=mib * 1024 * 1024)


def place():
    me = lax.axis_index("dp")
    core = lax.rem(me, 2)
    return lax.div(me, 2), core, 1 - 2 * core


def owner_of(block, chips):
    step, mine = block
    z, core, sign = place()
    target = lax.rem(z + chips + step * sign, chips)
    return 2 * target + (core if mine else 1 - core)


def section_product(section, queue, count, x_of, rows, dy_ref, tile, store):
    slots = dy_ref.shape[0]
    width = dy_ref.shape[2]
    half = slots // 2
    live = count[0]
    picked = []
    for micro in range(half):
        slot = jnp.int32(0)
        for place_in_stash in range(slots):
            slot = jnp.where(queue[0, place_in_stash] == section * half + micro, place_in_stash, slot)
        picked.append(slot)
    dy = []
    for micro, slot in enumerate(picked):
        value = dy_ref[slot]
        dy.append(jnp.where(micro < live, value, jnp.zeros_like(value)))
    dy = jnp.concatenate(dy, axis=0)
    for start in range(0, rows, tile):
        x = jnp.concatenate([x_of(slot, start, tile) for slot in picked], axis=0)
        store(
            start,
            lax.dot_general(x, dy, (((0,), (0,)), ((), ())), preferred_element_type=jnp.float32),
        )


def product_kernel(sections, chips, block, n_others, n_ready, stacked, *refs):
    queue, count, x_ref, dy_ref = refs[:4]
    others = refs[4 : 4 + n_others]
    ready = refs[4 + n_others : 4 + n_others + n_ready]
    outs = refs[4 + n_others + n_ready :]
    rows = outs[0].shape[-2]
    tile = min(256, rows)
    first = owner_of(block, chips) * rows

    def x_of(slot, start, size):
        if len(x_ref.shape) == 3:
            return x_ref[slot, :, start : start + size]
        return x_ref[0, 0, slot, :, pl.ds(pl.multiple_of(first + start, size), size)]

    for i, value in enumerate(ready):
        outs[0][i] = value[...]
    for i, section in enumerate(sections):

        def store(start, total, i=i):
            span = pl.ds(start, tile)
            if others:
                other = others[i][span, :] if len(others) == len(sections) else others[0][i, span, :]
                total = total + other.astype(jnp.float32)
            if stacked:
                outs[0][n_ready + i, span, :] = total.astype(outs[0].dtype)
            else:
                outs[i][span, :] = total.astype(outs[i].dtype)

        section_product(section, queue, count, x_of, rows, dy_ref, tile, store)


def first_kernel(chips, blocks, queue_hbm, count, x_hbm, dy_hbm, out, dy_ref, *rest):
    buffers, (queue, sems) = rest[:-2], rest[-2:]
    rows = buffers[0].shape[2]
    copies = [
        pltpu.make_async_copy(queue_hbm, queue, sems.at[0]),
        pltpu.make_async_copy(dy_hbm.at[0, 0], dy_ref, sems.at[1]),
    ]
    for i, (block, buffer) in enumerate(zip(blocks, buffers)):
        first = pl.multiple_of(owner_of(block, chips) * rows, rows)
        copies.append(pltpu.make_async_copy(x_hbm.at[0, 0, :, :, pl.ds(first, rows)], buffer, sems.at[2 + i]))
    for copy in copies:
        copy.start()
    for copy in copies[:3]:
        copy.wait()
    tile = min(256, rows)

    def x_of(slot, start, size):
        return buffers[0][slot, :, start : start + size]

    def store(start, total):
        out[pl.ds(start, tile), :] = total.astype(out.dtype)

    section_product(0, queue, count, x_of, rows, dy_ref, tile, store)
    for copy in copies[3:]:
        copy.wait()


COSTS = dict()


def cost(name):
    return pl.CostEstimate(flops=COSTS.get(name, 1), bytes_accessed=1, transcendentals=0)


SMEM = pl.BlockSpec(memory_space=pltpu.SMEM)
VMEM = pl.BlockSpec(memory_space=pltpu.VMEM)
HBM = pl.BlockSpec(memory_space=pl.ANY)


def first_product(queue, count, x, dy, chips, blocks):
    slots, tokens, features = x.shape[2:]
    width = dy.shape[4]
    rows = features // (2 * chips)
    return pl.pallas_call(
        functools.partial(first_kernel, chips, blocks),
        out_shape=(
            jax.ShapeDtypeStruct((rows, width), jnp.bfloat16),
            jax.ShapeDtypeStruct((slots, tokens, width), dy.dtype),
        )
        + (jax.ShapeDtypeStruct((slots, tokens, rows), x.dtype),) * len(blocks),
        in_specs=[HBM, SMEM, HBM, HBM],
        out_specs=(VMEM,) * (2 + len(blocks)),
        scratch_shapes=[
            pltpu.SMEM(queue.shape, queue.dtype),
            pltpu.SemaphoreType.DMA((2 + len(blocks),)),
        ],
        compiler_params=vmem_limit(12),
        cost_estimate=cost("first_product"),
        name="first_product",
    )(queue, count, x, dy)


def product(queue, count, x, dy, block, chips, rows, sections=(0, 1), others=(), ready=(), stacked=False, dtype=jnp.bfloat16, name=""):
    width = dy.shape[2]
    if stacked:
        outs = (jax.ShapeDtypeStruct((len(ready) + len(sections), rows, width), dtype),)
    else:
        outs = (jax.ShapeDtypeStruct((rows, width), dtype),) * len(sections)
    return pl.pallas_call(
        functools.partial(product_kernel, sections, chips, block, len(others), len(ready), stacked),
        out_shape=outs,
        in_specs=[SMEM, SMEM] + [VMEM] * (2 + len(others) + len(ready)),
        out_specs=(VMEM,) * len(outs),
        compiler_params=vmem_limit(8),
        cost_estimate=cost(name),
        name=name,
    )(queue, count, x, dy, *others, *ready)


def sum_kernel(a, b, out):
    sections, rows, _ = a.shape
    slab = 64
    per = rows // slab

    def step(i, carry):
        section, span = lax.div(i, per), pl.ds(pl.multiple_of(lax.rem(i, per) * slab, slab), slab)
        out[section, span, :] = (
            a[section, span, :].astype(jnp.float32) + b[section, span, :].astype(jnp.float32)
        ).astype(out.dtype)
        return carry

    lax.fori_loop(0, sections * per, step, 0)


def add(a, b):
    return pl.pallas_call(
        sum_kernel,
        out_shape=jax.ShapeDtypeStruct(a.shape, a.dtype),
        in_specs=[VMEM, VMEM],
        out_specs=VMEM,
        compiler_params=vmem_limit(4),
        cost_estimate=cost("ring_add"),
        name="ring_add",
    )(a, b)


def total_kernel(own, summed, plain, grad, squares):
    slab = 16
    _, rows, width = own.shape

    def step(i, kept):
        span = pl.ds(pl.multiple_of(i * slab, slab), slab)
        for section in range(own.shape[0]):
            total = own[section, span, :] + summed[section, span, :].astype(jnp.float32)
            total = total + plain[section, span, :].astype(jnp.float32)
            grad[section, span, :] = total
            kept = kept + total * total
        return kept

    kept = lax.fori_loop(0, rows // slab, step, jnp.zeros((slab, width), jnp.float32))
    squares[...] = jnp.full(squares.shape, jnp.sum(kept), jnp.float32)


def totals(peers, own, summed, plain):
    return pl.pallas_call(
        total_kernel,
        out_shape=(
            jax.ShapeDtypeStruct(own.shape, jnp.float32),
            jax.ShapeDtypeStruct((peers, 128), jnp.float32),
        ),
        in_specs=[VMEM] * 3,
        out_specs=(VMEM, VMEM),
        compiler_params=vmem_limit(4),
        cost_estimate=cost("totals"),
        name="totals",
    )(own, summed, plain)


def update_kernel(max_norm, squares, grad, master, moment, variance, new_master, new_moment, norm_out, masters, moments, sems):
    norm = jnp.sqrt(jnp.sum(squares[:, 0:1]))
    clip = jnp.minimum(jnp.float32(1.0), max_norm / (norm + 1e-06))
    norm_out[0, 0] = norm
    sections, rows, width = grad.shape
    chunk, slab = 128, 64
    per = rows // chunk

    def copies(i):
        section, span = lax.div(i, per), pl.ds(pl.multiple_of(lax.rem(i, per) * chunk, chunk), chunk)
        return (
            pltpu.make_async_copy(masters.at[section, span], new_master.at[section, span], sems.at[0, i]),
            pltpu.make_async_copy(moments.at[section, span], new_moment.at[section, span], sems.at[1, i]),
        )

    def one(i, carry):
        section = lax.div(i, per)

        def step(j, inner):
            span = pl.ds(pl.multiple_of(lax.rem(i, per) * chunk + j * slab, slab), slab)
            scaled = clip * grad[section, span, :]
            fresh = 0.9 * moment[section, span, :] + 0.1 * scaled
            second = (0.95 / second_fix) * variance[section, span, :] + (0.05 / second_fix) * (scaled * scaled)
            update = ((0.01 / first_fix) * fresh) / (jnp.sqrt(second) + 1e-08)
            moments[section, span, :] = fresh
            masters[section, span, :] = (1.0 - 0.001) * master[section, span, :] - update
            return inner

        lax.fori_loop(0, chunk // slab, step, 0)
        for copy in copies(i):
            copy.start()
        return carry

    lax.fori_loop(0, sections * per, one, 0)

    def finish(i, carry):
        for copy in copies(i):
            copy.wait()
        return carry

    lax.fori_loop(0, sections * per, finish, 0)


def adam(max_norm, squares, grad, master, moment, variance):
    sections, rows, width = grad.shape
    state = jax.ShapeDtypeStruct(grad.shape, jnp.float32)
    return pl.pallas_call(
        functools.partial(update_kernel, max_norm),
        out_shape=(state, state, jax.ShapeDtypeStruct((1, 1), jnp.float32)),
        in_specs=[VMEM] * 5,
        out_specs=(HBM, HBM, SMEM),
        scratch_shapes=[
            pltpu.VMEM(grad.shape, jnp.float32),
            pltpu.VMEM(grad.shape, jnp.float32),
            pltpu.SemaphoreType.DMA((2, sections * rows // 128)),
        ],
        compiler_params=vmem_limit(8),
        cost_estimate=cost("adam"),
        name="adam",
    )(squares, grad, master, moment, variance)


def after(value, *earlier):
    return lax.optimization_barrier((value, earlier))[0]


def on_device(stash_x, stash_dy, queue, micro_count, master, moment, variance):
    own_rows, kv_width = master.shape[2:]
    peers = lax.axis_size("dp")
    chips = peers // 2
    everyone = lax.axis_size("pipe") * peers
    hbm_queue, hbm_x, hbm_dy = (
        pltpu.with_memory_space_constraint(value, pltpu.HBM) for value in (queue, stash_x, stash_dy)
    )

    def ring(sign):
        return [
            (i, (i // 2 + sign * (1 - 2 * (i % 2))) % chips * 2 + i % 2) for i in range(peers)
        ]

    def sibling(value):
        return lax.ppermute(value, "dp", [(i, i ^ 1) for i in range(peers)])

    def along(value):
        return lax.ppermute(value, "dp", ring(1))

    def against(value):
        return lax.ppermute(value, "dp", ring(-1))

    sent_a, dy, x_send, x_keep = first_product(hbm_queue, micro_count, hbm_x, hbm_dy, chips, ((-2, False), (2, True)))
    other_a = sibling(sent_a)
    block = functools.partial(product, queue, micro_count, chips=chips, rows=own_rows)
    (sent_b,) = block(x_send, dy, (-2, False), sections=(1,), name="far_send_b")
    other_b = sibling(sent_b)
    others = {}

    def send(step, dy):
        sent = block(stash_x, dy, (step, False), name=f"send_{step % chips}")
        others[-step] = [sibling(value) for value in sent]
        return sent[0]

    def keep(step, dy, dtype=jnp.bfloat16):
        (kept,) = block(stash_x, dy, (step, True), others=others[step], stacked=True, dtype=dtype, name=f"keep_{step % chips}")
        return kept

    (far_a,) = block(x_keep, after(dy, sent_b), (2, True), sections=(0,), others=(other_a,), name="far_keep_a")
    (far,) = block(
        x_keep, after(dy, far_a), (2, True), sections=(1,), others=(other_b,), ready=(far_a,), stacked=True, name="far_keep_b"
    )
    came = along(far)
    dy = after(dy, send(1, after(dy, far)))
    dy = after(dy, send(-1, dy))
    near_b = keep(-1, dy)
    plain = against(near_b)
    near_a = keep(1, after(dy, near_b))
    near_a = add(near_a, came)
    summed = along(near_a)
    dy = after(dy, send(0, after(dy, near_a)))
    own = keep(0, dy, jnp.float32)
    grad, squares = totals(everyone, own, summed, plain)
    squares = lax.all_to_all(squares, ("pipe", "dp"), 0, 0, tiled=True)
    max_norm = 0.05 * math.sqrt(2 * lax.axis_size("pipe") * own_rows * peers * kv_width)
    new_master, new_moment, norm = adam(max_norm, squares, grad, master[0], moment[0], variance[0])
    return (new_master[None], new_moment[None], norm[0, 0])


def solution(mesh):
    in_specs = (
        P("pipe", "dp", None, None, None),
        P("pipe", "dp", None, None, None),
        P("pipe", None),
        P("dp"),
        P("pipe", None, "dp", None),
        P("pipe", None, "dp", None),
        P("pipe", None, "dp", None),
    )
    out_specs = (P("pipe", None, "dp", None), P("pipe", None, "dp", None), P())
    return jax.shard_map(
        on_device, mesh=mesh, in_specs=in_specs, out_specs=out_specs, check_vma=False
    )
```

time: 98.3 us -> 70.9 us (0.72)
  Pallas kernels: 53.6 us -> 21.3 us
  waiting for transfers between devices: 8.87 us -> 18.5 us
  local copies, waits for them, and re-layouts: 3.68 us -> 0.04 us
  starting transfers between devices: 12.7 us -> 10.8 us
  blocking collectives: 17.4 us -> 18.6 us
    pallas_call x10 -> x12, Pallas kernels: 49.4 us -> 20.9 us  [the longest x9 14.1 us: product(): pl.pallas_call(functools.partial(product_kernel, sections, chips, block,...]
    ppermute x3 -> x2, waiting for transfers between devices: 5.07 us -> 15.1 us  [along(): return lax.ppermute(value, 'dp', ring(1))]
    pallas_call x2 -> x1, Pallas kernels: 4.22 us -> 0.37 us  [add(): pl.pallas_call(sum_kernel, out_shape=jax.ShapeDtypeStruct(a.shape, a.dtyp...]
    unnamed x20 -> x14, local copies, waits for them, and re-layouts: 3.68 us -> 0.04 us
    ppermute x3 -> x1, waiting for transfers between devices: 3.78 us -> 0.29 us  [against(): return lax.ppermute(value, 'dp', ring(-1))]
    ppermute x8, waiting for transfers between devices: 0.02 us -> 3.12 us  [sibling(): return lax.ppermute(value, 'dp', [(i, i ^ 1) for i in range(peers)])]
    ppermute x3 -> x2, starting transfers between devices: 9 us -> 7.39 us  [along(): return lax.ppermute(value, 'dp', ring(1))]
    all_to_all x1, blocking collectives: 17.4 us -> 18.6 us  [on_device(): squares = lax.all_to_all(squares, ('pipe', 'dp'), 0, 0, tiled=True)]
  transfers between devices with their start and end apart: 14 -> 11, of which waited for: 2 -> 8; matrix products, arithmetic and copies ran while one was open for 0% -> 0% of each run, Pallas kernels for 42% -> 19%
where the time goes in v2:
time: 70.9 us; the launch traced here: 70.8 us
  Pallas kernels  21.3 us (30%)
  blocking collectives  18.6 us (26%)
  waiting for transfers between devices  18.5 us (26%)
  starting transfers between devices  10.8 us (15%)
  between operations  1.46 us (2%)
    all_to_all x1, blocking collectives, on_device(): squares = lax.all_to_all(squares, ('pipe', 'dp'), 0, 0, tiled=True)  18.6 us
    ppermute x2, waiting for transfers between devices, along(): return lax.ppermute(value, 'dp', ring(1))  15.1 us
    pallas_call x9, Pallas kernels, product(): pl.pallas_call(functools.partial(product_kernel, sections, chips, block,...  14.1 us
    ppermute x2, starting transfers between devices, along(): return lax.ppermute(value, 'dp', ring(1))  7.39 us
    ppermute x8, starting transfers between devices, sibling(): return lax.ppermute(value, 'dp', [(i, i ^ 1) for i in range(peers)])  3.36 us
    pallas_call x1, Pallas kernels, adam(): pl.pallas_call(functools.partial(update_kernel, max_norm), out_shape=(sta...  3.35 us
    ppermute x8, waiting for transfers between devices, sibling(): return lax.ppermute(value, 'dp', [(i, i ^ 1) for i in range(peers)])  3.12 us
    pallas_call x1, Pallas kernels, first_product(): pl.pallas_call(functools.partial(first_kernel, chips, blocks), out_shape=...  2.69 us
  transfers between devices with their start and end apart: 11, of which 8 were waited for; matrix products, arithmetic and copies ran while one was open for 0% of the time, Pallas kernels for 19%

profile of v2, /device:TPU:1, one launch (start us, length us, event | category | flops | bytes accessed | tf_op | source)
XLA Modules:
  0.0 70.8 jit_solution(2485821877687590762)
XLA Ops:
  1.3 2.7 %first_product.1 = (bf16[512,512]{1,0:T(8,128)(2,1)S(1)}, bf16[12,128,512]{2,1,0:T(8,128)(2,1)S(1)}, bf16[12,128,512]{2,1,0:T(8,128)(2,1)S(1)}, bf16[12,128,512]{2,1,0:T(8,128)(2,1)S(1)}) custom-call(s32[1,12]{1,0:T(1,128)} %refs_0_.17, s32[1]{0:T(128)S(6)} %copy.11.count.refs_1_, bf16[1,1,12,128,4096]{4,3,2,1,0:T(8,128)(2,1)} %refs_2_.11, ...), custom_call_target="tpu_custom_call" | custom-call | flops 1 | bytes 1 | tf_op jit(solution)/shard_map/first_product/pallas_call | solution.py:129
  4.0 1.5 %collective-permute-start = (bf16[512,512]{1,0:T(8,128)(2,1)S(1)}, bf16[512,512]{1,0:T(8,128)(2,1)S(1)}, u32[]{:S(2)}, u32[]{:S(2)}) collective-permute-start(bf16[512,512]{1,0:T(8,128)(2,1)S(1)} %get-tuple-element.30), channel_id=1, source_target_pairs={{0,1},{1,0},{2,3},{3,2},{4,5},{5,4},{6,7},{7,6},{8,9},{9,8},{10,11... | collective-permute-start | bytes 1572872 | tf_op jit(solution)/shard_map/ppermute | solution.py:305
  5.5 1.2 %far_send_b.1 = bf16[512,512]{1,0:T(8,128)(2,1)S(1)} custom-call(s32[1,12]{1,0:T(1,128)S(1)} %copy-done.3, s32[1]{0:T(128)S(6)} %copy.11.count.refs_1_, bf16[12,128,512]{2,1,0:T(8,128)(2,1)S(1)} %get-tuple-element.28.refs_2_, bf16[12,128,512]{2,1,0:T(8,128)(2,1)S(1)} %get-tuple-element.42.refs_3_), custom_call_target="tpu_custom_call" | custom-call | flops 1 | bytes 1 | tf_op jit(solution)/shard_map/far_send_b/pallas_call | solution.py:154
  6.7 0.1 collective-permute-start.1
  6.8 0.3 collective-permute-done.refs_4_
  7.0 1.2 %far_keep_a.1.refs_5_ = bf16[512,512]{1,0:T(8,128)(2,1)S(1)} custom-call(s32[1,12]{1,0:T(1,128)S(1)} %copy-done.3, s32[1]{0:T(128)S(6)} %copy.11.count.refs_1_, bf16[12,128,512]{2,1,0:T(8,128)(2,1)S(1)} %get-tuple-element.27.refs_2_, bf16[12,128,512]{2,1,0:T(8,128)(2,1)S(1)} %get-tuple-element.42.refs_3_, bf16[512,512]{1,0:T(8,128)(2,1)S(1)} %collective-permute-done.refs_4_), custom_call_target="tpu_custom_call" | custom-call | flops 1 | bytes 1 | tf_op jit(solution)/shard_map/far_keep_a/pallas_call | solution.py:154
  8.2 0.4 collective-permute-done.1.refs_4_
  8.7 1.2 %far_keep_b.1 = bf16[2,512,512]{2,1,0:T(8,128)(2,1)S(1)} custom-call(s32[1,12]{1,0:T(1,128)S(1)} %copy-done.3, s32[1]{0:T(128)S(6)} %copy.11.count.refs_1_, bf16[12,128,512]{2,1,0:T(8,128)(2,1)S(1)} %get-tuple-element.27.refs_2_, bf16[12,128,512]{2,1,0:T(8,128)(2,1)S(1)} %get-tuple-element.42.refs_3_, bf16[512,512]{1,0:T(8,128)(2,1)S(1)} %collective-permute-done.1.refs_4_, ...), custom_call_target="tpu_custom_call" | custom-call | flops 1 | bytes 1 | tf_op jit(solution)/shard_map/far_keep_b/pallas_call | solution.py:154
  9.9 3.9 %collective-permute-start.6 = (bf16[2,512,512]{2,1,0:T(8,128)(2,1)S(1)}, bf16[2,512,512]{2,1,0:T(8,128)(2,1)S(1)}, u32[]{:S(2)}, u32[]{:S(2)}) collective-permute-start(bf16[2,512,512]{2,1,0:T(8,128)(2,1)S(1)} %far_keep_b.1), channel_id=1, source_target_pairs={{0,2},{1,7},{2,4},{3,1},{4,6},{5,3},{6,0},{7,5},{8,10},{9,15},{10,... | collective-permute-start | bytes 3145736 | tf_op jit(solution)/shard_map/ppermute | solution.py:308
  13.8 1.8 %send_1.1 = (bf16[512,512]{1,0:T(8,128)(2,1)S(1)}, bf16[512,512]{1,0:T(8,128)(2,1)S(1)}) custom-call(s32[1,12]{1,0:T(1,128)S(1)} %copy-done.3, s32[1]{0:T(128)S(6)} %copy.11.count.refs_1_, bf16[1,1,12,128,4096]{4,3,2,1,0:T(8,128)(2,1)S(1)} %bitcast.11, bf16[12,128,512]{2,1,0:T(8,128)(2,1)S(1)} %get-tuple-element.42.refs_3_), custom_call_target="tpu_custom_call" | custom-call | flops 1 | bytes 1 | tf_op jit(solution)/shard_map/send_1/pallas_call | solution.py:154
  15.6 0.1 collective-permute-start.3
  15.6 0.5 collective-permute-start.2
  16.1 1.8 %send_3.1 = (bf16[512,512]{1,0:T(8,128)(2,1)S(1)}, bf16[512,512]{1,0:T(8,128)(2,1)S(1)}) custom-call(s32[1,12]{1,0:T(1,128)S(1)} %copy-done.3, s32[1]{0:T(128)S(6)} %copy.11.count.refs_1_, bf16[1,1,12,128,4096]{4,3,2,1,0:T(8,128)(2,1)S(1)} %bitcast.11, bf16[12,128,512]{2,1,0:T(8,128)(2,1)S(1)} %get-tuple-element.42.refs_3_), custom_call_target="tpu_custom_call" | custom-call | flops 1 | bytes 1 | tf_op jit(solution)/shard_map/send_3/pallas_call | solution.py:154
  17.9 0.2 collective-permute-start.5
  18.1 0.4 collective-permute-start.4
  18.5 1.8 %keep_3.1 = bf16[2,512,512]{2,1,0:T(8,128)(2,1)S(1)} custom-call(s32[1,12]{1,0:T(1,128)S(1)} %copy-done.3, s32[1]{0:T(128)S(6)} %copy.11.count.refs_1_, bf16[1,1,12,128,4096]{4,3,2,1,0:T(8,128)(2,1)S(1)} %bitcast.11, bf16[12,128,512]{2,1,0:T(8,128)(2,1)S(1)} %get-tuple-element.42.refs_3_, bf16[512,512]{1,0:T(8,128)(2,1)S(1)} %collective-permute-done.2.refs_4_, ...), custom_call_target="tpu_custom_call" | custom-call | flops 1 | bytes 1 | tf_op jit(solution)/shard_map/keep_3/pallas_call | solution.py:154
  20.4 0.3 collective-permute-done.4.refs_4_
  20.7 1.8 %keep_1.1.a = bf16[2,512,512]{2,1,0:T(8,128)(2,1)S(1)} custom-call(s32[1,12]{1,0:T(1,128)S(1)} %copy-done.3, s32[1]{0:T(128)S(6)} %copy.11.count.refs_1_, bf16[1,1,12,128,4096]{4,3,2,1,0:T(8,128)(2,1)S(1)} %bitcast.11, bf16[12,128,512]{2,1,0:T(8,128)(2,1)S(1)} %get-tuple-element.42.refs_3_, bf16[512,512]{1,0:T(8,128)(2,1)S(1)} %collective-permute-done.4.refs_4_, ...), custom_call_target="tpu_custom_call" | custom-call | flops 1 | bytes 1 | tf_op jit(solution)/shard_map/keep_1/pallas_call | solution.py:154
  22.4 7.0 %collective-permute-done.6.b = bf16[2,512,512]{2,1,0:T(8,128)(2,1)S(1)} collective-permute-done((bf16[2,512,512]{2,1,0:T(8,128)(2,1)S(1)}, bf16[2,512,512]{2,1,0:T(8,128)(2,1)S(1)}, u32[]{:S(2)}, u32[]{:S(2)}) %collective-permute-start.6) | collective-permute-done | bytes 1048608 | tf_op jit(solution)/shard_map/ppermute | solution.py:308
  29.4 0.4 ring_add.1
  29.8 3.5 %collective-permute-start.9 = (bf16[2,512,512]{2,1,0:T(8,128)(2,1)S(1)}, bf16[2,512,512]{2,1,0:T(8,128)(2,1)S(1)}, u32[]{:S(2)}, u32[]{:S(2)}) collective-permute-start(bf16[2,512,512]{2,1,0:T(8,128)(2,1)S(1)} %ring_add.1), channel_id=1, source_target_pairs={{0,2},{1,7},{2,4},{3,1},{4,6},{5,3},{6,0},{7,5},{8,10},{9,15},{10,... | collective-permute-start | bytes 3145736 | tf_op jit(solution)/shard_map/ppermute | solution.py:308
  33.3 1.7 %send_0.1 = (bf16[512,512]{1,0:T(8,128)(2,1)S(1)}, bf16[512,512]{1,0:T(8,128)(2,1)S(1)}) custom-call(s32[1,12]{1,0:T(1,128)S(1)} %copy-done.3, s32[1]{0:T(128)S(6)} %copy.11.count.refs_1_, bf16[1,1,12,128,4096]{4,3,2,1,0:T(8,128)(2,1)S(1)} %bitcast.11, bf16[12,128,512]{2,1,0:T(8,128)(2,1)S(1)} %get-tuple-element.42.refs_3_), custom_call_target="tpu_custom_call" | custom-call | flops 1 | bytes 1 | tf_op jit(solution)/shard_map/send_0/pallas_call | solution.py:154
  35.1 0.1 collective-permute-start.8
  35.1 0.5 collective-permute-start.7
  35.6 1.4 %collective-permute-done.8.refs_5_ = bf16[512,512]{1,0:T(8,128)(2,1)S(1)} collective-permute-done((bf16[512,512]{1,0:T(8,128)(2,1)S(1)}, bf16[512,512]{1,0:T(8,128)(2,1)S(1)}, u32[]{:S(2)}, u32[]{:S(2)}) %collective-permute-start.8) | collective-permute-done | bytes 524320 | tf_op jit(solution)/shard_map/ppermute | solution.py:305
  37.0 0.7 %collective-permute-done.7.refs_4_ = bf16[512,512]{1,0:T(8,128)(2,1)S(1)} collective-permute-done((bf16[512,512]{1,0:T(8,128)(2,1)S(1)}, bf16[512,512]{1,0:T(8,128)(2,1)S(1)}, u32[]{:S(2)}, u32[]{:S(2)}) %collective-permute-start.7) | collective-permute-done | bytes 524320 | tf_op jit(solution)/shard_map/ppermute | solution.py:305
  37.8 1.8 %keep_0.1.own = f32[2,512,512]{2,1,0:T(8,128)S(1)} custom-call(s32[1,12]{1,0:T(1,128)S(1)} %copy-done.3, s32[1]{0:T(128)S(6)} %copy.11.count.refs_1_, bf16[1,1,12,128,4096]{4,3,2,1,0:T(8,128)(2,1)S(1)} %bitcast.11, bf16[12,128,512]{2,1,0:T(8,128)(2,1)S(1)} %get-tuple-element.42.refs_3_, bf16[512,512]{1,0:T(8,128)(2,1)S(1)} %collective-permute-done.7.refs_4_, ...), custom_call_target="tpu_custom_call" | custom-call | flops 1 | bytes 1 | tf_op jit(solution)/shard_map/keep_0/pallas_call | solution.py:154
  39.6 0.3 collective-permute-done.10.plain
  39.9 8.1 %collective-permute-done.9.summed = bf16[2,512,512]{2,1,0:T(8,128)(2,1)S(1)} collective-permute-done((bf16[2,512,512]{2,1,0:T(8,128)(2,1)S(1)}, bf16[2,512,512]{2,1,0:T(8,128)(2,1)S(1)}, u32[]{:S(2)}, u32[]{:S(2)}) %collective-permute-start.9) | collective-permute-done | bytes 1048608 | tf_op jit(solution)/shard_map/ppermute | solution.py:308
  48.0 0.8 %totals.1 = (f32[2,512,512]{2,1,0:T(8,128)S(1)}, f32[128,128]{1,0:T(8,128)S(1)}) custom-call(f32[2,512,512]{2,1,0:T(8,128)S(1)} %keep_0.1.own, bf16[2,512,512]{2,1,0:T(8,128)(2,1)S(1)} %collective-permute-done.9.summed, bf16[2,512,512]{2,1,0:T(8,128)(2,1)S(1)} %collective-permute-done.10.plain), custom_call_target="tpu_custom_call" | custom-call | flops 1 | bytes 1 | tf_op jit(solution)/shard_map/totals/pallas_call | solution.py:210
  48.8 18.6 %all_to_all.11 = f32[128,1,128]{2,1,0:T(1,128)S(1)} all-to-all(f32[128,1,128]{2,1,0:T(1,128)S(1)} %bitcast.16), channel_id=1, replica_groups=mesh['pipe'=16,'dp'=8] {'pipe','dp'}, dimensions={0} | all-to-all | bytes 131072 | tf_op jit(solution)/shard_map/all_to_all | solution.py:344
  67.4 3.4 %adam.1 = (f32[2,512,512]{2,1,0:T(8,128)}, f32[2,512,512]{2,1,0:T(8,128)}, f32[1,1]{1,0:T(1,128)}) custom-call(f32[128,128]{1,0:T(8,128)S(1)} %bitcast.15, f32[2,512,512]{2,1,0:T(8,128)S(1)} %get-tuple-element.45.grad, f32[2,512,512]{2,1,0:T(8,128)S(1)} %bitcast.12, f32[2,512,512]{2,1,0:T(8,128)S(1)} %bitcast.13, f32[2,512,512]{2,1,0:T(8,128)S(1)} %bitcast.14), custom_call_target="tpu_custom_call" | custom-call | flops 1 | bytes 1 | tf_op jit(solution)/shard_map/adam/pallas_call | solution.py:270
  (19 shorter events, 0.1 us)
Async XLA Ops:
  1.3 4.2 %copy-start.3 = (s32[1,12]{1,0:T(1,128)S(1)}, s32[1,12]{1,0:T(1,128)}, u32[]{:S(2)}) copy-start(s32[1,12]{1,0:T(1,128)} %refs_0_.17) | copy-start | bytes 148
  1.3 12.5 %slice-start = ((s8[12582912]{0:T(1024)(128)(4,1)}), s8[4194304]{0:T(1024)(128)(4,1)S(1)}, s32[]{:S(2)}) async-start(s8[12582912]{0:T(1024)(128)(4,1)} %bitcast.10), calls=%async_computation.1 | async-start | bytes 8388608
  1.3 12.5 %slice-start.1 = ((s8[12582912]{0:T(1024)(128)(4,1)}), s8[4194304]{0:T(1024)(128)(4,1)S(1)}, s32[]{:S(2)}) async-start(s8[12582912]{0:T(1024)(128)(4,1)} %bitcast.10), calls=%async_computation.2 | async-start | bytes 8388608
  4.0 3.0 %collective-permute-start = (bf16[512,512]{1,0:T(8,128)(2,1)S(1)}, bf16[512,512]{1,0:T(8,128)(2,1)S(1)}, u32[]{:S(2)}, u32[]{:S(2)}) collective-permute-start(bf16[512,512]{1,0:T(8,128)(2,1)S(1)} %get-tuple-element.30), channel_id=1, source_target_pairs={{0,1},{1,0},{2,3},{3,2},{4,5},{5,4},{6,7},{7,6},{8,9},{9,8},{10,11... | collective-permute-start | bytes 1572872 | tf_op jit(solution)/shard_map/ppermute | solution.py:305
  6.7 2.0 %collective-permute-start.1 = (bf16[512,512]{1,0:T(8,128)(2,1)S(1)}, bf16[512,512]{1,0:T(8,128)(2,1)S(1)}, u32[]{:S(2)}, u32[]{:S(2)}) collective-permute-start(bf16[512,512]{1,0:T(8,128)(2,1)S(1)} %far_send_b.1), channel_id=1, source_target_pairs={{0,1},{1,0},{2,3},{3,2},{4,5},{5,4},{6,7},{7,6},{8,9},{9,8},{10,11... | collective-permute-start | bytes 1572872 | tf_op jit(solution)/shard_map/ppermute | solution.py:305
  7.0 6.7 %slice-start.2 = ((s8[12582912]{0:T(1024)(128)(4,1)}), s8[4194304]{0:T(1024)(128)(4,1)S(1)}, s32[]{:S(2)}) async-start(s8[12582912]{0:T(1024)(128)(4,1)} %bitcast.10), calls=%async_computation.3 | async-start | bytes 8388608
  9.9 19.6 %collective-permute-start.6 = (bf16[2,512,512]{2,1,0:T(8,128)(2,1)S(1)}, bf16[2,512,512]{2,1,0:T(8,128)(2,1)S(1)}, u32[]{:S(2)}, u32[]{:S(2)}) collective-permute-start(bf16[2,512,512]{2,1,0:T(8,128)(2,1)S(1)} %far_keep_b.1), channel_id=1, source_target_pairs={{0,2},{1,7},{2,4},{3,1},{4,6},{5,3},{6,0},{7,5},{8,10},{9,15},{10,... | collective-permute-start | bytes 3145736 | tf_op jit(solution)/shard_map/ppermute | solution.py:308
  15.6 3.0 %collective-permute-start.3 = (bf16[512,512]{1,0:T(8,128)(2,1)S(1)}, bf16[512,512]{1,0:T(8,128)(2,1)S(1)}, u32[]{:S(2)}, u32[]{:S(2)}) collective-permute-start(bf16[512,512]{1,0:T(8,128)(2,1)S(1)} %get-tuple-element.37), channel_id=1, source_target_pairs={{0,1},{1,0},{2,3},{3,2},{4,5},{5,4},{6,7},{7,6},{8,9},{9,8},{10,11... | collective-permute-start | bytes 1572872 | tf_op jit(solution)/shard_map/ppermute | solution.py:305
  15.6 2.9 %collective-permute-start.2 = (bf16[512,512]{1,0:T(8,128)(2,1)S(1)}, bf16[512,512]{1,0:T(8,128)(2,1)S(1)}, u32[]{:S(2)}, u32[]{:S(2)}) collective-permute-start(bf16[512,512]{1,0:T(8,128)(2,1)S(1)} %get-tuple-element.33), channel_id=1, source_target_pairs={{0,1},{1,0},{2,3},{3,2},{4,5},{5,4},{6,7},{7,6},{8,9},{9,8},{10,11... | collective-permute-start | bytes 1572872 | tf_op jit(solution)/shard_map/ppermute | solution.py:305
  17.9 2.5 %collective-permute-start.5 = (bf16[512,512]{1,0:T(8,128)(2,1)S(1)}, bf16[512,512]{1,0:T(8,128)(2,1)S(1)}, u32[]{:S(2)}, u32[]{:S(2)}) collective-permute-start(bf16[512,512]{1,0:T(8,128)(2,1)S(1)} %get-tuple-element.39), channel_id=1, source_target_pairs={{0,1},{1,0},{2,3},{3,2},{4,5},{5,4},{6,7},{7,6},{8,9},{9,8},{10,11... | collective-permute-start | bytes 1572872 | tf_op jit(solution)/shard_map/ppermute | solution.py:305
  18.1 2.6 %collective-permute-start.4 = (bf16[512,512]{1,0:T(8,128)(2,1)S(1)}, bf16[512,512]{1,0:T(8,128)(2,1)S(1)}, u32[]{:S(2)}, u32[]{:S(2)}) collective-permute-start(bf16[512,512]{1,0:T(8,128)(2,1)S(1)} %get-tuple-element.35), channel_id=1, source_target_pairs={{0,1},{1,0},{2,3},{3,2},{4,5},{5,4},{6,7},{7,6},{8,9},{9,8},{10,11... | collective-permute-start | bytes 1572872 | tf_op jit(solution)/shard_map/ppermute | solution.py:305
  20.3 19.6 %collective-permute-start.10 = (bf16[2,512,512]{2,1,0:T(8,128)(2,1)S(1)}, bf16[2,512,512]{2,1,0:T(8,128)(2,1)S(1)}, u32[]{:S(2)}, u32[]{:S(2)}) collective-permute-start(bf16[2,512,512]{2,1,0:T(8,128)(2,1)S(1)} %keep_3.1), channel_id=1, source_target_pairs={{0,6},{1,3},{2,0},{3,5},{4,2},{5,7},{6,4},{7,1},{8,14},{9,11},{10,... | collective-permute-start | bytes 3145736 | tf_op jit(solution)/shard_map/ppermute | solution.py:311
  29.8 18.2 %collective-permute-start.9 = (bf16[2,512,512]{2,1,0:T(8,128)(2,1)S(1)}, bf16[2,512,512]{2,1,0:T(8,128)(2,1)S(1)}, u32[]{:S(2)}, u32[]{:S(2)}) collective-permute-start(bf16[2,512,512]{2,1,0:T(8,128)(2,1)S(1)} %ring_add.1), channel_id=1, source_target_pairs={{0,2},{1,7},{2,4},{3,1},{4,6},{5,3},{6,0},{7,5},{8,10},{9,15},{10,... | collective-permute-start | bytes 3145736 | tf_op jit(solution)/shard_map/ppermute | solution.py:308
  35.1 2.0 %collective-permute-start.8 = (bf16[512,512]{1,0:T(8,128)(2,1)S(1)}, bf16[512,512]{1,0:T(8,128)(2,1)S(1)}, u32[]{:S(2)}, u32[]{:S(2)}) collective-permute-start(bf16[512,512]{1,0:T(8,128)(2,1)S(1)} %get-tuple-element.43), channel_id=1, source_target_pairs={{0,1},{1,0},{2,3},{3,2},{4,5},{5,4},{6,7},{7,6},{8,9},{9,8},{10,11... | collective-permute-start | bytes 1572872 | tf_op jit(solution)/shard_map/ppermute | solution.py:305
  35.1 2.6 %collective-permute-start.7 = (bf16[512,512]{1,0:T(8,128)(2,1)S(1)}, bf16[512,512]{1,0:T(8,128)(2,1)S(1)}, u32[]{:S(2)}, u32[]{:S(2)}) collective-permute-start(bf16[512,512]{1,0:T(8,128)(2,1)S(1)} %get-tuple-element.41), channel_id=1, source_target_pairs={{0,1},{1,0},{2,3},{3,2},{4,5},{5,4},{6,7},{7,6},{8,9},{9,8},{10,11... | collective-permute-start | bytes 1572872 | tf_op jit(solution)/shard_map/ppermute | solution.py:305
  37.8 29.6 %copy-start.2 = (f32[1,2,512,512]{3,2,1,0:T(8,128)S(1)}, f32[1,2,512,512]{3,2,1,0:T(8,128)}, u32[]{:S(2)}) copy-start(f32[1,2,512,512]{3,2,1,0:T(8,128)} %param.13) | copy-start | bytes 6291460
  39.6 27.8 %copy-start = (f32[1,2,512,512]{3,2,1,0:T(8,128)S(1)}, f32[1,2,512,512]{3,2,1,0:T(8,128)}, u32[]{:S(2)}) copy-start(f32[1,2,512,512]{3,2,1,0:T(8,128)} %param.11) | copy-start | bytes 6291460
  39.6 27.8 %copy-start.1 = (f32[1,2,512,512]{3,2,1,0:T(8,128)S(1)}, f32[1,2,512,512]{3,2,1,0:T(8,128)}, u32[]{:S(2)}) copy-start(f32[1,2,512,512]{3,2,1,0:T(8,128)} %param.12) | copy-start | bytes 6291460

commit v3 on v2

--- a/solution.py
+++ b/solution.py
@@ -28,37 +28,22 @@
     return 2 * target + (core if mine else 1 - core)
 
 
-def section_product(section, queue, count, x_of, rows, dy_ref, tile, store):
-    slots = dy_ref.shape[0]
-    width = dy_ref.shape[2]
-    half = slots // 2
-    live = count[0]
-    picked = []
-    for micro in range(half):
-        slot = jnp.int32(0)
-        for place_in_stash in range(slots):
-            slot = jnp.where(queue[0, place_in_stash] == section * half + micro, place_in_stash, slot)
-        picked.append(slot)
-    dy = []
-    for micro, slot in enumerate(picked):
-        value = dy_ref[slot]
-        dy.append(jnp.where(micro < live, value, jnp.zeros_like(value)))
-    dy = jnp.concatenate(dy, axis=0)
+def section_product(slots, section, x_of, dy_ref, rows, store):
+    tile = min(256, rows)
     for start in range(0, rows, tile):
-        x = jnp.concatenate([x_of(slot, start, tile) for slot in picked], axis=0)
+        x = jnp.concatenate([x_of(slot, start, tile) for slot in slots], axis=0)
         store(
-            start,
-            lax.dot_general(x, dy, (((0,), (0,)), ((), ())), preferred_element_type=jnp.float32),
+            pl.ds(start, tile),
+            lax.dot_general(x, dy_ref[section], (((0,), (0,)), ((), ())), preferred_element_type=jnp.float32),
         )
 
 
-def product_kernel(sections, chips, block, n_others, n_ready, stacked, *refs):
-    queue, count, x_ref, dy_ref = refs[:4]
-    others = refs[4 : 4 + n_others]
-    ready = refs[4 + n_others : 4 + n_others + n_ready]
-    outs = refs[4 + n_others + n_ready :]
-    rows = outs[0].shape[-2]
-    tile = min(256, rows)
+def product_kernel(section, chips, block, has_other, place_in, *refs):
+    plan, x_ref, dy_ref = refs[:3]
+    out = refs[-1]
+    rows = out.shape[-2]
+    half = plan.shape[0] // 2
+    slots = [plan[section * half + micro, 0] for micro in range(half)]
     first = owner_of(block, chips) * rows
 
     def x_of(slot, start, size):
@@ -66,46 +51,57 @@
             return x_ref[slot, :, start : start + size]
         return x_ref[0, 0, slot, :, pl.ds(pl.multiple_of(first + start, size), size)]
 
-    for i, value in enumerate(ready):
-        outs[0][i] = value[...]
-    for i, section in enumerate(sections):
-
-        def store(start, total, i=i):
-            span = pl.ds(start, tile)
-            if others:
-                other = others[i][span, :] if len(others) == len(sections) else others[0][i, span, :]
-                total = total + other.astype(jnp.float32)
-            if stacked:
-                outs[0][n_ready + i, span, :] = total.astype(outs[0].dtype)
-            else:
-                outs[i][span, :] = total.astype(outs[i].dtype)
-
-        section_product(section, queue, count, x_of, rows, dy_ref, tile, store)
-
-
-def first_kernel(chips, blocks, queue_hbm, count, x_hbm, dy_hbm, out, dy_ref, *rest):
-    buffers, (queue, sems) = rest[:-2], rest[-2:]
+    def store(span, total):
+        if has_other:
+            total = total + refs[3][span, :].astype(jnp.float32)
+        if place_in is None:
+            out[span, :] = total.astype(out.dtype)
+        else:
+            out[place_in, span, :] = total.astype(out.dtype)
+
+    section_product(slots, section, x_of, dy_ref, rows, store)
+
+
+def first_kernel(chips, blocks, queue_hbm, count, x_hbm, dy_hbm, out, plan, dy_ref, *rest):
+    buffers, (raw, queue, slot_of, sems) = rest[:-4], rest[-4:]
     rows = buffers[0].shape[2]
+    slots, tokens, _ = raw.shape
+    half = slots // 2
     copies = [
         pltpu.make_async_copy(queue_hbm, queue, sems.at[0]),
-        pltpu.make_async_copy(dy_hbm.at[0, 0], dy_ref, sems.at[1]),
+        pltpu.make_async_copy(dy_hbm.at[0, 0], raw, sems.at[1]),
     ]
     for i, (block, buffer) in enumerate(zip(blocks, buffers)):
         first = pl.multiple_of(owner_of(block, chips) * rows, rows)
         copies.append(pltpu.make_async_copy(x_hbm.at[0, 0, :, :, pl.ds(first, rows)], buffer, sems.at[2 + i]))
     for copy in copies:
         copy.start()
-    for copy in copies[:3]:
-        copy.wait()
-    tile = min(256, rows)
+    copies[0].wait()
+    for slot in range(slots):
+        code = queue[0, slot]
+        slot_of[code] = slot
+        plan[pl.ds(code, 1), :] = jnp.full((1, plan.shape[1]), slot, jnp.int32)
+    live = count[0]
+
+    def order_dy(section):
+        for micro in range(half):
+            value = raw[slot_of[section * half + micro]]
+            dy_ref[section, micro * tokens : (micro + 1) * tokens, :] = jnp.where(
+                micro < live, value, jnp.zeros_like(value)
+            )
+
+    copies[1].wait()
+    order_dy(0)
+    copies[2].wait()
 
     def x_of(slot, start, size):
         return buffers[0][slot, :, start : start + size]
 
-    def store(start, total):
-        out[pl.ds(start, tile), :] = total.astype(out.dtype)
-
-    section_product(0, queue, count, x_of, rows, dy_ref, tile, store)
+    def store(span, total):
+        out[span, :] = total.astype(out.dtype)
+
+    section_product([slot_of[micro] for micro in range(half)], 0, x_of, dy_ref, rows, store)
+    order_dy(1)
     for copy in copies[3:]:
         copy.wait()
 
@@ -130,13 +126,16 @@
         functools.partial(first_kernel, chips, blocks),
         out_shape=(
             jax.ShapeDtypeStruct((rows, width), jnp.bfloat16),
-            jax.ShapeDtypeStruct((slots, tokens, width), dy.dtype),
+            jax.ShapeDtypeStruct((slots, 128), jnp.int32),
+            jax.ShapeDtypeStruct((2, slots // 2 * tokens, width), dy.dtype),
         )
         + (jax.ShapeDtypeStruct((slots, tokens, rows), x.dtype),) * len(blocks),
         in_specs=[HBM, SMEM, HBM, HBM],
-        out_specs=(VMEM,) * (2 + len(blocks)),
+        out_specs=(VMEM,) * (3 + len(blocks)),
         scratch_shapes=[
+            pltpu.VMEM((slots, tokens, width), dy.dtype),
             pltpu.SMEM(queue.shape, queue.dtype),
+            pltpu.SMEM((slots,), jnp.int32),
             pltpu.SemaphoreType.DMA((2 + len(blocks),)),
         ],
         compiler_params=vmem_limit(12),
@@ -145,21 +144,20 @@
     )(queue, count, x, dy)
 
 
-def product(queue, count, x, dy, block, chips, rows, sections=(0, 1), others=(), ready=(), stacked=False, dtype=jnp.bfloat16, name=""):
+def product(plan, x, dy, block, section, chips, rows, other=None, stacked=False, beside=None, dtype=jnp.bfloat16, name=""):
     width = dy.shape[2]
-    if stacked:
-        outs = (jax.ShapeDtypeStruct((len(ready) + len(sections), rows, width), dtype),)
-    else:
-        outs = (jax.ShapeDtypeStruct((rows, width), dtype),) * len(sections)
-    return pl.pallas_call(
-        functools.partial(product_kernel, sections, chips, block, len(others), len(ready), stacked),
-        out_shape=outs,
-        in_specs=[SMEM, SMEM] + [VMEM] * (2 + len(others) + len(ready)),
-        out_specs=(VMEM,) * len(outs),
+    operands = [plan, x, dy] + ([] if other is None else [other]) + ([] if beside is None else [beside])
+    shape = (2, rows, width) if stacked else (rows, width)
+    return pl.pallas_call(
+        functools.partial(product_kernel, section, chips, block, other is not None, section if stacked else None),
+        out_shape=jax.ShapeDtypeStruct(shape, dtype),
+        in_specs=[VMEM] * len(operands),
+        out_specs=VMEM,
+        input_output_aliases={} if beside is None else {len(operands) - 1: 0},
         compiler_params=vmem_limit(8),
         cost_estimate=cost(name),
         name=name,
-    )(queue, count, x, dy, *others, *ready)
+    )(*operands)
 
 
 def sum_kernel(a, b, out):
@@ -244,7 +242,7 @@
             scaled = clip * grad[section, span, :]
             fresh = 0.9 * moment[section, span, :] + 0.1 * scaled
             second = (0.95 / second_fix) * variance[section, span, :] + (0.05 / second_fix) * (scaled * scaled)
-            update = ((0.01 / first_fix) * fresh) / (jnp.sqrt(second) + 1e-08)
+            update = ((0.01 / first_fix) * fresh) / (second * lax.rsqrt(second) + 1e-08)
             moments[section, span, :] = fresh
             masters[section, span, :] = (1.0 - 0.001) * master[section, span, :] - update
             return inner
@@ -296,6 +294,8 @@
         pltpu.with_memory_space_constraint(value, pltpu.HBM) for value in (queue, stash_x, stash_dy)
     )
 
+    held_x = pltpu.with_memory_space_constraint(stash_x, pltpu.VMEM)
+
     def ring(sign):
         return [
             (i, (i // 2 + sign * (1 - 2 * (i % 2))) % chips * 2 + i % 2) for i in range(peers)
@@ -310,36 +310,49 @@
     def against(value):
         return lax.ppermute(value, "dp", ring(-1))
 
-    sent_a, dy, x_send, x_keep = first_product(hbm_queue, micro_count, hbm_x, hbm_dy, chips, ((-2, False), (2, True)))
-    other_a = sibling(sent_a)
-    block = functools.partial(product, queue, micro_count, chips=chips, rows=own_rows)
-    (sent_b,) = block(x_send, dy, (-2, False), sections=(1,), name="far_send_b")
-    other_b = sibling(sent_b)
+    sent_a, plan, dy, x_send, x_keep = first_product(hbm_queue, micro_count, hbm_x, hbm_dy, chips, ((-2, False), (2, True)))
+    far_other = [sibling(sent_a)]
+    block = functools.partial(product, plan, chips=chips, rows=own_rows)
+    sent_b = block(x_send, dy, (-2, False), 1, name="far_send_b")
+    far_other.append(sibling(sent_b))
     others = {}
 
     def send(step, dy):
-        sent = block(stash_x, dy, (step, False), name=f"send_{step % chips}")
-        others[-step] = [sibling(value) for value in sent]
-        return sent[0]
-
-    def keep(step, dy, dtype=jnp.bfloat16):
-        (kept,) = block(stash_x, dy, (step, True), others=others[step], stacked=True, dtype=dtype, name=f"keep_{step % chips}")
+        others[-step] = []
+        for section in range(2):
+            sent = block(held_x, dy, (step, False), section, name=f"send_{step % chips}{'ab'[section]}")
+            others[-step].append(sibling(sent))
+            dy = after(dy, sent)
+        return dy
+
+    def keep(step, x, other, dy, dtype=jnp.bfloat16):
+        kept = None
+        for section in range(2):
+            kept = block(
+                x,
+                dy,
+                (step, True),
+                section,
+                other=other[section],
+                stacked=True,
+                beside=kept,
+                dtype=dtype,
+                name=f"keep_{step % chips}{'ab'[section]}",
+            )
+            dy = after(dy, kept)
         return kept
 
-    (far_a,) = block(x_keep, after(dy, sent_b), (2, True), sections=(0,), others=(other_a,), name="far_keep_a")
-    (far,) = block(
-        x_keep, after(dy, far_a), (2, True), sections=(1,), others=(other_b,), ready=(far_a,), stacked=True, name="far_keep_b"
-    )
+    far = keep(2, x_keep, far_other, after(dy, sent_b))
     came = along(far)
-    dy = after(dy, send(1, after(dy, far)))
-    dy = after(dy, send(-1, dy))
-    near_b = keep(-1, dy)
+    dy = send(-1, after(dy, far))
+    dy = send(1, dy)
+    near_a = keep(1, held_x, others[1], dy)
+    near_b = keep(-1, held_x, others[-1], after(dy, near_a))
     plain = against(near_b)
-    near_a = keep(1, after(dy, near_b))
-    near_a = add(near_a, came)
+    near_a = add(after(near_a, near_b), came)
     summed = along(near_a)
-    dy = after(dy, send(0, after(dy, near_a)))
-    own = keep(0, dy, jnp.float32)
+    dy = send(0, after(dy, near_a))
+    own = keep(0, held_x, others[0], dy, jnp.float32)
     grad, squares = totals(everyone, own, summed, plain)
     squares = lax.all_to_all(squares, ("pipe", "dp"), 0, 0, tiled=True)
     max_norm = 0.05 * math.sqrt(2 * lax.axis_size("pipe") * own_rows * peers * kv_width)

time: 70.9 us -> 69.6 us (0.982)
  Pallas kernels: 21.3 us -> 16.6 us
  waiting for transfers between devices: 18.5 us -> 21.6 us
    pallas_call x9 -> x15, Pallas kernels: 14.1 us -> 9.7 us  [product(): pl.pallas_call(functools.partial(product_kernel, section, chips, block, o...]
    ppermute x1, waiting for transfers between devices: 0.29 us -> 3.43 us  [against(): return lax.ppermute(value, 'dp', ring(-1))]
    ppermute x8, waiting for transfers between devices: 3.12 us -> 2.12 us  [sibling(): return lax.ppermute(value, 'dp', [(i, i ^ 1) for i in range(peers)])]
    ppermute x2, waiting for transfers between devices: 15.1 us -> 16 us  [along(): return lax.ppermute(value, 'dp', ring(1))]
  transfers between devices with their start and end apart: 11 -> 11, of which waited for: 8 -> 7; matrix products, arithmetic and copies ran while one was open for 0% -> 0% of each run, Pallas kernels for 19% -> 14%
where the time goes in v3:
time: 69.6 us; the launch traced here: 69.4 us
  waiting for transfers between devices  21.6 us (31%)
  blocking collectives  18.6 us (27%)
  Pallas kernels  16.6 us (24%)
  starting transfers between devices  11.1 us (16%)
  between operations  1.51 us (2%)
    all_to_all x1, blocking collectives, on_device(): squares = lax.all_to_all(squares, ('pipe', 'dp'), 0, 0, tiled=True)  18.6 us
    ppermute x2, waiting for transfers between devices, along(): return lax.ppermute(value, 'dp', ring(1))  16 us
    pallas_call x15, Pallas kernels, product(): pl.pallas_call(functools.partial(product_kernel, section, chips, block, o...  9.7 us
    ppermute x2, starting transfers between devices, along(): return lax.ppermute(value, 'dp', ring(1))  7.4 us
    ppermute x8, starting transfers between devices, sibling(): return lax.ppermute(value, 'dp', [(i, i ^ 1) for i in range(peers)])  3.58 us
    ppermute x1, waiting for transfers between devices, against(): return lax.ppermute(value, 'dp', ring(-1))  3.43 us
    pallas_call x1, Pallas kernels, adam(): pl.pallas_call(functools.partial(update_kernel, max_norm), out_shape=(sta...  3.03 us
    pallas_call x1, Pallas kernels, first_product(): pl.pallas_call(functools.partial(first_kernel, chips, blocks), out_shape=...  2.77 us
  transfers between devices with their start and end apart: 11, of which 7 were waited for; matrix products, arithmetic and copies ran while one was open for 0% of the time, Pallas kernels for 14%

profile of v3, /device:TPU:1, one launch (start us, length us, event | category | flops | bytes accessed | tf_op | source)
XLA Modules:
  0.0 69.4 jit_solution(14218731038213288808)
XLA Ops:
  1.3 2.8 %first_product.1 = (bf16[512,512]{1,0:T(8,128)(2,1)S(1)}, s32[12,128]{1,0:T(8,128)S(1)}, bf16[2,768,512]{2,1,0:T(8,128)(2,1)S(1)}, bf16[12,128,512]{2,1,0:T(8,128)(2,1)S(1)}, bf16[12,128,512]{2,1,0:T(8,128)(2,1)S(1)}) custom-call(s32[1,12]{1,0:T(1,128)} %queue_hbm.1, s32[1]{0:T(128)S(6)} %copy.19.count, bf16[1,1,12,128,4096]{4,3,2,1,0:T(8,128)(2,1)} %refs_1_.23, ...), custom_call_target="tpu_custom_call" | custom-call | flops 1 | bytes 1 | tf_op jit(solution)/shard_map/first_product/pallas_call | solution.py:125
  4.1 1.5 %collective-permute-start = (bf16[512,512]{1,0:T(8,128)(2,1)S(1)}, bf16[512,512]{1,0:T(8,128)(2,1)S(1)}, u32[]{:S(2)}, u32[]{:S(2)}) collective-permute-start(bf16[512,512]{1,0:T(8,128)(2,1)S(1)} %get-tuple-element.33), channel_id=1, source_target_pairs={{0,1},{1,0},{2,3},{3,2},{4,5},{5,4},{6,7},{7,6},{8,9},{9,8},{10,11... | collective-permute-start | bytes 1572872 | tf_op jit(solution)/shard_map/ppermute | solution.py:305
  5.6 0.6 far_send_b.1
  6.3 0.8 %collective-permute-done.refs_3_ = bf16[512,512]{1,0:T(8,128)(2,1)S(1)} collective-permute-done((bf16[512,512]{1,0:T(8,128)(2,1)S(1)}, bf16[512,512]{1,0:T(8,128)(2,1)S(1)}, u32[]{:S(2)}, u32[]{:S(2)}) %collective-permute-start) | collective-permute-done | bytes 524320 | tf_op jit(solution)/shard_map/ppermute | solution.py:305
  7.1 0.6 keep_2a.1.refs_4_
  7.8 0.4 collective-permute-done.1.refs_3_
  8.2 0.6 keep_2b.1
  8.9 3.9 %collective-permute-start.6 = (bf16[2,512,512]{2,1,0:T(8,128)(2,1)S(1)}, bf16[2,512,512]{2,1,0:T(8,128)(2,1)S(1)}, u32[]{:S(2)}, u32[]{:S(2)}) collective-permute-start(bf16[2,512,512]{2,1,0:T(8,128)(2,1)S(1)} %keep_2b.1), channel_id=1, source_target_pairs={{0,2},{1,7},{2,4},{3,1},{4,6},{5,3},{6,0},{7,5},{8,10},{9,15},{10,... | collective-permute-start | bytes 3145736 | tf_op jit(solution)/shard_map/ppermute | solution.py:308
  12.8 0.6 send_3a.1
  13.5 0.6 send_3b.1
  14.2 0.6 collective-permute-start.3
  14.8 0.6 send_1a.1
  15.5 0.7 send_1b.1
  16.2 0.6 collective-permute-start.5
  16.7 0.7 keep_1a.1.refs_4_
  17.4 0.6 keep_1b.1.a
  18.1 0.6 keep_3a.1.refs_4_
  18.7 0.7 keep_3b.1
  19.5 8.3 %collective-permute-done.6.b = bf16[2,512,512]{2,1,0:T(8,128)(2,1)S(1)} collective-permute-done((bf16[2,512,512]{2,1,0:T(8,128)(2,1)S(1)}, bf16[2,512,512]{2,1,0:T(8,128)(2,1)S(1)}, u32[]{:S(2)}, u32[]{:S(2)}) %collective-permute-start.6) | collective-permute-done | bytes 1048608 | tf_op jit(solution)/shard_map/ppermute | solution.py:308
  27.8 0.4 ring_add.1
  28.1 3.5 %collective-permute-start.9 = (bf16[2,512,512]{2,1,0:T(8,128)(2,1)S(1)}, bf16[2,512,512]{2,1,0:T(8,128)(2,1)S(1)}, u32[]{:S(2)}, u32[]{:S(2)}) collective-permute-start(bf16[2,512,512]{2,1,0:T(8,128)(2,1)S(1)} %ring_add.1), channel_id=1, source_target_pairs={{0,2},{1,7},{2,4},{3,1},{4,6},{5,3},{6,0},{7,5},{8,10},{9,15},{10,... | collective-permute-start | bytes 3145736 | tf_op jit(solution)/shard_map/ppermute | solution.py:308
  31.6 0.6 send_0a.1
  32.4 0.6 send_0b.1
  33.0 0.6 collective-permute-start.8
  33.6 0.7 collective-permute-done.7.refs_3_
  34.3 0.7 keep_0a.1.refs_4_
  35.1 0.6 keep_0b.1.own
  35.8 3.4 %collective-permute-done.10.plain = bf16[2,512,512]{2,1,0:T(8,128)(2,1)S(1)} collective-permute-done((bf16[2,512,512]{2,1,0:T(8,128)(2,1)S(1)}, bf16[2,512,512]{2,1,0:T(8,128)(2,1)S(1)}, u32[]{:S(2)}, u32[]{:S(2)}) %collective-permute-start.10) | collective-permute-done | bytes 1048608 | tf_op jit(solution)/shard_map/ppermute | solution.py:311
  39.3 7.7 %collective-permute-done.9.summed = bf16[2,512,512]{2,1,0:T(8,128)(2,1)S(1)} collective-permute-done((bf16[2,512,512]{2,1,0:T(8,128)(2,1)S(1)}, bf16[2,512,512]{2,1,0:T(8,128)(2,1)S(1)}, u32[]{:S(2)}, u32[]{:S(2)}) %collective-permute-start.9) | collective-permute-done | bytes 1048608 | tf_op jit(solution)/shard_map/ppermute | solution.py:308
  47.0 0.7 %totals.1 = (f32[2,512,512]{2,1,0:T(8,128)S(1)}, f32[128,128]{1,0:T(8,128)S(1)}) custom-call(f32[2,512,512]{2,1,0:T(8,128)S(1)} %keep_0b.1.own, bf16[2,512,512]{2,1,0:T(8,128)(2,1)S(1)} %collective-permute-done.9.summed, bf16[2,512,512]{2,1,0:T(8,128)(2,1)S(1)} %collective-permute-done.10.plain), custom_call_target="tpu_custom_call" | custom-call | flops 1 | bytes 1 | tf_op jit(solution)/shard_map/totals/pallas_call | solution.py:208
  47.8 18.6 %all_to_all.11 = f32[128,1,128]{2,1,0:T(1,128)S(1)} all-to-all(f32[128,1,128]{2,1,0:T(1,128)S(1)} %bitcast.16), channel_id=1, replica_groups=mesh['pipe'=16,'dp'=8] {'pipe','dp'}, dimensions={0} | all-to-all | bytes 131072 | tf_op jit(solution)/shard_map/all_to_all | solution.py:357
  66.4 3.0 %adam.1 = (f32[2,512,512]{2,1,0:T(8,128)}, f32[2,512,512]{2,1,0:T(8,128)}, f32[1,1]{1,0:T(1,128)}) custom-call(f32[128,128]{1,0:T(8,128)S(1)} %bitcast.15, f32[2,512,512]{2,1,0:T(8,128)S(1)} %get-tuple-element.49.grad, f32[2,512,512]{2,1,0:T(8,128)S(1)} %bitcast.12, f32[2,512,512]{2,1,0:T(8,128)S(1)} %bitcast.13, f32[2,512,512]{2,1,0:T(8,128)S(1)} %bitcast.14), custom_call_target="tpu_custom_call" | custom-call | flops 1 | bytes 1 | tf_op jit(solution)/shard_map/adam/pallas_call | solution.py:268
  (23 shorter events, 0.7 us)
Async XLA Ops:
  1.3 11.5 %slice-start = ((s8[12582912]{0:T(1024)(128)(4,1)}), s8[4194304]{0:T(1024)(128)(4,1)S(1)}, s32[]{:S(2)}) async-start(s8[12582912]{0:T(1024)(128)(4,1)} %bitcast.10), calls=%async_computation.1 | async-start | bytes 8388608
  1.3 11.5 %slice-start.1 = ((s8[12582912]{0:T(1024)(128)(4,1)}), s8[4194304]{0:T(1024)(128)(4,1)S(1)}, s32[]{:S(2)}) async-start(s8[12582912]{0:T(1024)(128)(4,1)} %bitcast.10), calls=%async_computation.2 | async-start | bytes 8388608
  4.1 3.0 %collective-permute-start = (bf16[512,512]{1,0:T(8,128)(2,1)S(1)}, bf16[512,512]{1,0:T(8,128)(2,1)S(1)}, u32[]{:S(2)}, u32[]{:S(2)}) collective-permute-start(bf16[512,512]{1,0:T(8,128)(2,1)S(1)} %get-tuple-element.33), channel_id=1, source_target_pairs={{0,1},{1,0},{2,3},{3,2},{4,5},{5,4},{6,7},{7,6},{8,9},{9,8},{10,11... | collective-permute-start | bytes 1572872 | tf_op jit(solution)/shard_map/ppermute | solution.py:305
  6.2 2.0 %collective-permute-start.1 = (bf16[512,512]{1,0:T(8,128)(2,1)S(1)}, bf16[512,512]{1,0:T(8,128)(2,1)S(1)}, u32[]{:S(2)}, u32[]{:S(2)}) collective-permute-start(bf16[512,512]{1,0:T(8,128)(2,1)S(1)} %far_send_b.1), channel_id=1, source_target_pairs={{0,1},{1,0},{2,3},{3,2},{4,5},{5,4},{6,7},{7,6},{8,9},{9,8},{10,11... | collective-permute-start | bytes 1572872 | tf_op jit(solution)/shard_map/ppermute | solution.py:305
  7.1 5.7 %slice-start.2 = ((s8[12582912]{0:T(1024)(128)(4,1)}), s8[4194304]{0:T(1024)(128)(4,1)S(1)}, s32[]{:S(2)}) async-start(s8[12582912]{0:T(1024)(128)(4,1)} %bitcast.10), calls=%async_computation.3 | async-start | bytes 8388608
  8.9 18.9 %collective-permute-start.6 = (bf16[2,512,512]{2,1,0:T(8,128)(2,1)S(1)}, bf16[2,512,512]{2,1,0:T(8,128)(2,1)S(1)}, u32[]{:S(2)}, u32[]{:S(2)}) collective-permute-start(bf16[2,512,512]{2,1,0:T(8,128)(2,1)S(1)} %keep_2b.1), channel_id=1, source_target_pairs={{0,2},{1,7},{2,4},{3,1},{4,6},{5,3},{6,0},{7,5},{8,10},{9,15},{10,... | collective-permute-start | bytes 3145736 | tf_op jit(solution)/shard_map/ppermute | solution.py:308
  13.4 3.3 %collective-permute-start.2 = (bf16[512,512]{1,0:T(8,128)(2,1)S(1)}, bf16[512,512]{1,0:T(8,128)(2,1)S(1)}, u32[]{:S(2)}, u32[]{:S(2)}) collective-permute-start(bf16[512,512]{1,0:T(8,128)(2,1)S(1)} %send_3a.1), channel_id=1, source_target_pairs={{0,1},{1,0},{2,3},{3,2},{4,5},{5,4},{6,7},{7,6},{8,9},{9,8},{10,11... | collective-permute-start | bytes 1572872 | tf_op jit(solution)/shard_map/ppermute | solution.py:305
  14.2 3.2 %collective-permute-start.3 = (bf16[512,512]{1,0:T(8,128)(2,1)S(1)}, bf16[512,512]{1,0:T(8,128)(2,1)S(1)}, u32[]{:S(2)}, u32[]{:S(2)}) collective-permute-start(bf16[512,512]{1,0:T(8,128)(2,1)S(1)} %send_3b.1), channel_id=1, source_target_pairs={{0,1},{1,0},{2,3},{3,2},{4,5},{5,4},{6,7},{7,6},{8,9},{9,8},{10,11... | collective-permute-start | bytes 1572872 | tf_op jit(solution)/shard_map/ppermute | solution.py:305
  15.4 2.6 %collective-permute-start.4 = (bf16[512,512]{1,0:T(8,128)(2,1)S(1)}, bf16[512,512]{1,0:T(8,128)(2,1)S(1)}, u32[]{:S(2)}, u32[]{:S(2)}) collective-permute-start(bf16[512,512]{1,0:T(8,128)(2,1)S(1)} %send_1a.1), channel_id=1, source_target_pairs={{0,1},{1,0},{2,3},{3,2},{4,5},{5,4},{6,7},{7,6},{8,9},{9,8},{10,11... | collective-permute-start | bytes 1572872 | tf_op jit(solution)/shard_map/ppermute | solution.py:305
  16.2 2.6 %collective-permute-start.5 = (bf16[512,512]{1,0:T(8,128)(2,1)S(1)}, bf16[512,512]{1,0:T(8,128)(2,1)S(1)}, u32[]{:S(2)}, u32[]{:S(2)}) collective-permute-start(bf16[512,512]{1,0:T(8,128)(2,1)S(1)} %send_1b.1), channel_id=1, source_target_pairs={{0,1},{1,0},{2,3},{3,2},{4,5},{5,4},{6,7},{7,6},{8,9},{9,8},{10,11... | collective-permute-start | bytes 1572872 | tf_op jit(solution)/shard_map/ppermute | solution.py:305
  19.4 19.9 %collective-permute-start.10 = (bf16[2,512,512]{2,1,0:T(8,128)(2,1)S(1)}, bf16[2,512,512]{2,1,0:T(8,128)(2,1)S(1)}, u32[]{:S(2)}, u32[]{:S(2)}) collective-permute-start(bf16[2,512,512]{2,1,0:T(8,128)(2,1)S(1)} %keep_3b.1), channel_id=1, source_target_pairs={{0,6},{1,3},{2,0},{3,5},{4,2},{5,7},{6,4},{7,1},{8,14},{9,11},{10,... | collective-permute-start | bytes 3145736 | tf_op jit(solution)/shard_map/ppermute | solution.py:311
  28.1 18.8 %collective-permute-start.9 = (bf16[2,512,512]{2,1,0:T(8,128)(2,1)S(1)}, bf16[2,512,512]{2,1,0:T(8,128)(2,1)S(1)}, u32[]{:S(2)}, u32[]{:S(2)}) collective-permute-start(bf16[2,512,512]{2,1,0:T(8,128)(2,1)S(1)} %ring_add.1), channel_id=1, source_target_pairs={{0,2},{1,7},{2,4},{3,1},{4,6},{5,3},{6,0},{7,5},{8,10},{9,15},{10,... | collective-permute-start | bytes 3145736 | tf_op jit(solution)/shard_map/ppermute | solution.py:308
  32.3 2.0 %collective-permute-start.7 = (bf16[512,512]{1,0:T(8,128)(2,1)S(1)}, bf16[512,512]{1,0:T(8,128)(2,1)S(1)}, u32[]{:S(2)}, u32[]{:S(2)}) collective-permute-start(bf16[512,512]{1,0:T(8,128)(2,1)S(1)} %send_0a.1), channel_id=1, source_target_pairs={{0,1},{1,0},{2,3},{3,2},{4,5},{5,4},{6,7},{7,6},{8,9},{9,8},{10,11... | collective-permute-start | bytes 1572872 | tf_op jit(solution)/shard_map/ppermute | solution.py:305
  33.0 2.1 %collective-permute-start.8 = (bf16[512,512]{1,0:T(8,128)(2,1)S(1)}, bf16[512,512]{1,0:T(8,128)(2,1)S(1)}, u32[]{:S(2)}, u32[]{:S(2)}) collective-permute-start(bf16[512,512]{1,0:T(8,128)(2,1)S(1)} %send_0b.1), channel_id=1, source_target_pairs={{0,1},{1,0},{2,3},{3,2},{4,5},{5,4},{6,7},{7,6},{8,9},{9,8},{10,11... | collective-permute-start | bytes 1572872 | tf_op jit(solution)/shard_map/ppermute | solution.py:305
  35.1 31.3 %copy-start.2 = (f32[1,2,512,512]{3,2,1,0:T(8,128)S(1)}, f32[1,2,512,512]{3,2,1,0:T(8,128)}, u32[]{:S(2)}) copy-start(f32[1,2,512,512]{3,2,1,0:T(8,128)} %param.13) | copy-start | bytes 6291460
  35.8 30.6 %copy-start = (f32[1,2,512,512]{3,2,1,0:T(8,128)S(1)}, f32[1,2,512,512]{3,2,1,0:T(8,128)}, u32[]{:S(2)}) copy-start(f32[1,2,512,512]{3,2,1,0:T(8,128)} %param.11) | copy-start | bytes 6291460
  35.8 30.6 %copy-start.1 = (f32[1,2,512,512]{3,2,1,0:T(8,128)S(1)}, f32[1,2,512,512]{3,2,1,0:T(8,128)}, u32[]{:S(2)}) copy-start(f32[1,2,512,512]{3,2,1,0:T(8,128)} %param.12) | copy-start | bytes 6291460

commit v4 on v3

--- a/solution.py
+++ b/solution.py
@@ -125,11 +125,11 @@
     return pl.pallas_call(
         functools.partial(first_kernel, chips, blocks),
         out_shape=(
-            jax.ShapeDtypeStruct((rows, width), jnp.bfloat16),
-            jax.ShapeDtypeStruct((slots, 128), jnp.int32),
-            jax.ShapeDtypeStruct((2, slots // 2 * tokens, width), dy.dtype),
+            pltpu.VMEM((rows, width), jnp.bfloat16),
+            pltpu.VMEM((slots, 128), jnp.int32),
+            pltpu.VMEM((2, slots // 2 * tokens, width), dy.dtype),
         )
-        + (jax.ShapeDtypeStruct((slots, tokens, rows), x.dtype),) * len(blocks),
+        + (pltpu.VMEM((slots, tokens, rows), x.dtype),) * len(blocks),
         in_specs=[HBM, SMEM, HBM, HBM],
         out_specs=(VMEM,) * (3 + len(blocks)),
         scratch_shapes=[
@@ -138,7 +138,7 @@
             pltpu.SMEM((slots,), jnp.int32),
             pltpu.SemaphoreType.DMA((2 + len(blocks),)),
         ],
-        compiler_params=vmem_limit(12),
+        compiler_params=vmem_limit(54),
         cost_estimate=cost("first_product"),
         name="first_product",
     )(queue, count, x, dy)
@@ -188,7 +188,7 @@
 
 
 def total_kernel(own, summed, plain, grad, squares):
-    slab = 16
+    slab = 32
     _, rows, width = own.shape
 
     def step(i, kept):
@@ -344,15 +344,15 @@
 
     far = keep(2, x_keep, far_other, after(dy, sent_b))
     came = along(far)
-    dy = send(-1, after(dy, far))
+    dy = send(0, after(dy, far))
+    dy = send(-1, dy)
     dy = send(1, dy)
     near_a = keep(1, held_x, others[1], dy)
     near_b = keep(-1, held_x, others[-1], after(dy, near_a))
     plain = against(near_b)
     near_a = add(after(near_a, near_b), came)
     summed = along(near_a)
-    dy = send(0, after(dy, near_a))
-    own = keep(0, held_x, others[0], dy, jnp.float32)
+    own = keep(0, held_x, others[0], after(dy, near_a), jnp.float32)
     grad, squares = totals(everyone, own, summed, plain)
     squares = lax.all_to_all(squares, ("pipe", "dp"), 0, 0, tiled=True)
     max_norm = 0.05 * math.sqrt(2 * lax.axis_size("pipe") * own_rows * peers * kv_width)

time: 69.6 us -> 69.3 us (level)
    ppermute x2, waiting for transfers between devices: 16 us -> 10.8 us  [along(): return lax.ppermute(value, 'dp', ring(1))]
    ppermute x1, waiting for transfers between devices: 3.43 us -> 8.25 us  [against(): return lax.ppermute(value, 'dp', ring(-1))]
where the time goes in v4:
time: 69.3 us; the launch traced here: 69.1 us
  waiting for transfers between devices  21.8 us (31%)
  blocking collectives  18.6 us (27%)
  Pallas kernels  16.3 us (24%)
  starting transfers between devices  10.9 us (16%)
  between operations  1.48 us (2%)
    all_to_all x1, blocking collectives, on_device(): squares = lax.all_to_all(squares, ('pipe', 'dp'), 0, 0, tiled=True)  18.6 us
    ppermute x2, waiting for transfers between devices, along(): return lax.ppermute(value, 'dp', ring(1))  10.8 us
    pallas_call x15, Pallas kernels, product(): pl.pallas_call(functools.partial(product_kernel, section, chips, block, o...  9.69 us
    ppermute x1, waiting for transfers between devices, against(): return lax.ppermute(value, 'dp', ring(-1))  8.25 us
    ppermute x2, starting transfers between devices, along(): return lax.ppermute(value, 'dp', ring(1))  7.4 us
    ppermute x8, starting transfers between devices, sibling(): return lax.ppermute(value, 'dp', [(i, i ^ 1) for i in range(peers)])  3.44 us
    pallas_call x1, Pallas kernels, adam(): pl.pallas_call(functools.partial(update_kernel, max_norm), out_shape=(sta...  3.03 us
    ppermute x8, waiting for transfers between devices, sibling(): return lax.ppermute(value, 'dp', [(i, i ^ 1) for i in range(peers)])  2.75 us
  transfers between devices with their start and end apart: 11, of which 7 were waited for; matrix products, arithmetic and copies ran while one was open for 0% of the time, Pallas kernels for 14%

profile of v4, /device:TPU:1, one launch (start us, length us, event | category | flops | bytes accessed | tf_op | source)
XLA Modules:
  0.0 69.1 jit_solution(18218340725649402316)
XLA Ops:
  1.3 2.6 %first_product.1 = (bf16[512,512]{1,0:T(8,128)(2,1)S(1)}, s32[12,128]{1,0:T(8,128)S(1)}, bf16[2,768,512]{2,1,0:T(8,128)(2,1)S(1)}, bf16[12,128,512]{2,1,0:T(8,128)(2,1)S(1)}, bf16[12,128,512]{2,1,0:T(8,128)(2,1)S(1)}) custom-call(s32[1,12]{1,0:T(1,128)} %queue_hbm.1, s32[1]{0:T(128)S(6)} %copy.19.count, bf16[1,1,12,128,4096]{4,3,2,1,0:T(8,128)(2,1)} %refs_1_.23, ...), custom_call_target="tpu_custom_call" | custom-call | flops 1 | bytes 1 | tf_op jit(solution)/shard_map/first_product/pallas_call | solution.py:125
  3.9 1.5 %collective-permute-start = (bf16[512,512]{1,0:T(8,128)(2,1)S(1)}, bf16[512,512]{1,0:T(8,128)(2,1)S(1)}, u32[]{:S(2)}, u32[]{:S(2)}) collective-permute-start(bf16[512,512]{1,0:T(8,128)(2,1)S(1)} %get-tuple-element.33), channel_id=1, source_target_pairs={{0,1},{1,0},{2,3},{3,2},{4,5},{5,4},{6,7},{7,6},{8,9},{9,8},{10,11... | collective-permute-start | bytes 1572872 | tf_op jit(solution)/shard_map/ppermute | solution.py:305
  5.4 0.6 far_send_b.1
  6.2 0.8 %collective-permute-done.refs_3_ = bf16[512,512]{1,0:T(8,128)(2,1)S(1)} collective-permute-done((bf16[512,512]{1,0:T(8,128)(2,1)S(1)}, bf16[512,512]{1,0:T(8,128)(2,1)S(1)}, u32[]{:S(2)}, u32[]{:S(2)}) %collective-permute-start) | collective-permute-done | bytes 524320 | tf_op jit(solution)/shard_map/ppermute | solution.py:305
  6.9 0.6 keep_2a.1.refs_4_
  7.6 0.5 collective-permute-done.1.refs_3_
  8.0 0.6 keep_2b.1
  8.7 3.9 %collective-permute-start.6 = (bf16[2,512,512]{2,1,0:T(8,128)(2,1)S(1)}, bf16[2,512,512]{2,1,0:T(8,128)(2,1)S(1)}, u32[]{:S(2)}, u32[]{:S(2)}) collective-permute-start(bf16[2,512,512]{2,1,0:T(8,128)(2,1)S(1)} %keep_2b.1), channel_id=1, source_target_pairs={{0,2},{1,7},{2,4},{3,1},{4,6},{5,3},{6,0},{7,5},{8,10},{9,15},{10,... | collective-permute-start | bytes 3145736 | tf_op jit(solution)/shard_map/ppermute | solution.py:308
  12.6 0.7 send_0a.1
  13.3 0.7 send_0b.1
  13.9 0.6 send_3a.1
  14.7 0.7 send_3b.1
  15.3 0.6 collective-permute-start.3
  15.9 0.6 send_1a.1
  16.7 0.6 send_1b.1
  17.3 0.6 collective-permute-start.5
  17.9 0.6 keep_1a.1.refs_4_
  18.5 0.6 keep_1b.1.a
  19.2 0.6 keep_3a.1.refs_4_
  19.9 0.7 keep_3b.1
  20.6 5.2 %collective-permute-done.6.b = bf16[2,512,512]{2,1,0:T(8,128)(2,1)S(1)} collective-permute-done((bf16[2,512,512]{2,1,0:T(8,128)(2,1)S(1)}, bf16[2,512,512]{2,1,0:T(8,128)(2,1)S(1)}, u32[]{:S(2)}, u32[]{:S(2)}) %collective-permute-start.6) | collective-permute-done | bytes 1048608 | tf_op jit(solution)/shard_map/ppermute | solution.py:308
  25.8 0.4 ring_add.1
  26.2 3.5 %collective-permute-start.9 = (bf16[2,512,512]{2,1,0:T(8,128)(2,1)S(1)}, bf16[2,512,512]{2,1,0:T(8,128)(2,1)S(1)}, u32[]{:S(2)}, u32[]{:S(2)}) collective-permute-start(bf16[2,512,512]{2,1,0:T(8,128)(2,1)S(1)} %ring_add.1), channel_id=1, source_target_pairs={{0,2},{1,7},{2,4},{3,1},{4,6},{5,3},{6,0},{7,5},{8,10},{9,15},{10,... | collective-permute-start | bytes 3145736 | tf_op jit(solution)/shard_map/ppermute | solution.py:308
  29.7 0.5 collective-permute-start.8
  30.2 1.4 %collective-permute-done.7.refs_3_ = bf16[512,512]{1,0:T(8,128)(2,1)S(1)} collective-permute-done((bf16[512,512]{1,0:T(8,128)(2,1)S(1)}, bf16[512,512]{1,0:T(8,128)(2,1)S(1)}, u32[]{:S(2)}, u32[]{:S(2)}) %collective-permute-start.7) | collective-permute-done | bytes 524320 | tf_op jit(solution)/shard_map/ppermute | solution.py:305
  31.6 0.6 keep_0a.1.refs_4_
  32.3 0.6 keep_0b.1.own
  33.0 8.3 %collective-permute-done.10.plain = bf16[2,512,512]{2,1,0:T(8,128)(2,1)S(1)} collective-permute-done((bf16[2,512,512]{2,1,0:T(8,128)(2,1)S(1)}, bf16[2,512,512]{2,1,0:T(8,128)(2,1)S(1)}, u32[]{:S(2)}, u32[]{:S(2)}) %collective-permute-start.10) | collective-permute-done | bytes 1048608 | tf_op jit(solution)/shard_map/ppermute | solution.py:311
  41.3 5.6 %collective-permute-done.9.summed = bf16[2,512,512]{2,1,0:T(8,128)(2,1)S(1)} collective-permute-done((bf16[2,512,512]{2,1,0:T(8,128)(2,1)S(1)}, bf16[2,512,512]{2,1,0:T(8,128)(2,1)S(1)}, u32[]{:S(2)}, u32[]{:S(2)}) %collective-permute-start.9) | collective-permute-done | bytes 1048608 | tf_op jit(solution)/shard_map/ppermute | solution.py:308
  46.8 0.6 totals.1
  47.5 18.6 %all_to_all.11 = f32[128,1,128]{2,1,0:T(1,128)S(1)} all-to-all(f32[128,1,128]{2,1,0:T(1,128)S(1)} %bitcast.14), channel_id=1, replica_groups=mesh['pipe'=16,'dp'=8] {'pipe','dp'}, dimensions={0} | all-to-all | bytes 131072 | tf_op jit(solution)/shard_map/all_to_all | solution.py:357
  66.1 3.0 %adam.1 = (f32[2,512,512]{2,1,0:T(8,128)}, f32[2,512,512]{2,1,0:T(8,128)}, f32[1,1]{1,0:T(1,128)}) custom-call(f32[128,128]{1,0:T(8,128)S(1)} %bitcast.13, f32[2,512,512]{2,1,0:T(8,128)S(1)} %get-tuple-element.49.grad, f32[2,512,512]{2,1,0:T(8,128)S(1)} %bitcast.10, f32[2,512,512]{2,1,0:T(8,128)S(1)} %bitcast.11, f32[2,512,512]{2,1,0:T(8,128)S(1)} %bitcast.12), custom_call_target="tpu_custom_call" | custom-call | flops 1 | bytes 1 | tf_op jit(solution)/shard_map/adam/pallas_call | solution.py:268
  (18 shorter events, 0.5 us)
Async XLA Ops:
  3.9 3.0 %collective-permute-start = (bf16[512,512]{1,0:T(8,128)(2,1)S(1)}, bf16[512,512]{1,0:T(8,128)(2,1)S(1)}, u32[]{:S(2)}, u32[]{:S(2)}) collective-permute-start(bf16[512,512]{1,0:T(8,128)(2,1)S(1)} %get-tuple-element.33), channel_id=1, source_target_pairs={{0,1},{1,0},{2,3},{3,2},{4,5},{5,4},{6,7},{7,6},{8,9},{9,8},{10,11... | collective-permute-start | bytes 1572872 | tf_op jit(solution)/shard_map/ppermute | solution.py:305
  5.4 7.2 %copy-start = (bf16[1,1,12,128,4096]{4,3,2,1,0:T(8,128)(2,1)S(1)}, bf16[1,1,12,128,4096]{4,3,2,1,0:T(8,128)(2,1)}, u32[]{:S(2)}) copy-start(bf16[1,1,12,128,4096]{4,3,2,1,0:T(8,128)(2,1)} %refs_1_.23) | copy-start | bytes 37748740
  6.1 2.0 %collective-permute-start.1 = (bf16[512,512]{1,0:T(8,128)(2,1)S(1)}, bf16[512,512]{1,0:T(8,128)(2,1)S(1)}, u32[]{:S(2)}, u32[]{:S(2)}) collective-permute-start(bf16[512,512]{1,0:T(8,128)(2,1)S(1)} %far_send_b.1), channel_id=1, source_target_pairs={{0,1},{1,0},{2,3},{3,2},{4,5},{5,4},{6,7},{7,6},{8,9},{9,8},{10,11... | collective-permute-start | bytes 1572872 | tf_op jit(solution)/shard_map/ppermute | solution.py:305
  8.7 17.1 %collective-permute-start.6 = (bf16[2,512,512]{2,1,0:T(8,128)(2,1)S(1)}, bf16[2,512,512]{2,1,0:T(8,128)(2,1)S(1)}, u32[]{:S(2)}, u32[]{:S(2)}) collective-permute-start(bf16[2,512,512]{2,1,0:T(8,128)(2,1)S(1)} %keep_2b.1), channel_id=1, source_target_pairs={{0,2},{1,7},{2,4},{3,1},{4,6},{5,3},{6,0},{7,5},{8,10},{9,15},{10,... | collective-permute-start | bytes 3145736 | tf_op jit(solution)/shard_map/ppermute | solution.py:308
  14.6 3.3 %collective-permute-start.2 = (bf16[512,512]{1,0:T(8,128)(2,1)S(1)}, bf16[512,512]{1,0:T(8,128)(2,1)S(1)}, u32[]{:S(2)}, u32[]{:S(2)}) collective-permute-start(bf16[512,512]{1,0:T(8,128)(2,1)S(1)} %send_3a.1), channel_id=1, source_target_pairs={{0,1},{1,0},{2,3},{3,2},{4,5},{5,4},{6,7},{7,6},{8,9},{9,8},{10,11... | collective-permute-start | bytes 1572872 | tf_op jit(solution)/shard_map/ppermute | solution.py:305
  15.3 3.2 %collective-permute-start.3 = (bf16[512,512]{1,0:T(8,128)(2,1)S(1)}, bf16[512,512]{1,0:T(8,128)(2,1)S(1)}, u32[]{:S(2)}, u32[]{:S(2)}) collective-permute-start(bf16[512,512]{1,0:T(8,128)(2,1)S(1)} %send_3b.1), channel_id=1, source_target_pairs={{0,1},{1,0},{2,3},{3,2},{4,5},{5,4},{6,7},{7,6},{8,9},{9,8},{10,11... | collective-permute-start | bytes 1572872 | tf_op jit(solution)/shard_map/ppermute | solution.py:305
  16.6 2.6 %collective-permute-start.4 = (bf16[512,512]{1,0:T(8,128)(2,1)S(1)}, bf16[512,512]{1,0:T(8,128)(2,1)S(1)}, u32[]{:S(2)}, u32[]{:S(2)}) collective-permute-start(bf16[512,512]{1,0:T(8,128)(2,1)S(1)} %send_1a.1), channel_id=1, source_target_pairs={{0,1},{1,0},{2,3},{3,2},{4,5},{5,4},{6,7},{7,6},{8,9},{9,8},{10,11... | collective-permute-start | bytes 1572872 | tf_op jit(solution)/shard_map/ppermute | solution.py:305
  17.3 2.6 %collective-permute-start.5 = (bf16[512,512]{1,0:T(8,128)(2,1)S(1)}, bf16[512,512]{1,0:T(8,128)(2,1)S(1)}, u32[]{:S(2)}, u32[]{:S(2)}) collective-permute-start(bf16[512,512]{1,0:T(8,128)(2,1)S(1)} %send_1b.1), channel_id=1, source_target_pairs={{0,1},{1,0},{2,3},{3,2},{4,5},{5,4},{6,7},{7,6},{8,9},{9,8},{10,11... | collective-permute-start | bytes 1572872 | tf_op jit(solution)/shard_map/ppermute | solution.py:305
  20.5 20.7 %collective-permute-start.10 = (bf16[2,512,512]{2,1,0:T(8,128)(2,1)S(1)}, bf16[2,512,512]{2,1,0:T(8,128)(2,1)S(1)}, u32[]{:S(2)}, u32[]{:S(2)}) collective-permute-start(bf16[2,512,512]{2,1,0:T(8,128)(2,1)S(1)} %keep_3b.1), channel_id=1, source_target_pairs={{0,6},{1,3},{2,0},{3,5},{4,2},{5,7},{6,4},{7,1},{8,14},{9,11},{10,... | collective-permute-start | bytes 3145736 | tf_op jit(solution)/shard_map/ppermute | solution.py:311
  26.2 20.6 %collective-permute-start.9 = (bf16[2,512,512]{2,1,0:T(8,128)(2,1)S(1)}, bf16[2,512,512]{2,1,0:T(8,128)(2,1)S(1)}, u32[]{:S(2)}, u32[]{:S(2)}) collective-permute-start(bf16[2,512,512]{2,1,0:T(8,128)(2,1)S(1)} %ring_add.1), channel_id=1, source_target_pairs={{0,2},{1,7},{2,4},{3,1},{4,6},{5,3},{6,0},{7,5},{8,10},{9,15},{10,... | collective-permute-start | bytes 3145736 | tf_op jit(solution)/shard_map/ppermute | solution.py:308
  29.7 1.9 %collective-permute-start.7 = (bf16[512,512]{1,0:T(8,128)(2,1)S(1)}, bf16[512,512]{1,0:T(8,128)(2,1)S(1)}, u32[]{:S(2)}, u32[]{:S(2)}) collective-permute-start(bf16[512,512]{1,0:T(8,128)(2,1)S(1)} %send_0a.1), channel_id=1, source_target_pairs={{0,1},{1,0},{2,3},{3,2},{4,5},{5,4},{6,7},{7,6},{8,9},{9,8},{10,11... | collective-permute-start | bytes 1572872 | tf_op jit(solution)/shard_map/ppermute | solution.py:305
  29.7 2.7 %collective-permute-start.8 = (bf16[512,512]{1,0:T(8,128)(2,1)S(1)}, bf16[512,512]{1,0:T(8,128)(2,1)S(1)}, u32[]{:S(2)}, u32[]{:S(2)}) collective-permute-start(bf16[512,512]{1,0:T(8,128)(2,1)S(1)} %send_0b.1), channel_id=1, source_target_pairs={{0,1},{1,0},{2,3},{3,2},{4,5},{5,4},{6,7},{7,6},{8,9},{9,8},{10,11... | collective-permute-start | bytes 1572872 | tf_op jit(solution)/shard_map/ppermute | solution.py:305
  32.3 33.8 %copy-start.3 = (f32[1,2,512,512]{3,2,1,0:T(8,128)S(1)}, f32[1,2,512,512]{3,2,1,0:T(8,128)}, u32[]{:S(2)}) copy-start(f32[1,2,512,512]{3,2,1,0:T(8,128)} %param.13) | copy-start | bytes 6291460
  33.0 33.1 %copy-start.1 = (f32[1,2,512,512]{3,2,1,0:T(8,128)S(1)}, f32[1,2,512,512]{3,2,1,0:T(8,128)}, u32[]{:S(2)}) copy-start(f32[1,2,512,512]{3,2,1,0:T(8,128)} %param.11) | copy-start | bytes 6291460
  33.0 33.1 %copy-start.2 = (f32[1,2,512,512]{3,2,1,0:T(8,128)S(1)}, f32[1,2,512,512]{3,2,1,0:T(8,128)}, u32[]{:S(2)}) copy-start(f32[1,2,512,512]{3,2,1,0:T(8,128)} %param.12) | copy-start | bytes 6291460

commit v5 on v4

--- a/solution.py
+++ b/solution.py
@@ -160,30 +160,36 @@
     )(*operands)
 
 
-def sum_kernel(a, b, out):
+def sum_kernel(section, a, b, out):
     sections, rows, _ = a.shape
     slab = 64
     per = rows // slab
 
     def step(i, carry):
-        section, span = lax.div(i, per), pl.ds(pl.multiple_of(lax.rem(i, per) * slab, slab), slab)
-        out[section, span, :] = (
-            a[section, span, :].astype(jnp.float32) + b[section, span, :].astype(jnp.float32)
-        ).astype(out.dtype)
+        span = pl.ds(pl.multiple_of(lax.rem(i, per) * slab, slab), slab)
+        if section is None:
+            place_in = lax.div(i, per)
+            other = b[place_in, span, :]
+        else:
+            place_in = section
+            other = b[span, :]
+        out[place_in, span, :] = (a[place_in, span, :].astype(jnp.float32) + other.astype(jnp.float32)).astype(out.dtype)
         return carry
 
-    lax.fori_loop(0, sections * per, step, 0)
-
-
-def add(a, b):
-    return pl.pallas_call(
-        sum_kernel,
+    lax.fori_loop(0, per * (sections if section is None else 1), step, 0)
+
+
+def add(a, b, section=None):
+    name = "ring_add" if section is None else f"far_add_{'ab'[section]}"
+    return pl.pallas_call(
+        functools.partial(sum_kernel, section),
         out_shape=jax.ShapeDtypeStruct(a.shape, a.dtype),
         in_specs=[VMEM, VMEM],
         out_specs=VMEM,
+        input_output_aliases={0: 0},
         compiler_params=vmem_limit(4),
         cost_estimate=cost("ring_add"),
-        name="ring_add",
+        name=name,
     )(a, b)
 
 
@@ -224,7 +230,7 @@
     clip = jnp.minimum(jnp.float32(1.0), max_norm / (norm + 1e-06))
     norm_out[0, 0] = norm
     sections, rows, width = grad.shape
-    chunk, slab = 128, 64
+    chunk, slab = 128, 128
     per = rows // chunk
 
     def copies(i):
@@ -342,7 +348,10 @@
             dy = after(dy, kept)
         return kept
 
-    far = keep(2, x_keep, far_other, after(dy, sent_b))
+    far = block(x_keep, after(dy, sent_b), (2, True), 0, stacked=True, name="keep_2a")
+    far = block(x_keep, dy, (2, True), 1, stacked=True, beside=far, name="keep_2b")
+    far = add(far, far_other[0], 0)
+    far = add(far, far_other[1], 1)
     came = along(far)
     dy = send(0, after(dy, far))
     dy = send(-1, dy)

time: 69.3 us -> 69 us (level)
  waiting for transfers between devices: 21.8 us -> 21 us
    ppermute x1, waiting for transfers between devices: 8.25 us -> 10.4 us  [against(): return lax.ppermute(value, 'dp', ring(-1))]
    ppermute x2, waiting for transfers between devices: 10.8 us -> 8.68 us  [along(): return lax.ppermute(value, 'dp', ring(1))]
    ppermute x8, waiting for transfers between devices: 2.75 us -> 1.88 us  [sibling(): return lax.ppermute(value, 'dp', [(i, i ^ 1) for i in range(peers)])]
  transfers between devices with their start and end apart: 11 -> 11, of which waited for: 7 -> 6; matrix products, arithmetic and copies ran while one was open for 0% -> 0% of each run, Pallas kernels for 14% -> 15%
where the time goes in v5:
time: 69 us; the launch traced here: 68.8 us
  waiting for transfers between devices  21 us (30%)
  blocking collectives  18.6 us (27%)
  Pallas kernels  16.8 us (24%)
  starting transfers between devices  10.9 us (16%)
  between operations  1.51 us (2%)
    all_to_all x1, blocking collectives, on_device(): squares = lax.all_to_all(squares, ('pipe', 'dp'), 0, 0, tiled=True)  18.6 us
    ppermute x1, waiting for transfers between devices, against(): return lax.ppermute(value, 'dp', ring(-1))  10.4 us
    pallas_call x15, Pallas kernels, product(): pl.pallas_call(functools.partial(product_kernel, section, chips, block, o...  9.68 us
    ppermute x2, waiting for transfers between devices, along(): return lax.ppermute(value, 'dp', ring(1))  8.68 us
    ppermute x2, starting transfers between devices, along(): return lax.ppermute(value, 'dp', ring(1))  7.09 us
    ppermute x8, starting transfers between devices, sibling(): return lax.ppermute(value, 'dp', [(i, i ^ 1) for i in range(peers)])  3.42 us
    pallas_call x1, Pallas kernels, adam(): pl.pallas_call(functools.partial(update_kernel, max_norm), out_shape=(sta...  3.02 us
    pallas_call x1, Pallas kernels, first_product(): pl.pallas_call(functools.partial(first_kernel, chips, blocks), out_shape=...  2.62 us
  transfers between devices with their start and end apart: 11, of which 6 were waited for; matrix products, arithmetic and copies ran while one was open for 0% of the time, Pallas kernels for 15%

profile of v5, /device:TPU:1, one launch (start us, length us, event | category | flops | bytes accessed | tf_op | source)
XLA Modules:
  0.0 68.8 jit_solution(11321274878371365097)
XLA Ops:
  1.3 2.6 %first_product.1 = (bf16[512,512]{1,0:T(8,128)(2,1)S(1)}, s32[12,128]{1,0:T(8,128)S(1)}, bf16[2,768,512]{2,1,0:T(8,128)(2,1)S(1)}, bf16[12,128,512]{2,1,0:T(8,128)(2,1)S(1)}, bf16[12,128,512]{2,1,0:T(8,128)(2,1)S(1)}) custom-call(s32[1,12]{1,0:T(1,128)} %queue_hbm.1, s32[1]{0:T(128)S(6)} %copy.25.count, bf16[1,1,12,128,4096]{4,3,2,1,0:T(8,128)(2,1)} %refs_1_.23, ...), custom_call_target="tpu_custom_call" | custom-call | flops 1 | bytes 1 | tf_op jit(solution)/shard_map/first_product/pallas_call | solution.py:125
  3.9 1.5 %collective-permute-start = (bf16[512,512]{1,0:T(8,128)(2,1)S(1)}, bf16[512,512]{1,0:T(8,128)(2,1)S(1)}, u32[]{:S(2)}, u32[]{:S(2)}) collective-permute-start(bf16[512,512]{1,0:T(8,128)(2,1)S(1)} %get-tuple-element.32), channel_id=1, source_target_pairs={{0,1},{1,0},{2,3},{3,2},{4,5},{5,4},{6,7},{7,6},{8,9},{9,8},{10,11... | collective-permute-start | bytes 1572872 | tf_op jit(solution)/shard_map/ppermute | solution.py:311
  5.4 0.6 far_send_b.1
  6.2 0.6 keep_2a.1.refs_3_
  6.8 0.6 keep_2b.1.a
  7.7 0.4 collective-permute-done.1.b
  8.2 3.9 %collective-permute-start.6 = (bf16[2,512,512]{2,1,0:T(8,128)(2,1)S(1)}, bf16[2,512,512]{2,1,0:T(8,128)(2,1)S(1)}, u32[]{:S(2)}, u32[]{:S(2)}) collective-permute-start(bf16[2,512,512]{2,1,0:T(8,128)(2,1)S(1)} %far_add_b.1), channel_id=1, source_target_pairs={{0,2},{1,7},{2,4},{3,1},{4,6},{5,3},{6,0},{7,5},{8,10},{9,15},{10,... | collective-permute-start | bytes 3145736 | tf_op jit(solution)/shard_map/ppermute | solution.py:314
  12.2 0.6 send_0a.1
  12.8 0.6 send_0b.1
  13.5 0.6 send_3a.1
  14.2 0.6 send_3b.1
  14.9 0.6 collective-permute-start.3
  15.4 0.6 send_1a.1
  16.2 0.6 send_1b.1
  16.8 0.6 collective-permute-start.5
  17.4 0.6 keep_1a.1.refs_4_
  18.1 0.6 keep_1b.1.a
  18.7 0.7 keep_3a.1.refs_4_
  19.4 0.7 keep_3b.1
  20.1 0.4 collective-permute-start.10
  20.5 3.4 %collective-permute-done.6.b = bf16[2,512,512]{2,1,0:T(8,128)(2,1)S(1)} collective-permute-done((bf16[2,512,512]{2,1,0:T(8,128)(2,1)S(1)}, bf16[2,512,512]{2,1,0:T(8,128)(2,1)S(1)}, u32[]{:S(2)}, u32[]{:S(2)}) %collective-permute-start.6) | collective-permute-done | bytes 1048608 | tf_op jit(solution)/shard_map/ppermute | solution.py:314
  23.9 0.4 ring_add.1
  24.3 3.2 %collective-permute-start.9 = (bf16[2,512,512]{2,1,0:T(8,128)(2,1)S(1)}, bf16[2,512,512]{2,1,0:T(8,128)(2,1)S(1)}, u32[]{:S(2)}, u32[]{:S(2)}) collective-permute-start(bf16[2,512,512]{2,1,0:T(8,128)(2,1)S(1)} %ring_add.1), channel_id=1, source_target_pairs={{0,2},{1,7},{2,4},{3,1},{4,6},{5,3},{6,0},{7,5},{8,10},{9,15},{10,... | collective-permute-start | bytes 3145736 | tf_op jit(solution)/shard_map/ppermute | solution.py:314
  27.5 0.5 collective-permute-start.8
  28.0 1.4 %collective-permute-done.7.refs_3_ = bf16[512,512]{1,0:T(8,128)(2,1)S(1)} collective-permute-done((bf16[512,512]{1,0:T(8,128)(2,1)S(1)}, bf16[512,512]{1,0:T(8,128)(2,1)S(1)}, u32[]{:S(2)}, u32[]{:S(2)}) %collective-permute-start.7) | collective-permute-done | bytes 524320 | tf_op jit(solution)/shard_map/ppermute | solution.py:311
  29.4 0.6 keep_0a.1.refs_4_
  30.2 0.6 keep_0b.1.own
  30.8 10.4 %collective-permute-done.10.plain = bf16[2,512,512]{2,1,0:T(8,128)(2,1)S(1)} collective-permute-done((bf16[2,512,512]{2,1,0:T(8,128)(2,1)S(1)}, bf16[2,512,512]{2,1,0:T(8,128)(2,1)S(1)}, u32[]{:S(2)}, u32[]{:S(2)}) %collective-permute-start.10) | collective-permute-done | bytes 1048608 | tf_op jit(solution)/shard_map/ppermute | solution.py:317
  41.3 5.2 %collective-permute-done.9.summed = bf16[2,512,512]{2,1,0:T(8,128)(2,1)S(1)} collective-permute-done((bf16[2,512,512]{2,1,0:T(8,128)(2,1)S(1)}, bf16[2,512,512]{2,1,0:T(8,128)(2,1)S(1)}, u32[]{:S(2)}, u32[]{:S(2)}) %collective-permute-start.9) | collective-permute-done | bytes 1048608 | tf_op jit(solution)/shard_map/ppermute | solution.py:314
  46.5 0.7 totals.1
  47.2 18.6 %all_to_all.11 = f32[128,1,128]{2,1,0:T(1,128)S(1)} all-to-all(f32[128,1,128]{2,1,0:T(1,128)S(1)} %bitcast.14), channel_id=1, replica_groups=mesh['pipe'=16,'dp'=8] {'pipe','dp'}, dimensions={0} | all-to-all | bytes 131072 | tf_op jit(solution)/shard_map/all_to_all | solution.py:366
  65.8 3.0 %adam.1 = (f32[2,512,512]{2,1,0:T(8,128)}, f32[2,512,512]{2,1,0:T(8,128)}, f32[1,1]{1,0:T(1,128)}) custom-call(f32[128,128]{1,0:T(8,128)S(1)} %bitcast.13, f32[2,512,512]{2,1,0:T(8,128)S(1)} %get-tuple-element.47.grad, f32[2,512,512]{2,1,0:T(8,128)S(1)} %bitcast.10, f32[2,512,512]{2,1,0:T(8,128)S(1)} %bitcast.11, f32[2,512,512]{2,1,0:T(8,128)S(1)} %bitcast.12), custom_call_target="tpu_custom_call" | custom-call | flops 1 | bytes 1 | tf_op jit(solution)/shard_map/adam/pallas_call | solution.py:274
  (20 shorter events, 0.8 us)
Async XLA Ops:
  3.9 3.5 %collective-permute-start = (bf16[512,512]{1,0:T(8,128)(2,1)S(1)}, bf16[512,512]{1,0:T(8,128)(2,1)S(1)}, u32[]{:S(2)}, u32[]{:S(2)}) collective-permute-start(bf16[512,512]{1,0:T(8,128)(2,1)S(1)} %get-tuple-element.32), channel_id=1, source_target_pairs={{0,1},{1,0},{2,3},{3,2},{4,5},{5,4},{6,7},{7,6},{8,9},{9,8},{10,11... | collective-permute-start | bytes 1572872 | tf_op jit(solution)/shard_map/ppermute | solution.py:311
  6.1 2.0 %collective-permute-start.1 = (bf16[512,512]{1,0:T(8,128)(2,1)S(1)}, bf16[512,512]{1,0:T(8,128)(2,1)S(1)}, u32[]{:S(2)}, u32[]{:S(2)}) collective-permute-start(bf16[512,512]{1,0:T(8,128)(2,1)S(1)} %far_send_b.1), channel_id=1, source_target_pairs={{0,1},{1,0},{2,3},{3,2},{4,5},{5,4},{6,7},{7,6},{8,9},{9,8},{10,11... | collective-permute-start | bytes 1572872 | tf_op jit(solution)/shard_map/ppermute | solution.py:311
  6.1 6.0 %copy-start = (bf16[1,1,12,128,4096]{4,3,2,1,0:T(8,128)(2,1)S(1)}, bf16[1,1,12,128,4096]{4,3,2,1,0:T(8,128)(2,1)}, u32[]{:S(2)}) copy-start(bf16[1,1,12,128,4096]{4,3,2,1,0:T(8,128)(2,1)} %refs_1_.23) | copy-start | bytes 37748740
  8.2 15.6 %collective-permute-start.6 = (bf16[2,512,512]{2,1,0:T(8,128)(2,1)S(1)}, bf16[2,512,512]{2,1,0:T(8,128)(2,1)S(1)}, u32[]{:S(2)}, u32[]{:S(2)}) collective-permute-start(bf16[2,512,512]{2,1,0:T(8,128)(2,1)S(1)} %far_add_b.1), channel_id=1, source_target_pairs={{0,2},{1,7},{2,4},{3,1},{4,6},{5,3},{6,0},{7,5},{8,10},{9,15},{10,... | collective-permute-start | bytes 3145736 | tf_op jit(solution)/shard_map/ppermute | solution.py:314
  14.1 3.3 %collective-permute-start.2 = (bf16[512,512]{1,0:T(8,128)(2,1)S(1)}, bf16[512,512]{1,0:T(8,128)(2,1)S(1)}, u32[]{:S(2)}, u32[]{:S(2)}) collective-permute-start(bf16[512,512]{1,0:T(8,128)(2,1)S(1)} %send_3a.1), channel_id=1, source_target_pairs={{0,1},{1,0},{2,3},{3,2},{4,5},{5,4},{6,7},{7,6},{8,9},{9,8},{10,11... | collective-permute-start | bytes 1572872 | tf_op jit(solution)/shard_map/ppermute | solution.py:311
  14.9 3.2 %collective-permute-start.3 = (bf16[512,512]{1,0:T(8,128)(2,1)S(1)}, bf16[512,512]{1,0:T(8,128)(2,1)S(1)}, u32[]{:S(2)}, u32[]{:S(2)}) collective-permute-start(bf16[512,512]{1,0:T(8,128)(2,1)S(1)} %send_3b.1), channel_id=1, source_target_pairs={{0,1},{1,0},{2,3},{3,2},{4,5},{5,4},{6,7},{7,6},{8,9},{9,8},{10,11... | collective-permute-start | bytes 1572872 | tf_op jit(solution)/shard_map/ppermute | solution.py:311
  16.1 2.6 %collective-permute-start.4 = (bf16[512,512]{1,0:T(8,128)(2,1)S(1)}, bf16[512,512]{1,0:T(8,128)(2,1)S(1)}, u32[]{:S(2)}, u32[]{:S(2)}) collective-permute-start(bf16[512,512]{1,0:T(8,128)(2,1)S(1)} %send_1a.1), channel_id=1, source_target_pairs={{0,1},{1,0},{2,3},{3,2},{4,5},{5,4},{6,7},{7,6},{8,9},{9,8},{10,11... | collective-permute-start | bytes 1572872 | tf_op jit(solution)/shard_map/ppermute | solution.py:311
  16.8 2.6 %collective-permute-start.5 = (bf16[512,512]{1,0:T(8,128)(2,1)S(1)}, bf16[512,512]{1,0:T(8,128)(2,1)S(1)}, u32[]{:S(2)}, u32[]{:S(2)}) collective-permute-start(bf16[512,512]{1,0:T(8,128)(2,1)S(1)} %send_1b.1), channel_id=1, source_target_pairs={{0,1},{1,0},{2,3},{3,2},{4,5},{5,4},{6,7},{7,6},{8,9},{9,8},{10,11... | collective-permute-start | bytes 1572872 | tf_op jit(solution)/shard_map/ppermute | solution.py:311
  20.1 21.2 %collective-permute-start.10 = (bf16[2,512,512]{2,1,0:T(8,128)(2,1)S(1)}, bf16[2,512,512]{2,1,0:T(8,128)(2,1)S(1)}, u32[]{:S(2)}, u32[]{:S(2)}) collective-permute-start(bf16[2,512,512]{2,1,0:T(8,128)(2,1)S(1)} %keep_3b.1), channel_id=1, source_target_pairs={{0,6},{1,3},{2,0},{3,5},{4,2},{5,7},{6,4},{7,1},{8,14},{9,11},{10,... | collective-permute-start | bytes 3145736 | tf_op jit(solution)/shard_map/ppermute | solution.py:317
  24.3 22.2 %collective-permute-start.9 = (bf16[2,512,512]{2,1,0:T(8,128)(2,1)S(1)}, bf16[2,512,512]{2,1,0:T(8,128)(2,1)S(1)}, u32[]{:S(2)}, u32[]{:S(2)}) collective-permute-start(bf16[2,512,512]{2,1,0:T(8,128)(2,1)S(1)} %ring_add.1), channel_id=1, source_target_pairs={{0,2},{1,7},{2,4},{3,1},{4,6},{5,3},{6,0},{7,5},{8,10},{9,15},{10,... | collective-permute-start | bytes 3145736 | tf_op jit(solution)/shard_map/ppermute | solution.py:314
  27.5 1.9 %collective-permute-start.7 = (bf16[512,512]{1,0:T(8,128)(2,1)S(1)}, bf16[512,512]{1,0:T(8,128)(2,1)S(1)}, u32[]{:S(2)}, u32[]{:S(2)}) collective-permute-start(bf16[512,512]{1,0:T(8,128)(2,1)S(1)} %send_0a.1), channel_id=1, source_target_pairs={{0,1},{1,0},{2,3},{3,2},{4,5},{5,4},{6,7},{7,6},{8,9},{9,8},{10,11... | collective-permute-start | bytes 1572872 | tf_op jit(solution)/shard_map/ppermute | solution.py:311
  27.5 2.7 %collective-permute-start.8 = (bf16[512,512]{1,0:T(8,128)(2,1)S(1)}, bf16[512,512]{1,0:T(8,128)(2,1)S(1)}, u32[]{:S(2)}, u32[]{:S(2)}) collective-permute-start(bf16[512,512]{1,0:T(8,128)(2,1)S(1)} %send_0b.1), channel_id=1, source_target_pairs={{0,1},{1,0},{2,3},{3,2},{4,5},{5,4},{6,7},{7,6},{8,9},{9,8},{10,11... | collective-permute-start | bytes 1572872 | tf_op jit(solution)/shard_map/ppermute | solution.py:311
  30.2 35.6 %copy-start.3 = (f32[1,2,512,512]{3,2,1,0:T(8,128)S(1)}, f32[1,2,512,512]{3,2,1,0:T(8,128)}, u32[]{:S(2)}) copy-start(f32[1,2,512,512]{3,2,1,0:T(8,128)} %param.13) | copy-start | bytes 6291460
  30.8 35.0 %copy-start.1 = (f32[1,2,512,512]{3,2,1,0:T(8,128)S(1)}, f32[1,2,512,512]{3,2,1,0:T(8,128)}, u32[]{:S(2)}) copy-start(f32[1,2,512,512]{3,2,1,0:T(8,128)} %param.11) | copy-start | bytes 6291460
  30.8 35.0 %copy-start.2 = (f32[1,2,512,512]{3,2,1,0:T(8,128)S(1)}, f32[1,2,512,512]{3,2,1,0:T(8,128)}, u32[]{:S(2)}) copy-start(f32[1,2,512,512]{3,2,1,0:T(8,128)} %param.12) | copy-start | bytes 6291460

commit v6 on v5

--- a/solution.py
+++ b/solution.py
@@ -38,7 +38,7 @@
         )
 
 
-def product_kernel(section, chips, block, has_other, place_in, *refs):
+def product_kernel(section, chips, block, n_others, place_in, *refs):
     plan, x_ref, dy_ref = refs[:3]
     out = refs[-1]
     rows = out.shape[-2]
@@ -52,8 +52,9 @@
         return x_ref[0, 0, slot, :, pl.ds(pl.multiple_of(first + start, size), size)]
 
     def store(span, total):
-        if has_other:
-            total = total + refs[3][span, :].astype(jnp.float32)
+        for ref in refs[3 : 3 + n_others]:
+            other = ref[span, :] if len(ref.shape) == 2 else ref[section, span, :]
+            total = total + other.astype(jnp.float32)
         if place_in is None:
             out[span, :] = total.astype(out.dtype)
         else:
@@ -144,12 +145,12 @@
     )(queue, count, x, dy)
 
 
-def product(plan, x, dy, block, section, chips, rows, other=None, stacked=False, beside=None, dtype=jnp.bfloat16, name=""):
+def product(plan, x, dy, block, section, chips, rows, others=(), stacked=False, beside=None, dtype=jnp.bfloat16, name=""):
     width = dy.shape[2]
-    operands = [plan, x, dy] + ([] if other is None else [other]) + ([] if beside is None else [beside])
+    operands = [plan, x, dy, *others] + ([] if beside is None else [beside])
     shape = (2, rows, width) if stacked else (rows, width)
     return pl.pallas_call(
-        functools.partial(product_kernel, section, chips, block, other is not None, section if stacked else None),
+        functools.partial(product_kernel, section, chips, block, len(others), section if stacked else None),
         out_shape=jax.ShapeDtypeStruct(shape, dtype),
         in_specs=[VMEM] * len(operands),
         out_specs=VMEM,
@@ -193,7 +194,7 @@
     )(a, b)
 
 
-def total_kernel(own, summed, plain, grad, squares):
+def total_kernel(own, summed, grad, squares):
     slab = 32
     _, rows, width = own.shape
 
@@ -201,7 +202,6 @@
         span = pl.ds(pl.multiple_of(i * slab, slab), slab)
         for section in range(own.shape[0]):
             total = own[section, span, :] + summed[section, span, :].astype(jnp.float32)
-            total = total + plain[section, span, :].astype(jnp.float32)
             grad[section, span, :] = total
             kept = kept + total * total
         return kept
@@ -210,19 +210,19 @@
     squares[...] = jnp.full(squares.shape, jnp.sum(kept), jnp.float32)
 
 
-def totals(peers, own, summed, plain):
+def totals(peers, own, summed):
     return pl.pallas_call(
         total_kernel,
         out_shape=(
             jax.ShapeDtypeStruct(own.shape, jnp.float32),
             jax.ShapeDtypeStruct((peers, 128), jnp.float32),
         ),
-        in_specs=[VMEM] * 3,
+        in_specs=[VMEM] * 2,
         out_specs=(VMEM, VMEM),
         compiler_params=vmem_limit(4),
         cost_estimate=cost("totals"),
         name="totals",
-    )(own, summed, plain)
+    )(own, summed)
 
 
 def update_kernel(max_norm, squares, grad, master, moment, variance, new_master, new_moment, norm_out, masters, moments, sems):
@@ -331,7 +331,7 @@
             dy = after(dy, sent)
         return dy
 
-    def keep(step, x, other, dy, dtype=jnp.bfloat16):
+    def keep(step, x, other, dy, dtype=jnp.bfloat16, more=()):
         kept = None
         for section in range(2):
             kept = block(
@@ -339,7 +339,7 @@
                 dy,
                 (step, True),
                 section,
-                other=other[section],
+                others=(other[section], *more),
                 stacked=True,
                 beside=kept,
                 dtype=dtype,
@@ -361,8 +361,8 @@
     plain = against(near_b)
     near_a = add(after(near_a, near_b), came)
     summed = along(near_a)
-    own = keep(0, held_x, others[0], after(dy, near_a), jnp.float32)
-    grad, squares = totals(everyone, own, summed, plain)
+    own = keep(0, held_x, others[0], after(dy, near_a), jnp.float32, (plain,))
+    grad, squares = totals(everyone, own, summed)
     squares = lax.all_to_all(squares, ("pipe", "dp"), 0, 0, tiled=True)
     max_norm = 0.05 * math.sqrt(2 * lax.axis_size("pipe") * own_rows * peers * kv_width)
     new_master, new_moment, norm = adam(max_norm, squares, grad, master[0], moment[0], variance[0])

time: 69 us -> 68.8 us (level)
    ppermute x1, waiting for transfers between devices: 10.4 us -> 11.8 us  [against(): return lax.ppermute(value, 'dp', ring(-1))]
    ppermute x2, waiting for transfers between devices: 8.68 us -> 7.3 us  [along(): return lax.ppermute(value, 'dp', ring(1))]
  transfers between devices with their start and end apart: 11 -> 11, of which waited for: 6 -> 5; matrix products, arithmetic and copies ran while one was open for 0% -> 0% of each run, Pallas kernels for 15% -> 15%
where the time goes in v6:
time: 68.8 us; the launch traced here: 68.7 us
  waiting for transfers between devices  20.9 us (30%)
  blocking collectives  18.6 us (27%)
  Pallas kernels  16.7 us (24%)
  starting transfers between devices  10.9 us (16%)
  between operations  1.52 us (2%)
    all_to_all x1, blocking collectives, on_device(): squares = lax.all_to_all(squares, ('pipe', 'dp'), 0, 0, tiled=True)  18.6 us
    ppermute x1, waiting for transfers between devices, against(): return lax.ppermute(value, 'dp', ring(-1))  11.8 us
    pallas_call x15, Pallas kernels, product(): pl.pallas_call(functools.partial(product_kernel, section, chips, block, l...  9.7 us
    ppermute x2, waiting for transfers between devices, along(): return lax.ppermute(value, 'dp', ring(1))  7.3 us
    ppermute x2, starting transfers between devices, along(): return lax.ppermute(value, 'dp', ring(1))  7.09 us
    ppermute x8, starting transfers between devices, sibling(): return lax.ppermute(value, 'dp', [(i, i ^ 1) for i in range(peers)])  3.42 us
    pallas_call x1, Pallas kernels, adam(): pl.pallas_call(functools.partial(update_kernel, max_norm), out_shape=(sta...  3.02 us
    pallas_call x1, Pallas kernels, first_product(): pl.pallas_call(functools.partial(first_kernel, chips, blocks), out_shape=...  2.62 us
  transfers between devices with their start and end apart: 11, of which 5 were waited for; matrix products, arithmetic and copies ran while one was open for 0% of the time, Pallas kernels for 15%

profile of v6, /device:TPU:1, one launch (start us, length us, event | category | flops | bytes accessed | tf_op | source)
XLA Modules:
  0.0 68.7 jit_solution(5902814822506648947)
XLA Ops:
  1.3 2.6 %first_product.1 = (bf16[512,512]{1,0:T(8,128)(2,1)S(1)}, s32[12,128]{1,0:T(8,128)S(1)}, bf16[2,768,512]{2,1,0:T(8,128)(2,1)S(1)}, bf16[12,128,512]{2,1,0:T(8,128)(2,1)S(1)}, bf16[12,128,512]{2,1,0:T(8,128)(2,1)S(1)}) custom-call(s32[1,12]{1,0:T(1,128)} %queue_hbm.1, s32[1]{0:T(128)S(6)} %copy.25.count, bf16[1,1,12,128,4096]{4,3,2,1,0:T(8,128)(2,1)} %refs_1_.23, ...), custom_call_target="tpu_custom_call" | custom-call | flops 1 | bytes 1 | tf_op jit(solution)/shard_map/first_product/pallas_call | solution.py:126
  3.9 1.5 %collective-permute-start = (bf16[512,512]{1,0:T(8,128)(2,1)S(1)}, bf16[512,512]{1,0:T(8,128)(2,1)S(1)}, u32[]{:S(2)}, u32[]{:S(2)}) collective-permute-start(bf16[512,512]{1,0:T(8,128)(2,1)S(1)} %get-tuple-element.32), channel_id=1, source_target_pairs={{0,1},{1,0},{2,3},{3,2},{4,5},{5,4},{6,7},{7,6},{8,9},{9,8},{10,11... | collective-permute-start | bytes 1572872 | tf_op jit(solution)/shard_map/ppermute | solution.py:311
  5.4 0.6 far_send_b.1
  6.2 0.6 keep_2a.1.refs_3_
  6.8 0.6 keep_2b.1.a
  7.7 0.4 collective-permute-done.1.b
  8.2 3.9 %collective-permute-start.6 = (bf16[2,512,512]{2,1,0:T(8,128)(2,1)S(1)}, bf16[2,512,512]{2,1,0:T(8,128)(2,1)S(1)}, u32[]{:S(2)}, u32[]{:S(2)}) collective-permute-start(bf16[2,512,512]{2,1,0:T(8,128)(2,1)S(1)} %far_add_b.1), channel_id=1, source_target_pairs={{0,2},{1,7},{2,4},{3,1},{4,6},{5,3},{6,0},{7,5},{8,10},{9,15},{10,... | collective-permute-start | bytes 3145736 | tf_op jit(solution)/shard_map/ppermute | solution.py:314
  12.2 0.6 send_0a.1
  12.8 0.6 send_0b.1
  13.5 0.6 send_3a.1
  14.2 0.6 send_3b.1
  14.9 0.6 collective-permute-start.3
  15.4 0.6 send_1a.1
  16.2 0.6 send_1b.1
  16.8 0.6 collective-permute-start.5
  17.4 0.6 keep_1a.1.refs_4_
  18.1 0.6 keep_1b.1.a
  18.7 0.7 keep_3a.1.refs_4_
  19.4 0.7 keep_3b.1
  20.1 0.4 collective-permute-start.8
  20.5 3.4 %collective-permute-done.6.b = bf16[2,512,512]{2,1,0:T(8,128)(2,1)S(1)} collective-permute-done((bf16[2,512,512]{2,1,0:T(8,128)(2,1)S(1)}, bf16[2,512,512]{2,1,0:T(8,128)(2,1)S(1)}, u32[]{:S(2)}, u32[]{:S(2)}) %collective-permute-start.6) | collective-permute-done | bytes 1048608 | tf_op jit(solution)/shard_map/ppermute | solution.py:314
  23.9 0.4 ring_add.1
  24.3 3.2 %collective-permute-start.10 = (bf16[2,512,512]{2,1,0:T(8,128)(2,1)S(1)}, bf16[2,512,512]{2,1,0:T(8,128)(2,1)S(1)}, u32[]{:S(2)}, u32[]{:S(2)}) collective-permute-start(bf16[2,512,512]{2,1,0:T(8,128)(2,1)S(1)} %ring_add.1), channel_id=1, source_target_pairs={{0,2},{1,7},{2,4},{3,1},{4,6},{5,3},{6,0},{7,5},{8,10},{9,15},{10,... | collective-permute-start | bytes 3145736 | tf_op jit(solution)/shard_map/ppermute | solution.py:314
  27.5 0.5 collective-permute-start.9
  28.0 1.4 %collective-permute-done.7.refs_3_ = bf16[512,512]{1,0:T(8,128)(2,1)S(1)} collective-permute-done((bf16[512,512]{1,0:T(8,128)(2,1)S(1)}, bf16[512,512]{1,0:T(8,128)(2,1)S(1)}, u32[]{:S(2)}, u32[]{:S(2)}) %collective-permute-start.7) | collective-permute-done | bytes 524320 | tf_op jit(solution)/shard_map/ppermute | solution.py:311
  29.4 11.8 %collective-permute-done.8.refs_4_ = bf16[2,512,512]{2,1,0:T(8,128)(2,1)S(1)} collective-permute-done((bf16[2,512,512]{2,1,0:T(8,128)(2,1)S(1)}, bf16[2,512,512]{2,1,0:T(8,128)(2,1)S(1)}, u32[]{:S(2)}, u32[]{:S(2)}) %collective-permute-start.8) | collective-permute-done | bytes 1048608 | tf_op jit(solution)/shard_map/ppermute | solution.py:317
  41.3 0.7 keep_0a.1.refs_5_
  42.0 0.7 keep_0b.1.own
  42.6 3.9 %collective-permute-done.10.summed = bf16[2,512,512]{2,1,0:T(8,128)(2,1)S(1)} collective-permute-done((bf16[2,512,512]{2,1,0:T(8,128)(2,1)S(1)}, bf16[2,512,512]{2,1,0:T(8,128)(2,1)S(1)}, u32[]{:S(2)}, u32[]{:S(2)}) %collective-permute-start.10) | collective-permute-done | bytes 1048608 | tf_op jit(solution)/shard_map/ppermute | solution.py:314
  46.5 0.5 totals.1
  47.0 18.6 %all_to_all.11 = f32[128,1,128]{2,1,0:T(1,128)S(1)} all-to-all(f32[128,1,128]{2,1,0:T(1,128)S(1)} %bitcast.14), channel_id=1, replica_groups=mesh['pipe'=16,'dp'=8] {'pipe','dp'}, dimensions={0} | all-to-all | bytes 131072 | tf_op jit(solution)/shard_map/all_to_all | solution.py:366
  65.6 3.0 %adam.1 = (f32[2,512,512]{2,1,0:T(8,128)}, f32[2,512,512]{2,1,0:T(8,128)}, f32[1,1]{1,0:T(1,128)}) custom-call(f32[128,128]{1,0:T(8,128)S(1)} %bitcast.13, f32[2,512,512]{2,1,0:T(8,128)S(1)} %get-tuple-element.47.grad, f32[2,512,512]{2,1,0:T(8,128)S(1)} %bitcast.10, f32[2,512,512]{2,1,0:T(8,128)S(1)} %bitcast.11, f32[2,512,512]{2,1,0:T(8,128)S(1)} %bitcast.12), custom_call_target="tpu_custom_call" | custom-call | flops 1 | bytes 1 | tf_op jit(solution)/shard_map/adam/pallas_call | solution.py:274
  (20 shorter events, 0.7 us)
Async XLA Ops:
  3.9 3.5 %collective-permute-start = (bf16[512,512]{1,0:T(8,128)(2,1)S(1)}, bf16[512,512]{1,0:T(8,128)(2,1)S(1)}, u32[]{:S(2)}, u32[]{:S(2)}) collective-permute-start(bf16[512,512]{1,0:T(8,128)(2,1)S(1)} %get-tuple-element.32), channel_id=1, source_target_pairs={{0,1},{1,0},{2,3},{3,2},{4,5},{5,4},{6,7},{7,6},{8,9},{9,8},{10,11... | collective-permute-start | bytes 1572872 | tf_op jit(solution)/shard_map/ppermute | solution.py:311
  6.1 2.0 %collective-permute-start.1 = (bf16[512,512]{1,0:T(8,128)(2,1)S(1)}, bf16[512,512]{1,0:T(8,128)(2,1)S(1)}, u32[]{:S(2)}, u32[]{:S(2)}) collective-permute-start(bf16[512,512]{1,0:T(8,128)(2,1)S(1)} %far_send_b.1), channel_id=1, source_target_pairs={{0,1},{1,0},{2,3},{3,2},{4,5},{5,4},{6,7},{7,6},{8,9},{9,8},{10,11... | collective-permute-start | bytes 1572872 | tf_op jit(solution)/shard_map/ppermute | solution.py:311
  6.1 6.0 %copy-start = (bf16[1,1,12,128,4096]{4,3,2,1,0:T(8,128)(2,1)S(1)}, bf16[1,1,12,128,4096]{4,3,2,1,0:T(8,128)(2,1)}, u32[]{:S(2)}) copy-start(bf16[1,1,12,128,4096]{4,3,2,1,0:T(8,128)(2,1)} %refs_1_.23) | copy-start | bytes 37748740
  8.2 15.6 %collective-permute-start.6 = (bf16[2,512,512]{2,1,0:T(8,128)(2,1)S(1)}, bf16[2,512,512]{2,1,0:T(8,128)(2,1)S(1)}, u32[]{:S(2)}, u32[]{:S(2)}) collective-permute-start(bf16[2,512,512]{2,1,0:T(8,128)(2,1)S(1)} %far_add_b.1), channel_id=1, source_target_pairs={{0,2},{1,7},{2,4},{3,1},{4,6},{5,3},{6,0},{7,5},{8,10},{9,15},{10,... | collective-permute-start | bytes 3145736 | tf_op jit(solution)/shard_map/ppermute | solution.py:314
  14.1 3.3 %collective-permute-start.2 = (bf16[512,512]{1,0:T(8,128)(2,1)S(1)}, bf16[512,512]{1,0:T(8,128)(2,1)S(1)}, u32[]{:S(2)}, u32[]{:S(2)}) collective-permute-start(bf16[512,512]{1,0:T(8,128)(2,1)S(1)} %send_3a.1), channel_id=1, source_target_pairs={{0,1},{1,0},{2,3},{3,2},{4,5},{5,4},{6,7},{7,6},{8,9},{9,8},{10,11... | collective-permute-start | bytes 1572872 | tf_op jit(solution)/shard_map/ppermute | solution.py:311
  14.9 3.2 %collective-permute-start.3 = (bf16[512,512]{1,0:T(8,128)(2,1)S(1)}, bf16[512,512]{1,0:T(8,128)(2,1)S(1)}, u32[]{:S(2)}, u32[]{:S(2)}) collective-permute-start(bf16[512,512]{1,0:T(8,128)(2,1)S(1)} %send_3b.1), channel_id=1, source_target_pairs={{0,1},{1,0},{2,3},{3,2},{4,5},{5,4},{6,7},{7,6},{8,9},{9,8},{10,11... | collective-permute-start | bytes 1572872 | tf_op jit(solution)/shard_map/ppermute | solution.py:311
  16.1 2.6 %collective-permute-start.4 = (bf16[512,512]{1,0:T(8,128)(2,1)S(1)}, bf16[512,512]{1,0:T(8,128)(2,1)S(1)}, u32[]{:S(2)}, u32[]{:S(2)}) collective-permute-start(bf16[512,512]{1,0:T(8,128)(2,1)S(1)} %send_1a.1), channel_id=1, source_target_pairs={{0,1},{1,0},{2,3},{3,2},{4,5},{5,4},{6,7},{7,6},{8,9},{9,8},{10,11... | collective-permute-start | bytes 1572872 | tf_op jit(solution)/shard_map/ppermute | solution.py:311
  16.8 2.6 %collective-permute-start.5 = (bf16[512,512]{1,0:T(8,128)(2,1)S(1)}, bf16[512,512]{1,0:T(8,128)(2,1)S(1)}, u32[]{:S(2)}, u32[]{:S(2)}) collective-permute-start(bf16[512,512]{1,0:T(8,128)(2,1)S(1)} %send_1b.1), channel_id=1, source_target_pairs={{0,1},{1,0},{2,3},{3,2},{4,5},{5,4},{6,7},{7,6},{8,9},{9,8},{10,11... | collective-permute-start | bytes 1572872 | tf_op jit(solution)/shard_map/ppermute | solution.py:311
  20.1 21.2 %collective-permute-start.8 = (bf16[2,512,512]{2,1,0:T(8,128)(2,1)S(1)}, bf16[2,512,512]{2,1,0:T(8,128)(2,1)S(1)}, u32[]{:S(2)}, u32[]{:S(2)}) collective-permute-start(bf16[2,512,512]{2,1,0:T(8,128)(2,1)S(1)} %keep_3b.1), channel_id=1, source_target_pairs={{0,6},{1,3},{2,0},{3,5},{4,2},{5,7},{6,4},{7,1},{8,14},{9,11},{10,... | collective-permute-start | bytes 3145736 | tf_op jit(solution)/shard_map/ppermute | solution.py:317
  24.3 22.2 %collective-permute-start.10 = (bf16[2,512,512]{2,1,0:T(8,128)(2,1)S(1)}, bf16[2,512,512]{2,1,0:T(8,128)(2,1)S(1)}, u32[]{:S(2)}, u32[]{:S(2)}) collective-permute-start(bf16[2,512,512]{2,1,0:T(8,128)(2,1)S(1)} %ring_add.1), channel_id=1, source_target_pairs={{0,2},{1,7},{2,4},{3,1},{4,6},{5,3},{6,0},{7,5},{8,10},{9,15},{10,... | collective-permute-start | bytes 3145736 | tf_op jit(solution)/shard_map/ppermute | solution.py:314
  27.5 1.9 %collective-permute-start.7 = (bf16[512,512]{1,0:T(8,128)(2,1)S(1)}, bf16[512,512]{1,0:T(8,128)(2,1)S(1)}, u32[]{:S(2)}, u32[]{:S(2)}) collective-permute-start(bf16[512,512]{1,0:T(8,128)(2,1)S(1)} %send_0a.1), channel_id=1, source_target_pairs={{0,1},{1,0},{2,3},{3,2},{4,5},{5,4},{6,7},{7,6},{8,9},{9,8},{10,11... | collective-permute-start | bytes 1572872 | tf_op jit(solution)/shard_map/ppermute | solution.py:311
  27.5 14.4 %collective-permute-start.9 = (bf16[512,512]{1,0:T(8,128)(2,1)S(1)}, bf16[512,512]{1,0:T(8,128)(2,1)S(1)}, u32[]{:S(2)}, u32[]{:S(2)}) collective-permute-start(bf16[512,512]{1,0:T(8,128)(2,1)S(1)} %send_0b.1), channel_id=1, source_target_pairs={{0,1},{1,0},{2,3},{3,2},{4,5},{5,4},{6,7},{7,6},{8,9},{9,8},{10,11... | collective-permute-start | bytes 1572872 | tf_op jit(solution)/shard_map/ppermute | solution.py:311
  41.9 23.7 %copy-start.2 = (f32[1,2,512,512]{3,2,1,0:T(8,128)S(1)}, f32[1,2,512,512]{3,2,1,0:T(8,128)}, u32[]{:S(2)}) copy-start(f32[1,2,512,512]{3,2,1,0:T(8,128)} %param.12) | copy-start | bytes 6291460
  41.9 23.7 %copy-start.3 = (f32[1,2,512,512]{3,2,1,0:T(8,128)S(1)}, f32[1,2,512,512]{3,2,1,0:T(8,128)}, u32[]{:S(2)}) copy-start(f32[1,2,512,512]{3,2,1,0:T(8,128)} %param.13) | copy-start | bytes 6291460
  42.6 23.0 %copy-start.1 = (f32[1,2,512,512]{3,2,1,0:T(8,128)S(1)}, f32[1,2,512,512]{3,2,1,0:T(8,128)}, u32[]{:S(2)}) copy-start(f32[1,2,512,512]{3,2,1,0:T(8,128)} %param.11) | copy-start | bytes 6291460

commit v7 on v6

--- a/solution.py
+++ b/solution.py
@@ -195,7 +195,7 @@
 
 
 def total_kernel(own, summed, grad, squares):
-    slab = 32
+    slab = 64
     _, rows, width = own.shape
 
     def step(i, kept):

time: 68.8 us -> 68.8 us (level)
  no operation moved by 1% of the time
where the time goes in v7:
time: 68.8 us; the launch traced here: 68.6 us
  waiting for transfers between devices  20.9 us (30%)
  blocking collectives  18.6 us (27%)
  Pallas kernels  16.7 us (24%)
  starting transfers between devices  10.9 us (16%)
  between operations  1.52 us (2%)
    all_to_all x1, blocking collectives, on_device(): squares = lax.all_to_all(squares, ('pipe', 'dp'), 0, 0, tiled=True)  18.6 us
    ppermute x1, waiting for transfers between devices, against(): return lax.ppermute(value, 'dp', ring(-1))  11.8 us
    pallas_call x15, Pallas kernels, product(): pl.pallas_call(functools.partial(product_kernel, section, chips, block, l...  9.7 us
    ppermute x2, waiting for transfers between devices, along(): return lax.ppermute(value, 'dp', ring(1))  7.3 us
    ppermute x2, starting transfers between devices, along(): return lax.ppermute(value, 'dp', ring(1))  7.09 us
    ppermute x8, starting transfers between devices, sibling(): return lax.ppermute(value, 'dp', [(i, i ^ 1) for i in range(peers)])  3.42 us
    pallas_call x1, Pallas kernels, adam(): pl.pallas_call(functools.partial(update_kernel, max_norm), out_shape=(sta...  3.02 us
    pallas_call x1, Pallas kernels, first_product(): pl.pallas_call(functools.partial(first_kernel, chips, blocks), out_shape=...  2.62 us
  transfers between devices with their start and end apart: 11, of which 5 were waited for; matrix products, arithmetic and copies ran while one was open for 0% of the time, Pallas kernels for 15%

profile of v7, /device:TPU:1, one launch (start us, length us, event | category | flops | bytes accessed | tf_op | source)
XLA Modules:
  0.0 68.6 jit_solution(15924667456553373674)
XLA Ops:
  1.3 2.6 %first_product.1 = (bf16[512,512]{1,0:T(8,128)(2,1)S(1)}, s32[12,128]{1,0:T(8,128)S(1)}, bf16[2,768,512]{2,1,0:T(8,128)(2,1)S(1)}, bf16[12,128,512]{2,1,0:T(8,128)(2,1)S(1)}, bf16[12,128,512]{2,1,0:T(8,128)(2,1)S(1)}) custom-call(s32[1,12]{1,0:T(1,128)} %queue_hbm.1, s32[1]{0:T(128)S(6)} %copy.25.count, bf16[1,1,12,128,4096]{4,3,2,1,0:T(8,128)(2,1)} %refs_1_.23, ...), custom_call_target="tpu_custom_call" | custom-call | flops 1 | bytes 1 | tf_op jit(solution)/shard_map/first_product/pallas_call | solution.py:126
  3.9 1.5 %collective-permute-start = (bf16[512,512]{1,0:T(8,128)(2,1)S(1)}, bf16[512,512]{1,0:T(8,128)(2,1)S(1)}, u32[]{:S(2)}, u32[]{:S(2)}) collective-permute-start(bf16[512,512]{1,0:T(8,128)(2,1)S(1)} %get-tuple-element.32), channel_id=1, source_target_pairs={{0,1},{1,0},{2,3},{3,2},{4,5},{5,4},{6,7},{7,6},{8,9},{9,8},{10,11... | collective-permute-start | bytes 1572872 | tf_op jit(solution)/shard_map/ppermute | solution.py:311
  5.4 0.6 far_send_b.1
  6.2 0.6 keep_2a.1.refs_3_
  6.8 0.6 keep_2b.1.a
  7.7 0.4 collective-permute-done.1.b
  8.2 3.9 %collective-permute-start.6 = (bf16[2,512,512]{2,1,0:T(8,128)(2,1)S(1)}, bf16[2,512,512]{2,1,0:T(8,128)(2,1)S(1)}, u32[]{:S(2)}, u32[]{:S(2)}) collective-permute-start(bf16[2,512,512]{2,1,0:T(8,128)(2,1)S(1)} %far_add_b.1), channel_id=1, source_target_pairs={{0,2},{1,7},{2,4},{3,1},{4,6},{5,3},{6,0},{7,5},{8,10},{9,15},{10,... | collective-permute-start | bytes 3145736 | tf_op jit(solution)/shard_map/ppermute | solution.py:314
  12.2 0.6 send_0a.1
  12.8 0.6 send_0b.1
  13.5 0.6 send_3a.1
  14.2 0.6 send_3b.1
  14.9 0.6 collective-permute-start.3
  15.4 0.6 send_1a.1
  16.2 0.6 send_1b.1
  16.8 0.6 collective-permute-start.5
  17.4 0.6 keep_1a.1.refs_4_
  18.1 0.6 keep_1b.1.a
  18.7 0.7 keep_3a.1.refs_4_
  19.4 0.7 keep_3b.1
  20.1 0.4 collective-permute-start.8
  20.5 3.4 %collective-permute-done.6.b = bf16[2,512,512]{2,1,0:T(8,128)(2,1)S(1)} collective-permute-done((bf16[2,512,512]{2,1,0:T(8,128)(2,1)S(1)}, bf16[2,512,512]{2,1,0:T(8,128)(2,1)S(1)}, u32[]{:S(2)}, u32[]{:S(2)}) %collective-permute-start.6) | collective-permute-done | bytes 1048608 | tf_op jit(solution)/shard_map/ppermute | solution.py:314
  23.9 0.4 ring_add.1
  24.3 3.2 %collective-permute-start.10 = (bf16[2,512,512]{2,1,0:T(8,128)(2,1)S(1)}, bf16[2,512,512]{2,1,0:T(8,128)(2,1)S(1)}, u32[]{:S(2)}, u32[]{:S(2)}) collective-permute-start(bf16[2,512,512]{2,1,0:T(8,128)(2,1)S(1)} %ring_add.1), channel_id=1, source_target_pairs={{0,2},{1,7},{2,4},{3,1},{4,6},{5,3},{6,0},{7,5},{8,10},{9,15},{10,... | collective-permute-start | bytes 3145736 | tf_op jit(solution)/shard_map/ppermute | solution.py:314
  27.5 0.5 collective-permute-start.9
  28.0 1.4 %collective-permute-done.7.refs_3_ = bf16[512,512]{1,0:T(8,128)(2,1)S(1)} collective-permute-done((bf16[512,512]{1,0:T(8,128)(2,1)S(1)}, bf16[512,512]{1,0:T(8,128)(2,1)S(1)}, u32[]{:S(2)}, u32[]{:S(2)}) %collective-permute-start.7) | collective-permute-done | bytes 524320 | tf_op jit(solution)/shard_map/ppermute | solution.py:311
  29.4 11.8 %collective-permute-done.8.refs_4_ = bf16[2,512,512]{2,1,0:T(8,128)(2,1)S(1)} collective-permute-done((bf16[2,512,512]{2,1,0:T(8,128)(2,1)S(1)}, bf16[2,512,512]{2,1,0:T(8,128)(2,1)S(1)}, u32[]{:S(2)}, u32[]{:S(2)}) %collective-permute-start.8) | collective-permute-done | bytes 1048608 | tf_op jit(solution)/shard_map/ppermute | solution.py:317
  41.3 0.7 keep_0a.1.refs_5_
  42.0 0.7 keep_0b.1.own
  42.6 3.9 %collective-permute-done.10.summed = bf16[2,512,512]{2,1,0:T(8,128)(2,1)S(1)} collective-permute-done((bf16[2,512,512]{2,1,0:T(8,128)(2,1)S(1)}, bf16[2,512,512]{2,1,0:T(8,128)(2,1)S(1)}, u32[]{:S(2)}, u32[]{:S(2)}) %collective-permute-start.10) | collective-permute-done | bytes 1048608 | tf_op jit(solution)/shard_map/ppermute | solution.py:314
  46.5 0.5 totals.1
  47.0 18.6 %all_to_all.11 = f32[128,1,128]{2,1,0:T(1,128)S(1)} all-to-all(f32[128,1,128]{2,1,0:T(1,128)S(1)} %bitcast.14), channel_id=1, replica_groups=mesh['pipe'=16,'dp'=8] {'pipe','dp'}, dimensions={0} | all-to-all | bytes 131072 | tf_op jit(solution)/shard_map/all_to_all | solution.py:366
  65.6 3.0 %adam.1 = (f32[2,512,512]{2,1,0:T(8,128)}, f32[2,512,512]{2,1,0:T(8,128)}, f32[1,1]{1,0:T(1,128)}) custom-call(f32[128,128]{1,0:T(8,128)S(1)} %bitcast.13, f32[2,512,512]{2,1,0:T(8,128)S(1)} %get-tuple-element.47.grad, f32[2,512,512]{2,1,0:T(8,128)S(1)} %bitcast.10, f32[2,512,512]{2,1,0:T(8,128)S(1)} %bitcast.11, f32[2,512,512]{2,1,0:T(8,128)S(1)} %bitcast.12), custom_call_target="tpu_custom_call" | custom-call | flops 1 | bytes 1 | tf_op jit(solution)/shard_map/adam/pallas_call | solution.py:274
  (20 shorter events, 0.7 us)
Async XLA Ops:
  3.9 3.5 %collective-permute-start = (bf16[512,512]{1,0:T(8,128)(2,1)S(1)}, bf16[512,512]{1,0:T(8,128)(2,1)S(1)}, u32[]{:S(2)}, u32[]{:S(2)}) collective-permute-start(bf16[512,512]{1,0:T(8,128)(2,1)S(1)} %get-tuple-element.32), channel_id=1, source_target_pairs={{0,1},{1,0},{2,3},{3,2},{4,5},{5,4},{6,7},{7,6},{8,9},{9,8},{10,11... | collective-permute-start | bytes 1572872 | tf_op jit(solution)/shard_map/ppermute | solution.py:311
  6.1 2.0 %collective-permute-start.1 = (bf16[512,512]{1,0:T(8,128)(2,1)S(1)}, bf16[512,512]{1,0:T(8,128)(2,1)S(1)}, u32[]{:S(2)}, u32[]{:S(2)}) collective-permute-start(bf16[512,512]{1,0:T(8,128)(2,1)S(1)} %far_send_b.1), channel_id=1, source_target_pairs={{0,1},{1,0},{2,3},{3,2},{4,5},{5,4},{6,7},{7,6},{8,9},{9,8},{10,11... | collective-permute-start | bytes 1572872 | tf_op jit(solution)/shard_map/ppermute | solution.py:311
  6.1 6.0 %copy-start = (bf16[1,1,12,128,4096]{4,3,2,1,0:T(8,128)(2,1)S(1)}, bf16[1,1,12,128,4096]{4,3,2,1,0:T(8,128)(2,1)}, u32[]{:S(2)}) copy-start(bf16[1,1,12,128,4096]{4,3,2,1,0:T(8,128)(2,1)} %refs_1_.23) | copy-start | bytes 37748740
  8.2 15.6 %collective-permute-start.6 = (bf16[2,512,512]{2,1,0:T(8,128)(2,1)S(1)}, bf16[2,512,512]{2,1,0:T(8,128)(2,1)S(1)}, u32[]{:S(2)}, u32[]{:S(2)}) collective-permute-start(bf16[2,512,512]{2,1,0:T(8,128)(2,1)S(1)} %far_add_b.1), channel_id=1, source_target_pairs={{0,2},{1,7},{2,4},{3,1},{4,6},{5,3},{6,0},{7,5},{8,10},{9,15},{10,... | collective-permute-start | bytes 3145736 | tf_op jit(solution)/shard_map/ppermute | solution.py:314
  14.1 3.3 %collective-permute-start.2 = (bf16[512,512]{1,0:T(8,128)(2,1)S(1)}, bf16[512,512]{1,0:T(8,128)(2,1)S(1)}, u32[]{:S(2)}, u32[]{:S(2)}) collective-permute-start(bf16[512,512]{1,0:T(8,128)(2,1)S(1)} %send_3a.1), channel_id=1, source_target_pairs={{0,1},{1,0},{2,3},{3,2},{4,5},{5,4},{6,7},{7,6},{8,9},{9,8},{10,11... | collective-permute-start | bytes 1572872 | tf_op jit(solution)/shard_map/ppermute | solution.py:311
  14.9 3.2 %collective-permute-start.3 = (bf16[512,512]{1,0:T(8,128)(2,1)S(1)}, bf16[512,512]{1,0:T(8,128)(2,1)S(1)}, u32[]{:S(2)}, u32[]{:S(2)}) collective-permute-start(bf16[512,512]{1,0:T(8,128)(2,1)S(1)} %send_3b.1), channel_id=1, source_target_pairs={{0,1},{1,0},{2,3},{3,2},{4,5},{5,4},{6,7},{7,6},{8,9},{9,8},{10,11... | collective-permute-start | bytes 1572872 | tf_op jit(solution)/shard_map/ppermute | solution.py:311
  16.1 2.6 %collective-permute-start.4 = (bf16[512,512]{1,0:T(8,128)(2,1)S(1)}, bf16[512,512]{1,0:T(8,128)(2,1)S(1)}, u32[]{:S(2)}, u32[]{:S(2)}) collective-permute-start(bf16[512,512]{1,0:T(8,128)(2,1)S(1)} %send_1a.1), channel_id=1, source_target_pairs={{0,1},{1,0},{2,3},{3,2},{4,5},{5,4},{6,7},{7,6},{8,9},{9,8},{10,11... | collective-permute-start | bytes 1572872 | tf_op jit(solution)/shard_map/ppermute | solution.py:311
  16.8 2.6 %collective-permute-start.5 = (bf16[512,512]{1,0:T(8,128)(2,1)S(1)}, bf16[512,512]{1,0:T(8,128)(2,1)S(1)}, u32[]{:S(2)}, u32[]{:S(2)}) collective-permute-start(bf16[512,512]{1,0:T(8,128)(2,1)S(1)} %send_1b.1), channel_id=1, source_target_pairs={{0,1},{1,0},{2,3},{3,2},{4,5},{5,4},{6,7},{7,6},{8,9},{9,8},{10,11... | collective-permute-start | bytes 1572872 | tf_op jit(solution)/shard_map/ppermute | solution.py:311
  20.1 21.2 %collective-permute-start.8 = (bf16[2,512,512]{2,1,0:T(8,128)(2,1)S(1)}, bf16[2,512,512]{2,1,0:T(8,128)(2,1)S(1)}, u32[]{:S(2)}, u32[]{:S(2)}) collective-permute-start(bf16[2,512,512]{2,1,0:T(8,128)(2,1)S(1)} %keep_3b.1), channel_id=1, source_target_pairs={{0,6},{1,3},{2,0},{3,5},{4,2},{5,7},{6,4},{7,1},{8,14},{9,11},{10,... | collective-permute-start | bytes 3145736 | tf_op jit(solution)/shard_map/ppermute | solution.py:317
  24.3 22.2 %collective-permute-start.10 = (bf16[2,512,512]{2,1,0:T(8,128)(2,1)S(1)}, bf16[2,512,512]{2,1,0:T(8,128)(2,1)S(1)}, u32[]{:S(2)}, u32[]{:S(2)}) collective-permute-start(bf16[2,512,512]{2,1,0:T(8,128)(2,1)S(1)} %ring_add.1), channel_id=1, source_target_pairs={{0,2},{1,7},{2,4},{3,1},{4,6},{5,3},{6,0},{7,5},{8,10},{9,15},{10,... | collective-permute-start | bytes 3145736 | tf_op jit(solution)/shard_map/ppermute | solution.py:314
  27.5 1.9 %collective-permute-start.7 = (bf16[512,512]{1,0:T(8,128)(2,1)S(1)}, bf16[512,512]{1,0:T(8,128)(2,1)S(1)}, u32[]{:S(2)}, u32[]{:S(2)}) collective-permute-start(bf16[512,512]{1,0:T(8,128)(2,1)S(1)} %send_0a.1), channel_id=1, source_target_pairs={{0,1},{1,0},{2,3},{3,2},{4,5},{5,4},{6,7},{7,6},{8,9},{9,8},{10,11... | collective-permute-start | bytes 1572872 | tf_op jit(solution)/shard_map/ppermute | solution.py:311
  27.5 14.4 %collective-permute-start.9 = (bf16[512,512]{1,0:T(8,128)(2,1)S(1)}, bf16[512,512]{1,0:T(8,128)(2,1)S(1)}, u32[]{:S(2)}, u32[]{:S(2)}) collective-permute-start(bf16[512,512]{1,0:T(8,128)(2,1)S(1)} %send_0b.1), channel_id=1, source_target_pairs={{0,1},{1,0},{2,3},{3,2},{4,5},{5,4},{6,7},{7,6},{8,9},{9,8},{10,11... | collective-permute-start | bytes 1572872 | tf_op jit(solution)/shard_map/ppermute | solution.py:311
  41.9 23.7 %copy-start.2 = (f32[1,2,512,512]{3,2,1,0:T(8,128)S(1)}, f32[1,2,512,512]{3,2,1,0:T(8,128)}, u32[]{:S(2)}) copy-start(f32[1,2,512,512]{3,2,1,0:T(8,128)} %param.12) | copy-start | bytes 6291460
  41.9 23.7 %copy-start.3 = (f32[1,2,512,512]{3,2,1,0:T(8,128)S(1)}, f32[1,2,512,512]{3,2,1,0:T(8,128)}, u32[]{:S(2)}) copy-start(f32[1,2,512,512]{3,2,1,0:T(8,128)} %param.13) | copy-start | bytes 6291460
  42.6 23.0 %copy-start.1 = (f32[1,2,512,512]{3,2,1,0:T(8,128)S(1)}, f32[1,2,512,512]{3,2,1,0:T(8,128)}, u32[]{:S(2)}) copy-start(f32[1,2,512,512]{3,2,1,0:T(8,128)} %param.11) | copy-start | bytes 6291460
